TPU v7x, 32 devices: a whole 2x2x4 slice. The times are simulated.
32 devices in a mesh: dp: 8 (over y, x, core), mp: 4 (over z).
Axes of the slice: x: 2, y: 2, z: 4, core: 2. Of those that a mesh axis runs over, the one named last changes fastest.
Arguments:
- tokens: bfloat16 [32, 2048, 1024], P(('dp', 'mp')), may hold values from -6 to 6
- cotangent: bfloat16 [32, 2048, 1024], P(('dp', 'mp')), may hold values from -6 to 6
- routed: int32 [32, 256], P(('dp', 'mp')), may hold values from 0 to 2047, as said below
- valid_mask: int32 [32, 2048], P(('dp', 'mp')), may hold values 0 or 1
- w_router: float32 [1024], replicated, may hold values from -0.1875 to 0.1875
- first_gain: float32 [1024], replicated, may hold values from 0.25 to 1.75
- query_weight: bfloat16 [1024, 1024], P(None, 'mp'), may hold values from -0.1875 to 0.1875
- key_weight: bfloat16 [1024, 1024], P(None, 'mp'), may hold values from -0.1875 to 0.1875
- value_weight: bfloat16 [1024, 1024], P(None, 'mp'), may hold values from -0.1875 to 0.1875
- output_weight: bfloat16 [1024, 1024], P('mp'), may hold values from -1.5 to 1.5
- second_gain: float32 [1024], replicated, may hold values from 0.25 to 1.75
- up_weight: bfloat16 [1024, 4096], P(None, 'mp'), may hold values from -0.1875 to 0.1875
- down_weight: bfloat16 [4096, 1024], P('mp'), may hold values from -0.09375 to 0.09375
Outputs:
- residual: bfloat16 [32, 2048, 1024], P(('dp', 'mp'))
- grad_tokens: bfloat16 [32, 2048, 1024], P(('dp', 'mp'))
- sublayer_rms: float32 [32], P(('dp', 'mp'))
- grad_router: float32 [1024], replicated
- grad_first: float32 [1024], replicated
- grad_query: float32 [1024, 1024], P('dp', 'mp')
- grad_key: float32 [1024, 1024], P('dp', 'mp')
- grad_value: float32 [1024, 1024], P('dp', 'mp')
- grad_output: float32 [1024, 1024], P('mp', 'dp')
- grad_second: float32 [1024], replicated
- grad_up: float32 [1024, 4096], P('dp', 'mp')
- grad_down: float32 [4096, 1024], P('mp', 'dp')
Inputs may be any that keep to these rules, and one draw needn't show every extreme that they name: `routed`: each row holds 256 distinct positions of its sequence in increasing order.
All inputs are finite; a program needn't handle non-finite values. No bound on the sum of `valid_mask` on one device may be relied on, other than what follows from the above.
Results may differ from a plain program's by a relative error of at most 0.018.
Values may be sent and summed in bfloat16 or wider, within the bound.
A program may use at most 256 MiB of HBM per device.

v0:
```python
import jax
import jax.numpy as jnp
from jax import lax
from jax.sharding import PartitionSpec as P

HEADS = 16
HEAD_DIM = 64


norm_eps = 1e-06


def rms_norm(value, gain):
    factor = lax.rsqrt(jnp.mean(value * value, axis=-1, keepdims=True) + norm_eps)
    return value * factor * gain


def gain_grad(value, grad):
    factor = lax.rsqrt(jnp.mean(value * value, axis=-1, keepdims=True) + norm_eps)
    return jnp.sum(grad * value * factor, axis=(0, 1))


def exact_gelu(value):
    return jax.nn.gelu(value, approximate=False)


def own_rows(whole, first, count):
    return lax.dynamic_slice_in_dim(whole, first, count, 0)


def project(left, right):
    return jnp.einsum("skd,dc->skc", left, right, preferred_element_type=jnp.float32)


def project_back(left, right):
    return jnp.einsum("skc,dc->skd", left, right, preferred_element_type=jnp.float32)


def weight_grad(left, right):
    return jnp.einsum("skd,skc->dc", left, right, preferred_element_type=jnp.float32)


def place_rows(base, rows, addend):
    return base.at[rows].add(addend)


def shards(
    tokens,
    cotangent,
    routed,
    valid_mask,
    w_router,
    first_gain,
    query_weight,
    key_weight,
    value_weight,
    output_weight,
    second_gain,
    up_weight,
    down_weight,
):
    seq_here = tokens.shape[0]
    model_width = tokens.shape[2]
    routed_count = routed.shape[1]
    heads_here = HEADS // lax.axis_size("mp")
    first_own = lax.axis_index("mp") * seq_here
    picked = routed[:, :, None]
    sent_tokens = jnp.take_along_axis(tokens, picked, axis=1)
    sent_cot = jnp.take_along_axis(cotangent, picked, axis=1)
    sent_valid = jnp.take_along_axis(valid_mask, routed, axis=1).astype(jnp.bfloat16)
    chosen, chosen_cot, chosen_valid = (
        lax.all_gather(sent_tokens, "mp", axis=0, tiled=True),
        lax.all_gather(sent_cot, "mp", axis=0, tiled=True),
        lax.all_gather(sent_valid, "mp", axis=0, tiled=True),
    )
    inputs = chosen.astype(jnp.float32)
    cot_rows = chosen_cot.astype(jnp.float32)
    valid_rows = chosen_valid.astype(jnp.float32)
    group_rows = inputs.shape[0]
    gate_value = (
        jnp.einsum("skd,d->sk", inputs, w_router, precision=lax.Precision.HIGHEST) * valid_rows
    )
    normed = rms_norm(inputs, first_gain).astype(jnp.bfloat16)
    head_shape = (group_rows, routed_count, heads_here, HEAD_DIM)
    flat_shape = (group_rows, routed_count, heads_here * HEAD_DIM)
    query_rows = project(normed, query_weight).astype(jnp.bfloat16).reshape(head_shape)
    key_rows = project(normed, key_weight).astype(jnp.bfloat16).reshape(head_shape)
    value_rows = project(normed, value_weight).astype(jnp.bfloat16).reshape(head_shape)
    score_scale = HEAD_DIM ** (-0.5)
    rank_order = jnp.arange(routed_count)
    causal = rank_order[:, None] >= rank_order[None, :]

    def masked_scores():
        raw_scores = (
            jnp.einsum("sqhe,skhe->shqk", query_rows, key_rows, preferred_element_type=jnp.float32)
            * score_scale
        )
        return jnp.where(causal, raw_scores, -1e30)

    scores = masked_scores()
    row_peak = jnp.max(scores, axis=-1, keepdims=True)
    log_total = row_peak + jnp.log(jnp.sum(jnp.exp(scores - row_peak), axis=-1, keepdims=True))
    weights_low = jnp.exp(scores - log_total).astype(jnp.bfloat16)
    context = jnp.einsum(
        "shqk,skhe->sqhe", weights_low, value_rows, preferred_element_type=jnp.float32
    )
    context = context.astype(jnp.bfloat16).reshape(flat_shape)
    attended = lax.psum(
        jnp.einsum(
            "skc,cd->skd", context, output_weight, preferred_element_type=jnp.float32
        ).astype(jnp.bfloat16),
        "mp",
    ).astype(jnp.float32)
    mixed_rows = inputs + attended
    normed_two = rms_norm(mixed_rows, second_gain).astype(jnp.bfloat16)
    upward = project(normed_two, up_weight)
    active = exact_gelu(upward).astype(jnp.bfloat16)
    feed_own = lax.psum_scatter(
        jnp.einsum("skf,fd->skd", active, down_weight, preferred_element_type=jnp.float32).astype(
            jnp.bfloat16
        ),
        "mp",
        scatter_dimension=0,
        tiled=True,
    ).astype(jnp.float32)
    gate_own = own_rows(gate_value, first_own, seq_here)
    branch_own = own_rows(attended, first_own, seq_here) + feed_own
    update = gate_own[..., None] * branch_own
    residual = jax.vmap(place_rows)(tokens.astype(jnp.float32), routed, update).astype(jnp.bfloat16)
    valid_count = jnp.sum(valid_mask.astype(jnp.float32), axis=1)
    sublayer_rms = jnp.sqrt(
        jnp.sum(update * update, axis=(1, 2)) / (model_width * jnp.maximum(valid_count, 1.0))
    )
    cot_own = own_rows(cot_rows, first_own, seq_here)
    valid_own = own_rows(valid_rows, first_own, seq_here)
    inputs_own = own_rows(inputs, first_own, seq_here)
    mixed_own = own_rows(mixed_rows, first_own, seq_here)
    score_grad = jnp.sum(cot_own * branch_own, axis=-1) * valid_own
    branch_grad = gate_value[..., None] * cot_rows
    feed_grad = branch_grad.astype(jnp.bfloat16)
    active_grad = jnp.einsum(
        "skd,fd->skf", feed_grad, down_weight, preferred_element_type=jnp.float32
    )
    grad_down = jnp.einsum("skf,skd->fd", active, feed_grad, preferred_element_type=jnp.float32)
    _, gelu_back = jax.vjp(exact_gelu, upward)
    upward_grad = gelu_back(active_grad)[0].astype(jnp.bfloat16)
    grad_up = weight_grad(normed_two, upward_grad)
    normed_two_grad = lax.psum(
        project_back(upward_grad, up_weight).astype(jnp.bfloat16), "mp"
    ).astype(jnp.float32)
    _, second_back = jax.vjp(lambda value: rms_norm(value, second_gain), mixed_rows)
    mixed_grad = second_back(normed_two_grad)[0]
    grad_second = gain_grad(mixed_own, own_rows(normed_two_grad, first_own, seq_here))
    attended_grad = (branch_grad + mixed_grad).astype(jnp.bfloat16)
    grad_output = jnp.einsum(
        "skc,skd->cd", context, attended_grad, preferred_element_type=jnp.float32
    )
    context_grad = jnp.einsum(
        "skd,cd->skc", attended_grad, output_weight, preferred_element_type=jnp.float32
    )
    context_grad = context_grad.astype(jnp.bfloat16).reshape(head_shape)
    weights_full = jnp.exp(masked_scores() - log_total)
    weights_grad = jnp.einsum(
        "sqhe,skhe->shqk", context_grad, value_rows, preferred_element_type=jnp.float32
    )
    value_grad = jnp.einsum(
        "shqk,sqhe->skhe",
        weights_full.astype(jnp.bfloat16),
        context_grad,
        preferred_element_type=jnp.float32,
    )
    value_grad = value_grad.astype(jnp.bfloat16).reshape(flat_shape)
    scores_grad = weights_full * (
        weights_grad - jnp.sum(weights_grad * weights_full, axis=-1, keepdims=True)
    )
    scores_grad = scores_grad.astype(jnp.bfloat16)
    query_grad = (
        jnp.einsum("shqk,skhe->sqhe", scores_grad, key_rows, preferred_element_type=jnp.float32)
        * score_scale
    )
    query_grad = query_grad.astype(jnp.bfloat16).reshape(flat_shape)
    key_grad = (
        jnp.einsum("shqk,sqhe->skhe", scores_grad, query_rows, preferred_element_type=jnp.float32)
        * score_scale
    )
    key_grad = key_grad.astype(jnp.bfloat16).reshape(flat_shape)
    grad_query = weight_grad(normed, query_grad)
    grad_key = weight_grad(normed, key_grad)
    grad_value = weight_grad(normed, value_grad)
    total_term = project_back(query_grad, query_weight) + project_back(key_grad, key_weight)
    normed_grad_own = lax.psum_scatter(
        (total_term + project_back(value_grad, value_weight)).astype(jnp.bfloat16),
        "mp",
        scatter_dimension=0,
        tiled=True,
    ).astype(jnp.float32)
    _, first_back = jax.vjp(rms_norm, inputs_own, first_gain)
    inputs_grad, grad_first = first_back(normed_grad_own)
    inputs_grad = (
        inputs_grad + own_rows(mixed_grad, first_own, seq_here) + score_grad[..., None] * w_router
    )
    grad_router = jnp.einsum("sk,skd->d", score_grad, inputs_own, precision=lax.Precision.HIGHEST)
    grad_tokens = jax.vmap(place_rows)(cotangent.astype(jnp.float32), routed, inputs_grad).astype(
        jnp.bfloat16
    )
    grad_router, grad_first, grad_second = lax.psum(
        (grad_router, grad_first, grad_second), ("dp", "mp")
    )
    grad_query, grad_key, grad_value, grad_up, grad_output, grad_down = (
        lax.psum_scatter(
            grad_query.astype(jnp.bfloat16), "dp", scatter_dimension=0, tiled=True
        ).astype(jnp.float32),
        lax.psum_scatter(
            grad_key.astype(jnp.bfloat16), "dp", scatter_dimension=0, tiled=True
        ).astype(jnp.float32),
        lax.psum_scatter(
            grad_value.astype(jnp.bfloat16), "dp", scatter_dimension=0, tiled=True
        ).astype(jnp.float32),
        lax.psum_scatter(
            grad_up.astype(jnp.bfloat16), "dp", scatter_dimension=0, tiled=True
        ).astype(jnp.float32),
        lax.psum_scatter(
            grad_output.astype(jnp.bfloat16), "dp", scatter_dimension=1, tiled=True
        ).astype(jnp.float32),
        lax.psum_scatter(
            grad_down.astype(jnp.bfloat16), "dp", scatter_dimension=1, tiled=True
        ).astype(jnp.float32),
    )
    return (
        residual,
        grad_tokens,
        sublayer_rms,
        grad_router,
        grad_first,
        grad_query,
        grad_key,
        grad_value,
        grad_output,
        grad_second,
        grad_up,
        grad_down,
    )


def solution(mesh):
    in_specs = (
        P(("dp", "mp"), None, None),
        P(("dp", "mp"), None, None),
        P(("dp", "mp"), None),
        P(("dp", "mp"), None),
        P(),
        P(),
        P(None, "mp"),
        P(None, "mp"),
        P(None, "mp"),
        P("mp", None),
        P(),
        P(None, "mp"),
        P("mp", None),
    )
    out_specs = (
        P(("dp", "mp"), None, None),
        P(("dp", "mp"), None, None),
        P(("dp", "mp")),
        P(),
        P(),
        P("dp", "mp"),
        P("dp", "mp"),
        P("dp", "mp"),
        P("mp", "dp"),
        P(),
        P("dp", "mp"),
        P("mp", "dp"),
    )
    return jax.shard_map(shards, mesh=mesh, in_specs=in_specs, out_specs=out_specs, check_vma=False)
```

profile of v0, /device:TPU:0, one launch (start us, length us, event | category | flops | bytes accessed | tf_op | source)
XLA Modules:
  0.0 719.8 jit_solution(262898032237126460)
XLA Ops:
  18.6 48.7 %all-gather.4.cloned.1.call-done = bf16[4,256,1024]{2,1,0:T(8,128)(2,1)} async-done(((bf16[1,256,1024]{2,1,0:T(8,128)(2,1)}), bf16[4,256,1024]{2,1,0:T(8,128)(2,1)}) %all-gather.4.cloned.1.call-update) | async-done | bytes 2097168 | tf_op jit(solution)/shard_map/all_gather | solution.py:72
  84.4 9.1 %all-gather = bf16[4,1,256]{2,1,0:T(2,128)(2,1)S(1)} all-gather(bf16[1,1,256]{2,1,0:T(2,128)(2,1)S(1)} %convert_bitcast_fusion.2), channel_id=1, replica_groups=mesh['dp'=8,'mp'=4] {'mp'}, dimensions={0}, use_global_device_ids=true | all-gather | bytes 2560 | tf_op jit(solution)/shard_map/all_gather | solution.py:74
  96.8 70.4 %all-reduce.4.cloned.1.call-done = bf16[4,256,1024]{2,1,0:T(8,128)(2,1)} async-done(((bf16[4,256,1024]{2,1,0:T(8,128)(2,1)}), bf16[4,256,1024]{2,1,0:T(8,128)(2,1)}) %all-reduce.4.cloned.1.call-update) | async-done | bytes 2097168 | tf_op jit(solution)/shard_map/psum | solution.py:108
  177.7 10.5 %multiply_convert_fusion.1 = (bf16[4,256,1024]{2,1,0:T(8,128)(2,1)}, f32[4,256,1024]{2,1,0:T(8,128)}) fusion(f32[4,256,1024]{2,1,0:T(8,128)S(1)} %get-tuple-element.32, u8[256,1024]{1,0:T(8,128)(4,1)S(1)} %get-tuple-element.18, u8[256,1024]{1,0:T(8,128)(4,1)S(1)} %get-tuple-element.17), kind=kLoop, calls=%fused_computation.23 | loop fusion | flops 73400320 | bytes 11010048 | tf_op jit(solution)/shard_map/convert_element_type | solution.py:117
  188.2 26.1 %all-gather.6.cloned.1.call-done = bf16[4,256,1024]{2,1,0:T(8,128)(2,1)} async-done(((bf16[1,256,1024]{2,1,0:T(8,128)(2,1)}), bf16[4,256,1024]{2,1,0:T(8,128)(2,1)}) %all-gather.6.cloned.1.call-update) | async-done | bytes 2097168 | tf_op jit(solution)/shard_map/all_gather | solution.py:73
  214.4 8.1 %add_convert_fusion.2 = bf16[4,256,1024]{2,1,0:T(8,128)(2,1)S(1)} fusion(f32[4,256,1024]{2,1,0:T(8,128)} %get-tuple-element.25, f32[4,256,1024]{2,1,0:T(8,128)} %copy-done.18, bf16[1024,1024]{1,0:T(8,128)(2,1)} %param.27, bf16[4,256,1024]{2,1,0:T(8,128)(2,1)} %all-gather.6.cloned.1.call-done, f32[4,256]{1,0:T(4,128)S(1)} %bitcast_multiply_fusion), kind=kOutput, calls=%fused_computation.22 | convolution fusion | flops 2165309440 | bytes 14684160 | tf_op jit(solution)/shard_map/skd,fd->skf/dot_general | solution.py:141
  227.5 85.3 %all-reduce.6.cloned.1.call-done = bf16[4,256,1024]{2,1,0:T(8,128)(2,1)} async-done(((bf16[4,256,1024]{2,1,0:T(8,128)(2,1)}), bf16[4,256,1024]{2,1,0:T(8,128)(2,1)}) %all-reduce.6.cloned.1.call-update) | async-done | bytes 2097168 | tf_op jit(solution)/shard_map/psum | solution.py:148
  326.1 10.1 %reduce-scatter.21.cloned.1.call-start = ((), (), s32[]{:S(2)}) async-start(), calls=%async_computation.16 | async-start | bytes 589824 | tf_op jit(solution)/shard_map/reduce_scatter | solution.py:216
  342.2 5.8 multiply_reduce_fusion
  360.9 6.1 bitcast_convert_fusion
  371.0 6.2 bitcast_convert_fusion.1
  377.4 5.9 fusion.18
  389.7 6.6 bitcast_convert_fusion.3
  414.0 20.0 %reduce-scatter.19.cloned.1.call-done = bf16[128,256]{1,0:T(8,128)(2,1)} async-done(((bf16[1024,256]{1,0:T(8,128)(2,1)}), bf16[128,256]{1,0:T(8,128)(2,1)}) %reduce-scatter.19.cloned.1.call-update) | async-done | bytes 65552 | tf_op jit(solution)/shard_map/reduce_scatter | solution.py:213
  435.5 36.6 %reduce-scatter.17.cloned.1.call-done = bf16[128,256]{1,0:T(8,128)(2,1)} async-done(((bf16[1024,256]{1,0:T(8,128)(2,1)}), bf16[128,256]{1,0:T(8,128)(2,1)}) %reduce-scatter.17.cloned.1.call-update) | async-done | bytes 65552 | tf_op jit(solution)/shard_map/reduce_scatter | solution.py:210
  473.6 43.0 %reduce-scatter.27.cloned.1.call-done = bf16[128,1024]{1,0:T(8,128)(2,1)} async-done(((bf16[1024,1024]{1,0:T(8,128)(2,1)}), bf16[128,1024]{1,0:T(8,128)(2,1)}) %reduce-scatter.27.cloned.1.call-update) | async-done | bytes 262160
  518.6 42.8 %reduce-scatter.23.cloned.1.call-done = bf16[128,1024]{1,0:T(8,128)(2,1)} async-done(((bf16[1024,1024]{1,0:T(8,128)(2,1)}), bf16[128,1024]{1,0:T(8,128)(2,1)}) %reduce-scatter.23.cloned.1.call-update) | async-done | bytes 262160 | tf_op jit(solution)/shard_map/reduce_scatter | solution.py:219
  563.2 44.4 %reduce-scatter.13.cloned.1.call-done = bf16[1,256,1024]{2,1,0:T(8,128)(2,1)} async-done(((bf16[4,256,1024]{2,1,0:T(8,128)(2,1)}), bf16[1,256,1024]{2,1,0:T(8,128)(2,1)}) %reduce-scatter.13.cloned.1.call-update) | async-done | bytes 524304 | tf_op jit(solution)/shard_map/reduce_scatter | solution.py:118
  611.0 10.5 %scatter_custom_fusion = f32[2048,1024]{1,0:T(8,128)} fusion(f32[2048,1024]{1,0:T(8,128)} %bitcast_convert_fusion.3, s32[256]{0:T(256)S(1)} %bitcast.204, f32[256]{0:T(256)S(1)} %bitcast.199, bf16[1,256,1024]{2,1,0:T(8,128)(2,1)} %reduce-scatter.13.cloned.1.call-done, f32[4,256,1024]{2,1,0:T(8,128)} %convert_element_type.162, s32[]{:T(128)S(6)} %select_n.43, ...), kind=kCustom, calls=%fused_computation.86 | custom fusion | flops 1048576 | bytes 9963012 | tf_op jit(solution)/shard_map/vmap()/scatter-add | solution.py:44
  621.8 6.1 convert_bitcast_fusion.1
  627.9 25.2 %reduce-scatter.15.cloned.1.call-done = bf16[1,256,1024]{2,1,0:T(8,128)(2,1)} async-done(((bf16[4,256,1024]{2,1,0:T(8,128)(2,1)}), bf16[1,256,1024]{2,1,0:T(8,128)(2,1)}) %reduce-scatter.15.cloned.1.call-update) | async-done | bytes 524304 | tf_op jit(solution)/shard_map/reduce_scatter | solution.py:191
  654.8 10.9 %scatter_custom_fusion.1 = f32[2048,1024]{1,0:T(8,128)} fusion(f32[2048,1024]{1,0:T(8,128)} %bitcast_convert_fusion.2, s32[256]{0:T(256)S(1)} %bitcast.205, bf16[1,256,1024]{2,1,0:T(8,128)(2,1)} %reduce-scatter.15.cloned.1.call-done, f32[4,256,1024]{2,1,0:T(8,128)} %get-tuple-element.23, s32[]{:T(128)S(6)} %select_n.43, s32[]{:T(128)} %constant.52.clone.1, ...), kind=kCustom, calls=%fused_computation.85 | custom fusion | flops 2621440 | bytes 11021828 | tf_op jit(solution)/shard_map/vmap()/scatter-add | solution.py:44
  665.7 6.1 convert_bitcast_fusion
  671.7 39.7 %all-reduce = (f32[1024]{0:T(1024)}, f32[1024]{0:T(1024)}, f32[1024]{0:T(1024)}) all-reduce(f32[1024]{0:T(1024)S(1)} %bitcast.196, f32[1024]{0:T(1024)S(1)} %get-tuple-element.13, f32[1024]{0:T(1024)S(1)} %multiply_reduce_fusion.4), channel_id=1, replica_groups=mesh['dp'=8,'mp'=4] {'dp','mp'}, use_global_device_ids=true, to_apply=%region_17.19 | all-reduce | flops 3072 | bytes 24576 | tf_op jit(solution)/shard_map/psum | solution.py:206
  (168 shorter events, 118.2 us)
Async XLA Ops:
  7.2 165.1 %copy-start = (bf16[1024,1024]{1,0:T(8,128)(2,1)S(1)}, bf16[1024,1024]{1,0:T(8,128)(2,1)}, u32[]{:S(2)}) copy-start(bf16[1024,1024]{1,0:T(8,128)(2,1)} %param.26) | copy-start | bytes 6291460
  7.2 60.1 %all-gather.4.cloned.1.call-start = ((), (), s32[]{:S(2)}) async-start(), calls=%async_computation.8 | async-start | bytes 2621440 | tf_op jit(solution)/shard_map/all_gather | solution.py:72
  13.1 56.5 %copy-start.32 = (f32[1024]{0:T(1024)S(1)}, f32[1024]{0:T(1024)}, u32[]{:S(2)}) copy-start(f32[1024]{0:T(1024)} %param.20) | copy-start | bytes 12292
  18.5 148.7 %all-reduce.4.cloned.1.call-start = ((), (), s32[]{:S(2)}) async-start(), calls=%async_computation.9 | async-start | bytes 4194304 | tf_op jit(solution)/shard_map/psum | solution.py:108
  78.9 14.5 %copy-start.31 = (f32[1024]{0:T(1024)S(1)}, f32[1024]{0:T(1024)}, u32[]{:S(2)}) copy-start(f32[1024]{0:T(1024)} %param.19) | copy-start | bytes 12292
  81.8 132.6 %all-gather.6.cloned.1.call-start = ((), (), s32[]{:S(2)}) async-start(), calls=%async_computation.11 | async-start | bytes 2621440 | tf_op jit(solution)/shard_map/all_gather | solution.py:73
  82.5 230.3 %all-reduce.6.cloned.1.call-start = ((), (), s32[]{:S(2)}) async-start(), calls=%async_computation.12 | async-start | bytes 4194304 | tf_op jit(solution)/shard_map/psum | solution.py:148
  96.8 75.5 %copy-start.30 = (f32[1024]{0:T(1024)S(1)}, f32[1024]{0:T(1024)}, u32[]{:S(2)}) copy-start(f32[1024]{0:T(1024)} %param.25) | copy-start | bytes 12292
  167.2 5.1 copy-start.4
  167.2 5.1 copy-start.7
  227.5 89.5 %copy-start.5 = (bf16[4,256,1024]{2,1,0:T(8,128)(2,1)S(1)}, bf16[4,256,1024]{2,1,0:T(8,128)(2,1)}, u32[]{:S(2)}) copy-start(bf16[4,256,1024]{2,1,0:T(8,128)(2,1)} %all-gather.4.cloned.1.call-done) | copy-start | bytes 6291460
  227.5 183.4 %reduce-scatter.25.cloned.1.call-start = ((), (), s32[]{:S(2)}) async-start(), calls=%async_computation.18 | async-start | bytes 589824
  326.1 86.4 %reduce-scatter.21.cloned.1.call-start = ((), (), s32[]{:S(2)}) async-start(), calls=%async_computation.16 | async-start | bytes 589824 | tf_op jit(solution)/shard_map/reduce_scatter | solution.py:216
  348.0 86.0 %reduce-scatter.19.cloned.1.call-start = ((), (), s32[]{:S(2)}) async-start(), calls=%async_computation.15 | async-start | bytes 589824 | tf_op jit(solution)/shard_map/reduce_scatter | solution.py:213
  356.7 115.4 %reduce-scatter.17.cloned.1.call-start = ((), (), s32[]{:S(2)}) async-start(), calls=%async_computation.14 | async-start | bytes 589824 | tf_op jit(solution)/shard_map/reduce_scatter | solution.py:210
  360.9 155.8 %reduce-scatter.27.cloned.1.call-start = ((), (), s32[]{:S(2)}) async-start(), calls=%async_computation.19 | async-start | bytes 2359296
  371.0 190.4 %reduce-scatter.23.cloned.1.call-start = ((), (), s32[]{:S(2)}) async-start(), calls=%async_computation.17 | async-start | bytes 2359296 | tf_op jit(solution)/shard_map/reduce_scatter | solution.py:219
  377.3 230.3 %reduce-scatter.13.cloned.1.call-start = ((), (), s32[]{:S(2)}) async-start(), calls=%async_computation.10 | async-start | bytes 2621440 | tf_op jit(solution)/shard_map/reduce_scatter | solution.py:118
  383.2 269.8 %reduce-scatter.15.cloned.1.call-start = ((), (), s32[]{:S(2)}) async-start(), calls=%async_computation.13 | async-start | bytes 2621440 | tf_op jit(solution)/shard_map/reduce_scatter | solution.py:191
  389.7 6.6 copy-start.13
  402.1 6.1 copy-start.14
  404.6 5.0 copy-start.15
  404.6 5.6 copy-start.12
  654.8 56.6 %copy-start.1 = (bf16[1024,1024]{1,0:T(8,128)(2,1)S(1)}, bf16[1024,1024]{1,0:T(8,128)(2,1)}, u32[]{:S(2)}) copy-start(bf16[1024,1024]{1,0:T(8,128)(2,1)} %param.26) | copy-start | bytes 6291460
  (23 other events, 59.2 us)
Sparse Core Ops, SparseCore 0:
  18.6 48.6 all-gather.3
  81.9 85.2 all-reduce.3
  169.4 44.8 all-gather.5
  227.6 85.2 all-reduce.5
  326.2 33.0 reduce-scatter.24
  362.6 34.1 reduce-scatter.20
  399.8 34.1 reduce-scatter.18
  437.9 34.1 reduce-scatter.16
  475.4 41.1 reduce-scatter.26
  520.1 41.2 reduce-scatter.22
  563.7 43.8 reduce-scatter.12
  609.8 43.1 reduce-scatter.14
where the time goes:
time: 729 us; the launch traced here: 720 us
  waiting for transfers between devices  443 us (61%)
  other arithmetic  97.1 us (13%)
  matrix products  72.1 us (10%)
  blocking collectives  48.8 us (7%)
  local copies, waits for them, and re-layouts  30 us (4%)
  between operations  17.6 us (2%)
  starting transfers between devices  10.7 us (1%)
    psum x1, waiting for transfers between devices, shards(): lax.psum(project_back(upward_grad, up_weight).astype(jnp.bfloat16), 'mp')  85.3 us
    psum x1, waiting for transfers between devices, shards(): lax.psum(jnp.einsum('skc,cd->skd', context, output_weight, preferred_elem...  70.4 us
    all_gather x1, waiting for transfers between devices, shards(): lax.all_gather(sent_tokens, 'mp', axis=0, tiled=True)  48.7 us
    reduce_scatter x1, waiting for transfers between devices, shards(): lax.psum_scatter(jnp.einsum('skf,fd->skd', active, down_weight, preferred...  44.4 us
    unnamed x14, waiting for transfers between devices  43.9 us
    reduce_scatter x1, waiting for transfers between devices, shards(): lax.psum_scatter(grad_up.astype(jnp.bfloat16), 'dp', scatter_dimension=0,...  42.8 us
    psum x1, blocking collectives, shards(): lax.psum((grad_router, grad_first, grad_second), ('dp', 'mp'))  39.7 us
    reduce_scatter x1, waiting for transfers between devices, shards(): lax.psum_scatter(grad_query.astype(jnp.bfloat16), 'dp', scatter_dimension...  36.6 us
  transfers between devices with their start and end apart: 12, of which 10 were waited for; matrix products, arithmetic and copies ran while one was open for 17% of the time, Pallas kernels for 0%

commit v1 on v0

v1 whole, which is shorter than its diff:
```python
import functools
import math

import jax
import jax.numpy as jnp
from jax import lax
from jax.experimental import pallas as pl
from jax.experimental.pallas import tpu as pltpu
from jax.sharding import PartitionSpec as P

HEADS = 16
HEAD_DIM = 64
EPS = 1e-06
F32 = jnp.float32
BF16 = jnp.bfloat16
TILE = 64


def mm(left, right):
    return jnp.dot(left, right, preferred_element_type=F32)


def mm_nt(left, right):
    return lax.dot_general(left, right, (((1,), (1,)), ((), ())), preferred_element_type=F32)


def mm_tn(left, right):
    return lax.dot_general(left, right, (((0,), (0,)), ((), ())), preferred_element_type=F32)


def row_tiles(rows, body, init=0):
    def step(index, carry):
        return body(pl.ds(pl.multiple_of(index * TILE, TILE), TILE), carry)

    return lax.fori_loop(0, rows // TILE, step, init)


def fold_rows(value):
    return jnp.sum(value.reshape(-1, 8, value.shape[-1]), axis=0)


def gelu_both(value):
    cdf = 0.5 * (1.0 + lax.erf(value * math.sqrt(0.5)))
    density = jnp.exp(-0.5 * value * value) * (1.0 / math.sqrt(2.0 * math.pi))
    return value * cdf, cdf + value * density


def block_kernel(size, *refs):
    shards, ybit, rows, width, length = size["S"], size["ybit"], size["R"], size["D"], size["L"]
    heads, narrow, hidden, cut = size["hh"], size["n"], size["f"], size["DB"]
    joined = size["joined"]
    quarter = 2 * cut
    refs = list(refs)

    def take(count):
        taken, refs[:count] = refs[:count], []
        return taken

    tokens, cotangent, routed, valid, w_router, first_gain, second_gain = take(7)
    qkv_in = take(1 if joined else 3)
    out_in, up_in, down_in = take(3)
    rows_res, rows_grad, rms_out, small_out, attn_out, feed_out = take(6)
    w_qkv, w_out, w_up, w_down = take(4)
    h1, dfeed, h2, datt, turn_a, turn_b = take(6)
    qkv, ctx, prob, act, dup = take(5)
    dqkv = take(1)[0] if joined else act.at[0, :, 0 : 3 * narrow]
    total, wide, sent, got = take(4)
    own_z, own_c, attended, dmixed, feed_own, columns = take(6)
    lane = lax.broadcasted_iota(jnp.int32, (1, 128), 1)

    def column(k, at):
        return columns[at][:, k : k + 1]

    def set_column(k, at, value):
        columns[at] = jnp.where(lane == k, value, columns[at])

    gate, live, dscore = (functools.partial(column, k) for k in range(3))
    grads, core_f, y_f, z_f, core_a, y_a, z_a, swap_f, swap_a = take(9)
    small_send, small_got = take(2)
    load_sem, tok_sem = take(2)
    wz_s, wz_r, wy_s, wy_r, wc_s, wc_r = take(6)
    x_s, x_r = take(2)
    gc_s, gc_r, gy_s, gy_r, gz_s, gz_r, gx_s, gx_r = take(8)
    sm_s, sm_r = take(2)

    dp = lax.axis_index("dp")
    z = lax.axis_index("mp")
    core = lax.rem(dp, 2)
    x = lax.rem(lax.div(dp, 2), 2)
    y = lax.rem(lax.div(dp, ybit), 2)
    core_dev = (dp + 1 - 2 * core, z)
    x_dev = (dp + 2 * (1 - 2 * x), z)
    y_dev = (dp + ybit * (1 - 2 * y), z)
    up_dev = (dp, z + 1)
    down_dev = (dp, z - 1)
    z_bits = [1 << k for k in range(int(math.log2(shards)))]
    z_partners = [(dp, z + bit * (1 - 2 * lax.rem(lax.div(z, bit), 2))) for bit in z_bits]

    def remote(src, dst, send, recv, device):
        return pltpu.make_async_remote_copy(
            src_ref=src,
            dst_ref=dst,
            send_sem=send,
            recv_sem=recv,
            device_id=device,
            device_id_type=pl.DeviceIdType.MESH,
        )

    barrier = pltpu.get_barrier_semaphore()

    def greet(device):
        pl.semaphore_signal(barrier, inc=1, device_id=device, device_id_type=pl.DeviceIdType.MESH)

    for device in [core_dev, x_dev, y_dev] + z_partners[1:]:
        greet(device)

    @pl.when(z > 0)
    def _():
        greet(down_dev)

    @pl.when(z < shards - 1)
    def _():
        greet(up_dev)

    ends = jnp.where(z == 0, 1, 0) + jnp.where(z == shards - 1, 1, 0)
    pl.semaphore_wait(barrier, 4 + len(z_partners) - ends)

    def order(j):
        high = lax.div(z, shards // 2)
        base = z + high * (shards - 1 - 2 * z)
        odd = lax.rem(j, 2)
        near = base + lax.div(j + 1, 2) * (2 * odd - 1)
        pick = jnp.where(j <= 2 * base, near, j)
        return pick + high * (shards - 1 - 2 * pick)

    attn_mats = list(range(len(qkv_in) + 1))
    feed_mats = [len(attn_mats), len(attn_mats) + 1]
    out_at, up_at = attn_mats[-1], feed_mats[0]

    def span(qy, qc):
        return pl.ds(pl.multiple_of((2 * qy + qc) * quarter, quarter), quarter)

    def lanes(count):
        return pl.ds(pl.multiple_of(x * count, count), count)

    def held(i, s, qy, qc):
        if i < out_at:
            part = w_qkv if joined else w_qkv.at[:, :, i * narrow : (i + 1) * narrow]
            return part.at[s, span(qy, qc)]
        if i == out_at:
            return w_out.at[s, :, span(qy, qc)]
        if i == up_at:
            return w_up.at[s, qy, qc]
        return w_down.at[s, :, span(qy, qc)]

    def own_piece(i):
        if i < out_at:
            part = qkv_in[i].at[span(y, core)]
            return part if joined else part.at[:, lanes(narrow)]
        if i == out_at:
            return out_in.at[lanes(narrow), span(y, core)]
        if i == up_at:
            return up_in.at[y, core, :, :, lanes(hidden)]
        return down_in.at[lanes(hidden), span(y, core)]

    def load_own(i):
        if i < out_at:
            if joined:
                src, dst = qkv_in[i], w_qkv.at[z]
            else:
                src, dst = qkv_in[i].at[:, lanes(narrow)], w_qkv.at[z, :, i * narrow : (i + 1) * narrow]
        elif i == out_at:
            src, dst = out_in.at[lanes(narrow), :], w_out.at[z]
        elif i == up_at:
            src, dst = up_in.at[:, :, :, :, lanes(hidden)], w_up.at[z]
        else:
            src, dst = down_in.at[lanes(hidden), :], w_down.at[z]
        return pltpu.make_async_copy(src, dst, load_sem.at[i])

    def own_up(i):
        return remote(own_piece(i), held(i, z, y, core), wz_s.at[i, z], wz_r.at[i, z], up_dev)

    def own_down(i):
        return remote(own_piece(i), held(i, z, y, core), wz_s.at[i, shards], wz_r.at[i, z], down_dev)

    def pass_on(i, s, device):
        piece = held(i, s, y, core)
        return remote(piece, piece, wz_s.at[i, s], wz_r.at[i, s], device)

    def across_y(i, s, qy):
        piece = held(i, s, qy, core)
        return remote(piece, piece, wy_s.at[i, s], wy_r.at[i, s], y_dev)

    def across_core(i, s, qy, qc, slot):
        piece = held(i, s, qy, qc)
        return remote(piece, piece, wc_s.at[i, slot, s], wc_r.at[i, slot, s], core_dev)

    def send_own(mats):
        @pl.when(z < shards - 1)
        def _():
            for i in mats:
                own_up(i).start()

        @pl.when(z > 0)
        def _():
            for i in mats:
                own_down(i).start()

    def passing(s, action):
        @pl.when((s < z) & (z < shards - 1))
        def _():
            action(up_dev)

        @pl.when((s > z) & (z > 0))
        def _():
            action(down_dev)

    def arrive(mats, j):
        s = order(j)
        for i in mats:
            pass_on(i, s, up_dev).wait_recv()
            passing(s, lambda device: pass_on(i, s, device).start())
            across_y(i, s, y).start()
            across_core(i, s, y, core, 0).start()

    def complete(mats, j):
        s = order(j)
        for i in mats:
            across_y(i, s, 1 - y).wait_recv()
            across_core(i, s, 1 - y, core, 1).start()
        for i in mats:
            across_core(i, s, y, 1 - core, 0).wait_recv()
            across_core(i, s, 1 - y, 1 - core, 1).wait_recv()

    def drain(mats):
        @pl.when(z < shards - 1)
        def _():
            for i in mats:
                own_up(i).wait_send()

        @pl.when(z > 0)
        def _():
            for i in mats:
                own_down(i).wait_send()

        def step(j, carry):
            s = order(j)
            for i in mats:
                passing(s, lambda device: pass_on(i, s, device).wait_send())
                across_y(i, s, y).wait_send()
                across_core(i, s, y, core, 0).wait_send()
                across_core(i, s, 1 - y, core, 1).wait_send()
            return carry

        lax.fori_loop(1, shards, step, 0)

    def exchange(slot, src, dst):
        return remote(src, dst, x_s.at[slot], x_r.at[slot], x_dev)

    x_h1 = exchange(0, h1.at[0], h1.at[1])
    x_dfeed = exchange(1, dfeed.at[0], dfeed.at[1])
    x_att = exchange(2, sent.at[0], got.at[0])
    x_h2 = exchange(3, h2.at[0], h2.at[1])
    x_dh2 = exchange(4, sent.at[0], got.at[0])
    x_feed = exchange(5, sent.at[1], got.at[1])
    x_datt = exchange(6, datt.at[0], datt.at[1])
    x_dh1 = exchange(7, sent.at[0], got.at[0])

    send_own(attn_mats)
    steps = length // rows

    def block_loads(t):
        slot = lax.rem(t, 2)
        where = pl.ds(pl.multiple_of(t * rows, rows), rows)
        return (
            pltpu.make_async_copy(tokens.at[0, where], got.at[slot], tok_sem.at[0, slot]),
            pltpu.make_async_copy(cotangent.at[0, where], sent.at[slot], tok_sem.at[1, slot]),
        )

    for copy in block_loads(0):
        copy.start()
    for i in attn_mats + feed_mats:
        load_own(i).start()

    as_rows = jnp.broadcast_to(routed[...].astype(F32), (8, rows))
    position = jnp.transpose(as_rows)[:, 0:1].astype(jnp.int32)
    total[...] = jnp.zeros_like(total)

    def gather(t, flags):
        @pl.when(t + 1 < steps)
        def _():
            for copy in block_loads(t + 1):
                copy.start()

        slot = lax.rem(t, 2)
        for copy in block_loads(t):
            copy.wait()
        hit = position == t * rows + lax.broadcasted_iota(jnp.int32, (rows, rows), 1)
        chosen = jnp.where(hit, 1.0, 0.0)
        pick = chosen.astype(BF16)
        total[0] += mm(pick, got[slot])
        total[1] += mm(pick, sent[slot])
        mask = valid[:, pl.ds(pl.multiple_of(t * rows, rows), rows)].astype(F32)
        return flags + jnp.sum(chosen * mask, axis=1, keepdims=True)

    flags = lax.fori_loop(0, steps, gather, jnp.zeros((rows, 1), F32))
    columns[...] = jnp.broadcast_to(flags, columns.shape)

    def prepare(at, carry):
        row, cot = total[0, at], total[1, at]
        own_z[at] = row.astype(BF16)
        own_c[at] = cot.astype(BF16)
        gate_here = jnp.sum(row * w_router[...], axis=1, keepdims=True) * live(at)
        set_column(0, at, gate_here)
        factor = lax.rsqrt(jnp.mean(row * row, axis=1, keepdims=True) + EPS)
        h1[0, at] = (row * factor * first_gain[...]).astype(BF16)
        dfeed[0, at] = (gate_here * cot).astype(BF16)
        return carry

    row_tiles(rows, prepare)
    x_h1.start()

    lane_head = lax.div(lax.broadcasted_iota(jnp.int32, (1, narrow), 1), HEAD_DIM)
    masks = [jnp.where(lane_head == h, 1.0, 0.0) for h in range(heads)]
    masks_low = [mask.astype(BF16) for mask in masks]

    def stacked(value):
        return jnp.concatenate([value * mask for mask in masks_low], axis=0) if heads > 1 else value

    def unstacked(value):
        if heads == 1:
            return value
        picked = value[0:rows] * masks[0]
        for h in range(1, heads):
            picked = picked + value[h * rows : (h + 1) * rows] * masks[h]
        return picked

    score_shape = (heads * rows, rows)
    causal = lax.rem(lax.broadcasted_iota(jnp.int32, score_shape, 0), rows) >= lax.broadcasted_iota(
        jnp.int32, score_shape, 1
    )

    for i in attn_mats:
        load_own(i).wait()
    x_h1.wait_recv()
    x_dfeed.start()

    def attend(j, carry):
        s = order(j)

        @pl.when(j + 1 < shards)
        def _():
            arrive(attn_mats, j + 1)

        @pl.when(j + 1 == shards)
        def _():
            send_own(feed_mats)

        @pl.when(j > 0)
        def _():
            complete(attn_mats, j)

        low = mm(h1[...].reshape(2 * rows, width), w_qkv[s]).astype(BF16)
        query = low[:, 0:narrow] * jnp.asarray(HEAD_DIM**-0.5, BF16)
        qkv[s] = jnp.concatenate([query, low[:, narrow:]], axis=1).reshape(2, rows, 3 * narrow)
        for half in range(2):
            query = qkv[s, half, :, 0:narrow]
            key = qkv[s, half, :, narrow : 2 * narrow]
            value = qkv[s, half, :, 2 * narrow : 3 * narrow]
            scores = jnp.where(causal, mm_nt(stacked(query), key), -1e30)
            raised = jnp.exp(scores - jnp.max(scores, axis=1, keepdims=True))
            weights = (raised / jnp.sum(raised, axis=1, keepdims=True)).astype(BF16)
            prob[s, half] = weights
            ctx[s, half * rows : (half + 1) * rows] = unstacked(mm(weights, value)).astype(BF16)
        return carry

    lax.fori_loop(0, shards, attend, 0)

    def project_out(half):
        parts = [ctx[s, half * rows : (half + 1) * rows] for s in range(shards)]
        return mm(jnp.concatenate(parts, axis=1), w_out[...].reshape(shards * narrow, width))

    sent[0] = project_out(1).astype(BF16)
    x_att.start()
    attended[...] = project_out(0)
    arrive(feed_mats, 1)
    x_att.wait()

    def mix(at, carry):
        att = attended[at] + got[0, at].astype(F32)
        attended[at] = att
        mixed = own_z[at].astype(F32) + att
        factor = lax.rsqrt(jnp.mean(mixed * mixed, axis=1, keepdims=True) + EPS)
        h2[0, at] = (mixed * factor * second_gain[...]).astype(BF16)
        return carry

    row_tiles(rows, mix)
    x_h2.start()
    x_dfeed.wait_recv()
    arrive(feed_mats, 2)
    x_h2.wait_recv()

    total[...] = jnp.zeros_like(total)
    for i in feed_mats:
        load_own(i).wait()

    def feed_step(j, carry):
        s = order(j)

        @pl.when((j > 0) & (j + 2 < shards))
        def _():
            arrive(feed_mats, j + 2)

        @pl.when(j > 0)
        def _():
            complete(feed_mats, j)

        up_here = w_up[s].reshape(width, hidden)
        wide[0] = mm(h2[...].reshape(2 * rows, width), up_here)
        wide[1] = mm_nt(dfeed[...].reshape(2 * rows, width), w_down[s])

        def turn(at, inner):
            active, slope = gelu_both(wide[0, at])
            act[s, at] = active.astype(BF16)
            dup[s, at] = (wide[1, at] * slope).astype(BF16)
            return inner

        row_tiles(2 * rows, turn)
        total[...] += mm_nt(dup[s], up_here).reshape(2, rows, width)
        return carry

    lax.fori_loop(0, shards, feed_step, 0)
    sent[0] = total[1].astype(BF16)
    x_dh2.start()

    def feed_rows(half):
        value = mm(act[0, half * rows : (half + 1) * rows], w_down[0])
        for s in range(1, shards):
            value += mm(act[s, half * rows : (half + 1) * rows], w_down[s])
        return value

    sent[1] = feed_rows(1).astype(BF16)
    feed_own[...] = feed_rows(0)

    def core_send(group, buf, into, s, at=None):
        src = buf.at[s, :, :, 1 - core]
        return remote(src, into.at[s], gc_s.at[group, s], gc_r.at[group, s], core_dev)

    def y_send(group, buf, into, s):
        return remote(buf.at[s, 1 - y, :, core], into.at[s], gy_s.at[group, s], gy_r.at[group, s], y_dev)

    def z_send(group, buf, into, s, device, slot):
        src = buf.at[s, y, :, core]
        return remote(src, into.at[slot], gz_s.at[group, s], gz_r.at[group, slot], device)

    def add_into(ref, *others):
        value = ref[...].astype(F32)
        for other in others:
            value = value + other[...].astype(F32)
        ref[...] = value.astype(BF16)

    def stage_core(group, buf, core_got, y_got, s):
        core_send(group, buf, core_got, s).wait_recv()
        for a in range(2):
            for b in range(2):
                add_into(buf.at[s, a, b, core], core_got.at[s, a, b])
        y_send(group, buf, y_got, s).start()

    def stage_y(group, buf, y_got, s):
        y_send(group, buf, y_got, s).wait_recv()
        for b in range(2):
            add_into(buf.at[s, y, b, core], y_got.at[s, b])

    def line_in(group, buf, z_got, s, slot):
        z_send(group, buf, z_got, s, up_dev, slot).wait_recv()
        for b in range(2):
            add_into(buf.at[s, y, b, core], z_got.at[slot, b])

    def stage_z(group, buf, z_got, s, action):
        @pl.when(s > z)
        def _():
            if action == "start":

                @pl.when(z > 0)
                def _():
                    line_in(group, buf, z_got, s, s)

            copy = z_send(group, buf, z_got, s, up_dev, s)
            copy.start() if action == "start" else copy.wait_send()

        @pl.when(s < z)
        def _():
            if action == "start":

                @pl.when(z < shards - 1)
                def _():
                    line_in(group, buf, z_got, s, s)

            slot = jnp.where(s == z - 1, shards, s)
            copy = z_send(group, buf, z_got, s, down_dev, slot)
            copy.start() if action == "start" else copy.wait_send()

    def swap(group, pair):
        return remote(pair.at[0], pair.at[1], gx_s.at[group], gx_r.at[group], x_dev)

    def stage_last(group, buf, z_got, pair, out):
        for b in range(2):
            out[b] = buf[z, y, b, core].astype(F32)

        @pl.when(z > 0)
        def _():
            z_send(group, buf, z_got, z, up_dev, z).wait_recv()
            out[...] += z_got[z].astype(F32)

        @pl.when(z < shards - 1)
        def _():
            z_send(group, buf, z_got, z, up_dev, shards).wait_recv()
            out[...] += z_got[shards].astype(F32)

        pair[0] = out[1 - x].astype(BF16)
        swap(group, pair).start()

    def stage_out(group, pair, out):
        swap(group, pair).wait_recv()
        out[1 - x] = pair[1].astype(F32)

    def reversed_order(k):
        return order(shards - 1 - k)

    def store_grads(buf, s, left, right, lo, count):
        for a in range(2):
            for b in range(2):
                start = (2 * a + b) * quarter
                value = mm(left[start : start + quarter, :], right).astype(BF16)
                buf[s, a, b, :, :, lo : lo + count] = value.reshape(2, cut, count)

    turn_a[...] = jnp.transpose(h2[...].reshape(2 * rows, width))
    turn_b[...] = jnp.transpose(dfeed[...].reshape(2 * rows, width))

    def feed_grads(k, carry):
        s = reversed_order(k)
        store_grads(grads, s, turn_a, dup[s], 0, hidden)
        store_grads(grads, s, turn_b, act[s], hidden, hidden)
        core_send(0, grads, core_f, s).start()

        @pl.when(k > 0)
        def _():
            stage_core(0, grads, core_f, y_f, reversed_order(k - 1))

        return carry

    x_dh2.wait()

    def second_back(at, carry):
        dh2 = total[0, at] + got[0, at].astype(F32)
        mixed = own_z[at].astype(F32) + attended[at]
        factor = lax.rsqrt(jnp.mean(mixed * mixed, axis=1, keepdims=True) + EPS)
        scaled = dh2 * second_gain[...]
        back = factor * scaled - mixed * (factor**3 * jnp.mean(mixed * scaled, axis=1, keepdims=True))
        dmixed[at] = back
        datt[0, at] = (gate(at) * own_c[at].astype(F32) + back).astype(BF16)
        return carry + fold_rows(dh2 * mixed * factor)

    second_sum = row_tiles(rows, second_back, jnp.zeros((8, width), F32))
    x_datt.start()
    x_feed.start()

    lax.fori_loop(0, shards, feed_grads, 0)
    stage_core(0, grads, core_f, y_f, z)
    x_datt.wait_recv()

    drain(feed_mats)
    turn_a[...] = jnp.transpose(h1[...].reshape(2 * rows, width))
    turn_b[...] = jnp.transpose(datt[...].reshape(2 * rows, width))
    total[...] = jnp.zeros_like(total)

    def attend_back(k, carry):
        s = reversed_order(k)
        dctx = mm_nt(datt[...].reshape(2 * rows, width), w_out[s]).astype(BF16)
        for half in range(2):
            query = qkv[s, half, :, 0:narrow]
            key = qkv[s, half, :, narrow : 2 * narrow]
            value = qkv[s, half, :, 2 * narrow : 3 * narrow]
            weights = prob[s, half]
            dhead = stacked(dctx[half * rows : (half + 1) * rows])
            dweights = mm_nt(dhead, value)
            full = weights.astype(F32)
            dscores = full * (dweights - jnp.sum(dweights * full, axis=1, keepdims=True))
            dscores = dscores.astype(BF16)
            dquery = unstacked(mm(dscores, key)) * HEAD_DIM**-0.5
            dkey = mm_tn(dscores, stacked(query))
            dvalue = mm_tn(weights, dhead)
            dqkv[half * rows : (half + 1) * rows] = jnp.concatenate([dquery, dkey, dvalue], axis=1).astype(BF16)
        total[...] += mm_nt(dqkv[...], w_qkv[s]).reshape(2, rows, width)
        store_grads(w_up, s, turn_a, dqkv[...], 0, 3 * narrow)
        store_grads(w_up, s, turn_b, ctx[s], 3 * narrow, narrow)
        core_send(1, w_up, core_a, s).start()
        return carry

    lax.fori_loop(0, shards, attend_back, 0)
    sent[0] = total[1].astype(BF16)
    x_dh1.start()

    x_feed.wait()

    def finish_forward(at, squares):
        branch = attended[at] + feed_own[at] + got[1, at].astype(F32)
        update = gate(at) * branch
        rows_res[at] = (own_z[at].astype(F32) + update).astype(BF16)
        dgate = jnp.sum(own_c[at].astype(F32) * branch, axis=1, keepdims=True)
        set_column(2, at, dgate * live(at))
        return squares + fold_rows(update * update)

    squares = row_tiles(rows, finish_forward, jnp.zeros((8, width), F32))
    count = jnp.sum(valid[...].astype(F32), axis=1, keepdims=True)
    energy = jnp.sum(jnp.sum(squares, axis=0, keepdims=True), axis=1, keepdims=True)
    rms_out[...] = jnp.broadcast_to(jnp.sqrt(energy / (width * jnp.maximum(count, 1.0))), rms_out.shape)

    def feed_line(k, carry):
        s = reversed_order(k)
        stage_y(0, grads, y_f, s)
        stage_z(0, grads, z_f, s, "start")
        return carry

    lax.fori_loop(0, shards - 1, feed_line, 0)
    stage_y(0, grads, y_f, z)
    stage_last(0, grads, z_f, swap_f, feed_out)

    def attn_core(k, carry):
        stage_core(1, w_up, core_a, y_a, reversed_order(k))
        return carry

    lax.fori_loop(0, shards, attn_core, 0)

    x_dh1.wait()

    def first_back(at, sums):
        dh1 = total[0, at] + got[0, at].astype(F32)
        row = own_z[at].astype(F32)
        factor = lax.rsqrt(jnp.mean(row * row, axis=1, keepdims=True) + EPS)
        scaled = dh1 * first_gain[...]
        back = factor * scaled - row * (factor**3 * jnp.mean(row * scaled, axis=1, keepdims=True))
        back = back + dmixed[at] + dscore(at) * w_router[...]
        rows_grad[at] = (own_c[at].astype(F32) + back).astype(BF16)
        return sums[0] + fold_rows(dscore(at) * row), sums[1] + fold_rows(dh1 * row * factor)

    zero = jnp.zeros((8, width), F32)
    router_sum, first_sum = row_tiles(rows, first_back, (zero, zero))
    parts = [jnp.sum(part, axis=0, keepdims=True) for part in (router_sum, first_sum, second_sum)]
    small = jnp.concatenate(parts + [jnp.zeros((5, width), F32)], axis=0)
    for k, device in enumerate([core_dev, x_dev, y_dev] + z_partners):
        small_send[k] = small
        copy = remote(small_send.at[k], small_got.at[k], sm_s.at[k], sm_r.at[k], device)
        copy.start()
        copy.wait()
        small = small + small_got[k]
    small_out[...] = small

    def attn_line(k, carry):
        s = reversed_order(k)
        stage_y(1, w_up, y_a, s)
        stage_z(1, w_up, z_a, s, "start")
        return carry

    lax.fori_loop(0, shards - 1, attn_line, 0)
    stage_y(1, w_up, y_a, z)
    stage_last(1, w_up, z_a, swap_a, attn_out)
    stage_out(0, swap_f, feed_out)
    stage_out(1, swap_a, attn_out)

    drain(attn_mats)
    for copy in (x_h1, x_dfeed, x_h2, x_datt):
        copy.wait_send()

    def drain_grads(k, carry):
        s = reversed_order(k)
        for group, buf, core_got, y_got, z_got in (
            (0, grads, core_f, y_f, z_f),
            (1, w_up, core_a, y_a, z_a),
        ):
            core_send(group, buf, core_got, s).wait_send()
            y_send(group, buf, y_got, s).wait_send()
            stage_z(group, buf, z_got, s, "wait")
        return carry

    lax.fori_loop(0, shards, drain_grads, 0)
    swap(0, swap_f).wait_send()
    swap(1, swap_a).wait_send()


def run_block(size, operands):
    shards, rows, width = size["S"], size["R"], size["D"]
    heads, narrow, hidden, cut = size["hh"], size["n"], size["f"], size["DB"]
    mats = (2 if size["joined"] else 4) + 2
    stages = 3 + int(math.log2(shards))
    attn, feed = 4 * narrow, 2 * hidden
    dma = pltpu.SemaphoreType.DMA
    vmem = lambda *shape: pltpu.VMEM(shape, BF16)
    full = lambda *shape: pltpu.VMEM(shape, F32)
    scratch = [
        vmem(shards, width, 3 * narrow),
        vmem(shards, narrow, width),
        vmem(shards, 2, 2, 2, cut, hidden),
        vmem(shards, hidden, width),
        *[vmem(2, rows, width) for _ in range(4)],
        *[vmem(width, 2 * rows) for _ in range(2)],
        vmem(shards, 2, rows, 3 * narrow),
        vmem(shards, 2 * rows, narrow),
        vmem(shards, 2, heads * rows, rows),
        vmem(shards, 2 * rows, hidden),
        vmem(shards, 2 * rows, hidden),
        *([vmem(2 * rows, 3 * narrow)] if size["joined"] else []),
        full(2, rows, width),
        full(2, 2 * rows, hidden),
        vmem(2, rows, width),
        vmem(2, rows, width),
        vmem(rows, width),
        vmem(rows, width),
        *[full(rows, width) for _ in range(3)],
        full(rows, 128),
        vmem(shards, 2, 2, 2, cut, feed),
        vmem(shards, 2, 2, cut, feed),
        vmem(shards, 2, cut, feed),
        vmem(shards + 1, 2, cut, feed),
        vmem(shards, 2, 2, cut, attn),
        vmem(shards, 2, cut, attn),
        vmem(shards + 1, 2, cut, attn),
        vmem(2, cut, feed),
        vmem(2, cut, attn),
        full(stages, 8, width),
        full(stages, 8, width),
        dma((mats,)),
        dma((2, 2)),
        dma((mats, shards + 1)),
        dma((mats, shards)),
        dma((mats, shards)),
        dma((mats, shards)),
        dma((mats, 2, shards)),
        dma((mats, 2, shards)),
        dma((8,)),
        dma((8,)),
        *[dma((2, shards)) for _ in range(5)],
        dma((2, shards + 1)),
        dma((2,)),
        dma((2,)),
        dma((stages,)),
        dma((stages,)),
    ]
    near = pl.BlockSpec(memory_space=pltpu.VMEM)
    far = pl.BlockSpec(memory_space=pl.ANY)
    outs = [
        jax.ShapeDtypeStruct((rows, width), BF16),
        jax.ShapeDtypeStruct((rows, width), BF16),
        jax.ShapeDtypeStruct((8, 128), F32),
        jax.ShapeDtypeStruct((8, width), F32),
        jax.ShapeDtypeStruct((2, cut, attn), F32),
        jax.ShapeDtypeStruct((2, cut, feed), F32),
    ]
    return pl.pallas_call(
        functools.partial(block_kernel, size),
        out_shape=outs,
        in_specs=[far, far] + [near] * 5 + [far] * (len(operands) - 7),
        out_specs=[near] * len(outs),
        scratch_shapes=scratch,
        compiler_params=pltpu.CompilerParams(
            collective_id=0, has_side_effects=True, vmem_limit_bytes=64 * 2**20 - 65536
        ),
    )(*operands)


def place_kernel(size, assemble, routed, tok, cot, rows_res, rows_grad, attn, feed, *outs):
    block, count = tok.shape[0], routed.shape[1]
    step = pl.program_id(0)
    line = step * block + lax.broadcasted_iota(jnp.int32, (block, count), 0)
    chosen = jnp.where(line == routed[...], 1.0, 0.0)
    taken = jnp.sum(chosen, axis=1, keepdims=True) > 0.0
    pick = chosen.astype(BF16)
    outs[0][...] = jnp.where(taken, mm(pick, rows_res[...]), tok[...].astype(F32)).astype(BF16)
    outs[1][...] = jnp.where(taken, mm(pick, rows_grad[...]), cot[...].astype(F32)).astype(BF16)
    if assemble:

        @pl.when(step == 0)
        def _():
            for ref, value in zip(outs[2:], weight_outputs(size, attn, feed)):
                ref[...] = value


def weight_outputs(size, attn, feed):
    narrow, hidden = size["n"], size["f"]

    def side_by_side(ref, lo, count):
        return jnp.concatenate([ref[0, :, lo : lo + count], ref[1, :, lo : lo + count]], axis=1)

    return (
        side_by_side(attn, 0, narrow),
        side_by_side(attn, narrow, narrow),
        side_by_side(attn, 2 * narrow, narrow),
        side_by_side(attn, 3 * narrow, narrow).T,
        side_by_side(feed, 0, hidden),
        side_by_side(feed, hidden, hidden).T,
    )


def place_rows(size, routed, tokens, cotangent, rows_res, rows_grad, attn, feed, assemble):
    length, width, rows = size["L"], size["D"], size["R"]
    block = 256
    cut, narrow, hidden = size["DB"], size["n"], size["f"]
    whole = lambda *shape: pl.BlockSpec(shape, lambda i: (0,) * len(shape))
    moving = pl.BlockSpec((block, width), lambda i: (i, 0))
    outs = [jax.ShapeDtypeStruct((length, width), BF16)] * 2
    out_specs = [moving] * 2
    if assemble:
        shapes = [(cut, 2 * narrow)] * 3 + [(2 * narrow, cut), (cut, 2 * hidden), (2 * hidden, cut)]
        outs = outs + [jax.ShapeDtypeStruct(shape, F32) for shape in shapes]
        out_specs = out_specs + [whole(*shape) for shape in shapes]
    return pl.pallas_call(
        functools.partial(place_kernel, size, assemble),
        grid=(length // block,),
        out_shape=outs,
        in_specs=[
            whole(1, rows),
            moving,
            moving,
            whole(rows, width),
            whole(rows, width),
            whole(*attn.shape),
            whole(*feed.shape),
        ],
        out_specs=out_specs,
        compiler_params=pltpu.CompilerParams(vmem_limit_bytes=48 * 2**20),
    )(routed, tokens, cotangent, rows_res, rows_grad, attn, feed)


def shards_of(
    groups,
    tokens,
    cotangent,
    routed,
    valid_mask,
    w_router,
    first_gain,
    query_weight,
    key_weight,
    value_weight,
    output_weight,
    second_gain,
    up_weight,
    down_weight,
):
    shards, data = lax.axis_size("mp"), lax.axis_size("dp")
    _, length, width = tokens.shape
    rows = routed.shape[1]
    narrow = query_weight.shape[1] // 2
    hidden = up_weight.shape[1] // 2
    cut = width // 8
    chips_x = 1 << ((data // 2).bit_length() - 1) // 2
    size = dict(
        S=shards, ybit=2 * chips_x, R=rows, D=width, L=length, hh=narrow // HEAD_DIM,
        n=narrow, f=hidden, DB=cut, joined=narrow % 128 != 0,
    )
    dp = lax.axis_index("dp")
    x, y = (dp // 2) % 2, (dp // size["ybit"]) % 2
    qkv = (query_weight, key_weight, value_weight)
    if size["joined"]:
        halves = [lax.dynamic_slice_in_dim(weight, x * narrow, narrow, 1) for weight in qkv]
        qkv = (jnp.concatenate(halves, axis=1),)
    row = lambda vector: vector.reshape(1, width)
    operands = (
        tokens, cotangent, routed, valid_mask, row(w_router), row(first_gain), row(second_gain),
        *qkv, output_weight, up_weight.reshape(2, 2, 2, cut, 2 * hidden), down_weight,
    )
    rows_res, rows_grad, rms, small, attn, feed = run_block(size, operands)
    whole_group = data == 8
    if not whole_group:
        block = 4 * y + 2 * x + dp % 2

        def over_groups(part):
            base = jnp.zeros((2, width, part.shape[2]), F32)
            placed = lax.dynamic_update_slice_in_dim(base, part, block * cut, 1)
            return lax.psum_scatter(placed, "dp", scatter_dimension=1, tiled=True)

        attn, feed = over_groups(attn), over_groups(feed)
        small = lax.psum(small, "dp") / 8.0
    placed = place_rows(size, routed, tokens[0], cotangent[0], rows_res, rows_grad, attn, feed, whole_group)
    residual, grad_tokens = placed[:2]
    weights = placed[2:] if whole_group else weight_outputs(size, attn, feed)
    grad_query, grad_key, grad_value, grad_output, grad_up, grad_down = weights
    return (
        residual[None],
        grad_tokens[None],
        rms[0, 0:1],
        small[0],
        small[1],
        grad_query,
        grad_key,
        grad_value,
        grad_output,
        small[2],
        grad_up,
        grad_down,
    )


def solution(mesh):
    in_specs = (
        P(("dp", "mp"), None, None),
        P(("dp", "mp"), None, None),
        P(("dp", "mp"), None),
        P(("dp", "mp"), None),
        P(),
        P(),
        P(None, "mp"),
        P(None, "mp"),
        P(None, "mp"),
        P("mp", None),
        P(),
        P(None, "mp"),
        P("mp", None),
    )
    out_specs = (
        P(("dp", "mp"), None, None),
        P(("dp", "mp"), None, None),
        P(("dp", "mp")),
        P(),
        P(),
        P("dp", "mp"),
        P("dp", "mp"),
        P("dp", "mp"),
        P("mp", "dp"),
        P(),
        P("dp", "mp"),
        P("mp", "dp"),
    )
    body = functools.partial(shards_of, mesh.shape["dp"] // 8)
    return jax.shard_map(body, mesh=mesh, in_specs=in_specs, out_specs=out_specs, check_vma=False)
```

time: 729 us -> 260 us (0.36); the launches traced: 720 us -> 259 us
  waiting for transfers between devices: 443 us -> 0 us
  Pallas kernels: 0 us -> 251 us
  other arithmetic: 97.1 us -> 0 us
  matrix products: 72.1 us -> 0 us
  blocking collectives: 48.8 us -> 0 us
  local copies, waits for them, and re-layouts: 30 us -> 7.69 us
  between operations: 17.6 us -> 0.82 us
  starting transfers between devices: 10.7 us -> 0 us
    pallas_call x0 -> x2, Pallas kernels: none -> 251 us  [the longest x1 240 us: run_block(): pl.pallas_call(functools.partial(block_kernel, size), out_shape=outs, in_...]
    reduce_scatter x6 -> x0, waiting for transfers between devices: 169 us -> none  [the longest x1 44.4 us: shards(): lax.psum_scatter(jnp.einsum('skf,fd->skd', active, down_weight, preferred...]
    psum x2 -> x0, waiting for transfers between devices: 156 us -> none  [the longest x1 85.3 us: shards(): lax.psum(project_back(upward_grad, up_weight).astype(jnp.bfloat16), 'mp')]
    all_gather x2 -> x0, waiting for transfers between devices: 74.8 us -> none  [the longest x1 48.7 us: shards(): lax.all_gather(sent_tokens, 'mp', axis=0, tiled=True)]
    dot_general x26 -> x0, matrix products: 72.1 us -> none  [the longest x4 11.7 us: weight_grad(): jnp.einsum('skd,skc->dc', left, right, preferred_element_type=jnp.float32)]
    convert_element_type x18 -> x0, other arithmetic: 55.3 us -> none  [the longest x1 10.5 us: shards(): active = exact_gelu(upward).astype(jnp.bfloat16)]
    unnamed x14 -> x0, waiting for transfers between devices: 43.9 us -> none
    psum x1 -> x0, blocking collectives: 39.7 us -> none  [shards(): lax.psum((grad_router, grad_first, grad_second), ('dp', 'mp'))]
  transfers between devices with their start and end apart: 12 -> 0, of which waited for: 10 -> 0; matrix products, arithmetic and copies ran while one was open for 17% -> 0% of each run, Pallas kernels for 0% -> 0%
where the time goes in v1:
time: 260 us; the launch traced here: 259 us
  Pallas kernels  251 us (97%)
  local copies, waits for them, and re-layouts  7.69 us (3%)
    pallas_call x1, Pallas kernels, run_block(): pl.pallas_call(functools.partial(block_kernel, size), out_shape=outs, in_...  240 us
    pallas_call x1, Pallas kernels, place_rows(): pl.pallas_call(functools.partial(place_kernel, size, assemble), grid=(len...  11.2 us

profile of v1, /device:TPU:0, one launch (start us, length us, event | category | flops | bytes accessed | tf_op | source)
XLA Modules:
  0.0 259.3 jit_solution(12457569467980294744)
XLA Ops:
  0.6 239.6 %shard_map.220 = (bf16[256,1024]{1,0:T(8,128)(2,1)}, bf16[256,1024]{1,0:T(8,128)(2,1)}, f32[8,128]{1,0:T(8,128)}, f32[8,1024]{1,0:T(8,128)}, f32[2,128,512]{2,1,0:T(8,128)}, /*index=5*/f32[2,128,1024]{2,1,0:T(8,128)}) custom-call(bf16[1,2048,1024]{2,1,0:T(8,128)(2,1)} %refs_0_.1, bf16[1,2048,1024]{2,1,0:T(8,128)(2,1)} %refs_1_.1, s32[1,256]{1,0:T(1,128)} %routed.1, ...), custom_call_target="tpu_custom_call" | custom-call | tf_op jit(solution)/shard_map/pallas_call | solution.py:759
  240.3 1.2 slice.12
  241.5 1.5 fusion
  243.0 0.0 copy-start
  243.0 1.2 copy-done
  244.2 0.0 copy-start.1
  244.2 1.0 copy-done.1
  245.2 0.0 copy-start.2
  245.2 1.0 copy-done.2
  246.3 0.0 copy-start.3
  246.3 1.0 copy-done.3
  247.3 0.0 copy-start.4
  247.3 0.7 copy-done.4
  248.0 11.2 %shard_map.221 = (bf16[2048,1024]{1,0:T(8,128)(2,1)}, bf16[2048,1024]{1,0:T(8,128)(2,1)}, f32[128,256]{1,0:T(8,128)}, f32[128,256]{1,0:T(8,128)}, f32[128,256]{1...) custom-call(s32[1,256]{1,0:T(1,128)S(1)} %copy-done.4, bf16[2048,1024]{1,0:T(8,128)(2,1)} %bitcast.12, ...), custom_call_target="tpu_custom_call" | custom-call | tf_op jit(solution)/shard_map/pallas_call | solution.py:816
Async XLA Ops:
  243.0 1.2 copy-start
  244.2 1.0 copy-start.1
  245.2 1.0 copy-start.2
  246.3 1.0 copy-start.3
  247.3 0.7 copy-start.4

commit v2 on v1

--- a/solution.py
+++ b/solution.py
@@ -59,11 +59,10 @@
     tokens, cotangent, routed, valid, w_router, first_gain, second_gain = take(7)
     qkv_in = take(1 if joined else 3)
     out_in, up_in, down_in = take(3)
-    rows_res, rows_grad, rms_out, small_out, attn_out, feed_out = take(6)
+    outputs = take(5)
     w_qkv, w_out, w_up, w_down = take(4)
     h1, dfeed, h2, datt, turn_a, turn_b = take(6)
     qkv, ctx, prob, act, dup = take(5)
-    dqkv = take(1)[0] if joined else act.at[0, :, 0 : 3 * narrow]
     total, wide, sent, got = take(4)
     own_z, own_c, attended, dmixed, feed_own, columns = take(6)
     lane = lax.broadcasted_iota(jnp.int32, (1, 128), 1)
@@ -76,8 +75,9 @@
 
     gate, live, dscore = (functools.partial(column, k) for k in range(3))
     grads, core_f, y_f, z_f, core_a, y_a, z_a, swap_f, swap_a = take(9)
+    attn_out, feed_out = take(2)
     small_send, small_got = take(2)
-    load_sem, tok_sem = take(2)
+    load_sem, tok_sem, out_sem = take(3)
     wz_s, wz_r, wy_s, wy_r, wc_s, wc_r = take(6)
     x_s, x_r = take(2)
     gc_s, gc_r, gy_s, gy_r, gz_s, gz_r, gx_s, gx_r = take(8)
@@ -93,8 +93,10 @@
     y_dev = (dp + ybit * (1 - 2 * y), z)
     up_dev = (dp, z + 1)
     down_dev = (dp, z - 1)
+    x_dp = dp + 2 * (1 - 2 * x)
     z_bits = [1 << k for k in range(int(math.log2(shards)))]
-    z_partners = [(dp, z + bit * (1 - 2 * lax.rem(lax.div(z, bit), 2))) for bit in z_bits]
+    small_devices = [core_dev, x_dev, (x_dp + ybit * (1 - 2 * y), z)]
+    small_devices += [(x_dp, z + bit * (1 - 2 * lax.rem(lax.div(z, bit), 2))) for bit in z_bits]
 
     def remote(src, dst, send, recv, device):
         return pltpu.make_async_remote_copy(
@@ -105,25 +107,6 @@
             device_id=device,
             device_id_type=pl.DeviceIdType.MESH,
         )
-
-    barrier = pltpu.get_barrier_semaphore()
-
-    def greet(device):
-        pl.semaphore_signal(barrier, inc=1, device_id=device, device_id_type=pl.DeviceIdType.MESH)
-
-    for device in [core_dev, x_dev, y_dev] + z_partners[1:]:
-        greet(device)
-
-    @pl.when(z > 0)
-    def _():
-        greet(down_dev)
-
-    @pl.when(z < shards - 1)
-    def _():
-        greet(up_dev)
-
-    ends = jnp.where(z == 0, 1, 0) + jnp.where(z == shards - 1, 1, 0)
-    pl.semaphore_wait(barrier, 4 + len(z_partners) - ends)
 
     def order(j):
         high = lax.div(z, shards // 2)
@@ -195,16 +178,13 @@
         piece = held(i, s, qy, qc)
         return remote(piece, piece, wc_s.at[i, slot, s], wc_r.at[i, slot, s], core_dev)
 
-    def send_own(mats):
-        @pl.when(z < shards - 1)
-        def _():
-            for i in mats:
-                own_up(i).start()
-
-        @pl.when(z > 0)
-        def _():
-            for i in mats:
-                own_down(i).start()
+    def send_own_up(mats):
+        for i in mats:
+            own_up(i).start()
+
+    def send_own_down(mats):
+        for i in mats:
+            own_down(i).start()
 
     def passing(s, action):
         @pl.when((s < z) & (z < shards - 1))
@@ -223,11 +203,26 @@
             across_y(i, s, y).start()
             across_core(i, s, y, core, 0).start()
 
-    def complete(mats, j):
+    def arrive_attn(j):
+        arrive(attn_mats, j)
+        s = order(j)
+
+        @pl.when((s == 0) & (z < shards - 1))
+        def _():
+            send_own_up(feed_mats)
+
+        @pl.when((s == shards - 1) & (z > 0))
+        def _():
+            send_own_down(feed_mats)
+
+    def relay(mats, j):
         s = order(j)
         for i in mats:
             across_y(i, s, 1 - y).wait_recv()
             across_core(i, s, 1 - y, core, 1).start()
+
+    def settle(mats, j):
+        s = order(j)
         for i in mats:
             across_core(i, s, y, 1 - core, 0).wait_recv()
             across_core(i, s, 1 - y, 1 - core, 1).wait_recv()
@@ -266,44 +261,78 @@
     x_datt = exchange(6, datt.at[0], datt.at[1])
     x_dh1 = exchange(7, sent.at[0], got.at[0])
 
-    send_own(attn_mats)
-    steps = length // rows
+    def put(k, src):
+        return pltpu.make_async_copy(src, outputs[k], out_sem.at[k])
+
+    steps = length // (2 * rows)
+    stages = ((got, sent), (h2, datt))
 
     def block_loads(t):
-        slot = lax.rem(t, 2)
-        where = pl.ds(pl.multiple_of(t * rows, rows), rows)
-        return (
-            pltpu.make_async_copy(tokens.at[0, where], got.at[slot], tok_sem.at[0, slot]),
-            pltpu.make_async_copy(cotangent.at[0, where], sent.at[slot], tok_sem.at[1, slot]),
-        )
-
-    for copy in block_loads(0):
-        copy.start()
+        copies = []
+        for k, (array, buf) in enumerate(zip((tokens, cotangent), stages[t % 2])):
+            for half in range(2):
+                src = array.at[0, (2 * t + half) * rows : (2 * t + half + 1) * rows]
+                copies.append(pltpu.make_async_copy(src, buf.at[half], tok_sem.at[t % 2, k, half]))
+        return copies
+
+    for t in range(2):
+        for copy in block_loads(t):
+            copy.start()
     for i in attn_mats + feed_mats:
         load_own(i).start()
 
+    barrier = pltpu.get_barrier_semaphore()
+
+    def greet(device):
+        pl.semaphore_signal(barrier, inc=1, device_id=device, device_id_type=pl.DeviceIdType.MESH)
+
+    for device in [y_dev] + small_devices:
+        greet(device)
+
+    @pl.when(z > 0)
+    def _():
+        greet(down_dev)
+
+    @pl.when(z < shards - 1)
+    def _():
+        greet(up_dev)
+
+    ends = jnp.where(z == 0, 1, 0) + jnp.where(z == shards - 1, 1, 0)
+    pl.semaphore_wait(barrier, 3 + len(small_devices) - ends)
+
+    @pl.when(z < shards - 1)
+    def _():
+        send_own_up(attn_mats)
+
+    @pl.when(z > 0)
+    def _():
+        send_own_down(attn_mats)
+
+    @pl.when(z == 0)
+    def _():
+        send_own_up(feed_mats)
+
+    @pl.when(z == shards - 1)
+    def _():
+        send_own_down(feed_mats)
+
     as_rows = jnp.broadcast_to(routed[...].astype(F32), (8, rows))
     position = jnp.transpose(as_rows)[:, 0:1].astype(jnp.int32)
-    total[...] = jnp.zeros_like(total)
-
-    def gather(t, flags):
-        @pl.when(t + 1 < steps)
-        def _():
-            for copy in block_loads(t + 1):
-                copy.start()
-
-        slot = lax.rem(t, 2)
+    flags = jnp.zeros((rows, 1), F32)
+    for t in range(steps):
         for copy in block_loads(t):
             copy.wait()
-        hit = position == t * rows + lax.broadcasted_iota(jnp.int32, (rows, rows), 1)
+        hit = position == 2 * t * rows + lax.broadcasted_iota(jnp.int32, (rows, 2 * rows), 1)
         chosen = jnp.where(hit, 1.0, 0.0)
         pick = chosen.astype(BF16)
-        total[0] += mm(pick, got[slot])
-        total[1] += mm(pick, sent[slot])
-        mask = valid[:, pl.ds(pl.multiple_of(t * rows, rows), rows)].astype(F32)
-        return flags + jnp.sum(chosen * mask, axis=1, keepdims=True)
-
-    flags = lax.fori_loop(0, steps, gather, jnp.zeros((rows, 1), F32))
+        for k, buf in enumerate(stages[t % 2]):
+            picked = mm(pick, buf[...].reshape(2 * rows, width))
+            total[k] = picked if t == 0 else total[k] + picked
+        if t + 2 < steps:
+            for copy in block_loads(t + 2):
+                copy.start()
+        mask = valid[:, 2 * t * rows : 2 * (t + 1) * rows].astype(F32)
+        flags = flags + jnp.sum(chosen * mask, axis=1, keepdims=True)
     columns[...] = jnp.broadcast_to(flags, columns.shape)
 
     def prepare(at, carry):
@@ -319,6 +348,7 @@
 
     row_tiles(rows, prepare)
     x_h1.start()
+    x_dfeed.start()
 
     lane_head = lax.div(lax.broadcasted_iota(jnp.int32, (1, narrow), 1), HEAD_DIM)
     masks = [jnp.where(lane_head == h, 1.0, 0.0) for h in range(heads)]
@@ -342,23 +372,23 @@
 
     for i in attn_mats:
         load_own(i).wait()
+    arrive_attn(1)
+    for j in range(2, shards):
+        arrive_attn(j)
+        relay(attn_mats, j - 1)
     x_h1.wait_recv()
-    x_dfeed.start()
 
     def attend(j, carry):
         s = order(j)
 
-        @pl.when(j + 1 < shards)
-        def _():
-            arrive(attn_mats, j + 1)
-
         @pl.when(j + 1 == shards)
         def _():
-            send_own(feed_mats)
+            arrive(feed_mats[:1], 1)
+            relay(attn_mats, j)
 
         @pl.when(j > 0)
         def _():
-            complete(attn_mats, j)
+            settle(attn_mats, j)
 
         low = mm(h1[...].reshape(2 * rows, width), w_qkv[s]).astype(BF16)
         query = low[:, 0:narrow] * jnp.asarray(HEAD_DIM**-0.5, BF16)
@@ -383,7 +413,8 @@
     sent[0] = project_out(1).astype(BF16)
     x_att.start()
     attended[...] = project_out(0)
-    arrive(feed_mats, 1)
+    arrive(feed_mats[1:], 1)
+    arrive(feed_mats[:1], 2)
     x_att.wait()
 
     def mix(at, carry):
@@ -396,51 +427,8 @@
 
     row_tiles(rows, mix)
     x_h2.start()
+    arrive(feed_mats[1:], 2)
     x_dfeed.wait_recv()
-    arrive(feed_mats, 2)
-    x_h2.wait_recv()
-
-    total[...] = jnp.zeros_like(total)
-    for i in feed_mats:
-        load_own(i).wait()
-
-    def feed_step(j, carry):
-        s = order(j)
-
-        @pl.when((j > 0) & (j + 2 < shards))
-        def _():
-            arrive(feed_mats, j + 2)
-
-        @pl.when(j > 0)
-        def _():
-            complete(feed_mats, j)
-
-        up_here = w_up[s].reshape(width, hidden)
-        wide[0] = mm(h2[...].reshape(2 * rows, width), up_here)
-        wide[1] = mm_nt(dfeed[...].reshape(2 * rows, width), w_down[s])
-
-        def turn(at, inner):
-            active, slope = gelu_both(wide[0, at])
-            act[s, at] = active.astype(BF16)
-            dup[s, at] = (wide[1, at] * slope).astype(BF16)
-            return inner
-
-        row_tiles(2 * rows, turn)
-        total[...] += mm_nt(dup[s], up_here).reshape(2, rows, width)
-        return carry
-
-    lax.fori_loop(0, shards, feed_step, 0)
-    sent[0] = total[1].astype(BF16)
-    x_dh2.start()
-
-    def feed_rows(half):
-        value = mm(act[0, half * rows : (half + 1) * rows], w_down[0])
-        for s in range(1, shards):
-            value += mm(act[s, half * rows : (half + 1) * rows], w_down[s])
-        return value
-
-    sent[1] = feed_rows(1).astype(BF16)
-    feed_own[...] = feed_rows(0)
 
     def core_send(group, buf, into, s, at=None):
         src = buf.at[s, :, :, 1 - core]
@@ -529,26 +517,108 @@
 
     def store_grads(buf, s, left, right, lo, count):
         for a in range(2):
-            for b in range(2):
-                start = (2 * a + b) * quarter
-                value = mm(left[start : start + quarter, :], right).astype(BF16)
-                buf[s, a, b, :, :, lo : lo + count] = value.reshape(2, cut, count)
-
-    turn_a[...] = jnp.transpose(h2[...].reshape(2 * rows, width))
-    turn_b[...] = jnp.transpose(dfeed[...].reshape(2 * rows, width))
-
-    def feed_grads(k, carry):
-        s = reversed_order(k)
+            value = mm(left[2 * a * quarter : 2 * (a + 1) * quarter, :], right).astype(BF16)
+            buf[s, a, :, :, :, lo : lo + count] = value.reshape(2, 2, cut, count)
+
+    total[...] = jnp.zeros_like(total)
+    for i in feed_mats:
+        load_own(i).wait()
+    def feed_grads(s):
         store_grads(grads, s, turn_a, dup[s], 0, hidden)
         store_grads(grads, s, turn_b, act[s], hidden, hidden)
         core_send(0, grads, core_f, s).start()
 
+    def feed_chunk(s, half):
+        part = pl.ds(pl.multiple_of(half * rows, rows), rows)
+        up_here = w_up[s].reshape(width, hidden)
+        wide[0] = mm(h2[half], up_here)
+        wide[1] = mm_nt(dfeed[half], w_down[s])
+
+        def turn(at, inner):
+            active, slope = gelu_both(wide[0, at])
+            out = pl.ds(pl.multiple_of(half * rows + at.start, TILE), TILE)
+            act[s, out] = active.astype(BF16)
+            dup[s, out] = (wide[1, at] * slope).astype(BF16)
+            return inner
+
+        row_tiles(rows, turn)
+        total[half] += mm_nt(dup[s, part], up_here)
+
+    def own_step(j, carry):
+        @pl.when(j > 0)
+        def _():
+            settle(feed_mats, j)
+
+        feed_chunk(order(j), 0)
+
+        @pl.when((j > 0) & (j + 2 < shards))
+        def _():
+            arrive(feed_mats[1:], j + 2)
+
+        @pl.when(j + 2 < shards)
+        def _():
+            relay(feed_mats, j + 1)
+
+        @pl.when(j + 3 < shards)
+        def _():
+            arrive(feed_mats[:1], j + 3)
+
+        return carry
+
+    lax.fori_loop(0, shards - 1, own_step, 0)
+    x_h2.wait_recv()
+    turn_a[...] = jnp.transpose(h2[...].reshape(2 * rows, width))
+    turn_b[...] = jnp.transpose(dfeed[...].reshape(2 * rows, width))
+
+    def other_step(j, carry):
+        feed_chunk(order(j), 1)
+
+        @pl.when(j == 0)
+        def _():
+            feed_grads(z)
+
+        @pl.when(j == 1)
+        def _():
+            stage_core(0, grads, core_f, y_f, z)
+
+        return carry
+
+    lax.fori_loop(0, shards - 1, other_step, 0)
+    relay(feed_mats, shards - 1)
+    settle(feed_mats, shards - 1)
+
+    def last_step(k, carry):
+        feed_chunk(order(shards - 1), 1 - k)
+
+        @pl.when(k == 0)
+        def _():
+            sent[0] = total[1].astype(BF16)
+            x_dh2.start()
+
+        return carry
+
+    lax.fori_loop(0, 2, last_step, 0)
+
+    def feed_grads_step(k, carry):
+        feed_grads(reversed_order(k))
+
         @pl.when(k > 0)
         def _():
             stage_core(0, grads, core_f, y_f, reversed_order(k - 1))
 
         return carry
 
+    lax.fori_loop(0, shards - 1, feed_grads_step, 0)
+    stage_core(0, grads, core_f, y_f, order(1))
+
+    def feed_rows(half):
+        value = mm(act[0, half * rows : (half + 1) * rows], w_down[0])
+        for s in range(1, shards):
+            value += mm(act[s, half * rows : (half + 1) * rows], w_down[s])
+        return value
+
+    sent[1] = feed_rows(1).astype(BF16)
+    feed_own[...] = feed_rows(0)
     x_dh2.wait()
 
     def second_back(at, carry):
@@ -565,24 +635,17 @@
     x_datt.start()
     x_feed.start()
 
-    lax.fori_loop(0, shards, feed_grads, 0)
-    stage_core(0, grads, core_f, y_f, z)
-    x_datt.wait_recv()
-
-    drain(feed_mats)
-    turn_a[...] = jnp.transpose(h1[...].reshape(2 * rows, width))
-    turn_b[...] = jnp.transpose(datt[...].reshape(2 * rows, width))
-    total[...] = jnp.zeros_like(total)
-
-    def attend_back(k, carry):
-        s = reversed_order(k)
-        dctx = mm_nt(datt[...].reshape(2 * rows, width), w_out[s]).astype(BF16)
-        for half in range(2):
+    def attend_back(half):
+        part = slice(half * rows, (half + 1) * rows)
+
+        def step(k, carry):
+            s = reversed_order(k)
+            dctx = mm_nt(datt[half], w_out[s]).astype(BF16)
             query = qkv[s, half, :, 0:narrow]
             key = qkv[s, half, :, narrow : 2 * narrow]
             value = qkv[s, half, :, 2 * narrow : 3 * narrow]
             weights = prob[s, half]
-            dhead = stacked(dctx[half * rows : (half + 1) * rows])
+            dhead = stacked(dctx)
             dweights = mm_nt(dhead, value)
             full = weights.astype(F32)
             dscores = full * (dweights - jnp.sum(dweights * full, axis=1, keepdims=True))
@@ -590,47 +653,89 @@
             dquery = unstacked(mm(dscores, key)) * HEAD_DIM**-0.5
             dkey = mm_tn(dscores, stacked(query))
             dvalue = mm_tn(weights, dhead)
-            dqkv[half * rows : (half + 1) * rows] = jnp.concatenate([dquery, dkey, dvalue], axis=1).astype(BF16)
-        total[...] += mm_nt(dqkv[...], w_qkv[s]).reshape(2, rows, width)
-        store_grads(w_up, s, turn_a, dqkv[...], 0, 3 * narrow)
+            act[s, part, 0 : 3 * narrow] = jnp.concatenate([dquery, dkey, dvalue], axis=1).astype(BF16)
+            return carry
+
+        lax.fori_loop(0, shards, step, 0)
+
+    def dh1_rows(half):
+        part = slice(half * rows, (half + 1) * rows)
+        value = mm_nt(act[0, part, 0 : 3 * narrow], w_qkv[0])
+        for s in range(1, shards):
+            value += mm_nt(act[s, part, 0 : 3 * narrow], w_qkv[s])
+        return value
+
+    attend_back(0)
+    total[0] = dh1_rows(0)
+    turn_a[...] = jnp.transpose(h1[...].reshape(2 * rows, width))
+    drain(feed_mats)
+    edge = (z == 0) | (z == shards - 1)
+
+    @pl.when(edge)
+    def _():
+        far = reversed_order(0)
+        stage_y(0, grads, y_f, far)
+        stage_z(0, grads, z_f, far, "start")
+
+    x_datt.wait_recv()
+    turn_b[...] = jnp.transpose(datt[...].reshape(2 * rows, width))
+    attend_back(1)
+    sent[0] = dh1_rows(1).astype(BF16)
+    x_dh1.start()
+
+    def attn_grads(k, carry):
+        s = reversed_order(k)
+        store_grads(w_up, s, turn_a, act[s, :, 0 : 3 * narrow], 0, 3 * narrow)
         store_grads(w_up, s, turn_b, ctx[s], 3 * narrow, narrow)
         core_send(1, w_up, core_a, s).start()
+
+        @pl.when(k > 0)
+        def _():
+            stage_core(1, w_up, core_a, y_a, reversed_order(k - 1))
+
         return carry
 
-    lax.fori_loop(0, shards, attend_back, 0)
-    sent[0] = total[1].astype(BF16)
-    x_dh1.start()
-
+    @pl.when(edge)
+    def _():
+        near = reversed_order(1)
+        stage_y(0, grads, y_f, near)
+        stage_z(0, grads, z_f, near, "start")
+
+    lax.fori_loop(0, shards, attn_grads, 0)
+    stage_core(1, w_up, core_a, y_a, z)
+
+    def line_step(group, buf, y_got, z_got):
+        def step(k, carry):
+            s = reversed_order(k)
+            stage_y(group, buf, y_got, s)
+            stage_z(group, buf, z_got, s, "start")
+            return carry
+
+        return step
+
+    feed_line = line_step(0, grads, y_f, z_f)
+    attn_line = line_step(1, w_up, y_a, z_a)
     x_feed.wait()
 
     def finish_forward(at, squares):
         branch = attended[at] + feed_own[at] + got[1, at].astype(F32)
         update = gate(at) * branch
-        rows_res[at] = (own_z[at].astype(F32) + update).astype(BF16)
+        sent[1, at] = (own_z[at].astype(F32) + update).astype(BF16)
         dgate = jnp.sum(own_c[at].astype(F32) * branch, axis=1, keepdims=True)
         set_column(2, at, dgate * live(at))
         return squares + fold_rows(update * update)
 
     squares = row_tiles(rows, finish_forward, jnp.zeros((8, width), F32))
+    put(0, sent.at[1]).start()
     count = jnp.sum(valid[...].astype(F32), axis=1, keepdims=True)
     energy = jnp.sum(jnp.sum(squares, axis=0, keepdims=True), axis=1, keepdims=True)
-    rms_out[...] = jnp.broadcast_to(jnp.sqrt(energy / (width * jnp.maximum(count, 1.0))), rms_out.shape)
-
-    def feed_line(k, carry):
-        s = reversed_order(k)
-        stage_y(0, grads, y_f, s)
-        stage_z(0, grads, z_f, s, "start")
-        return carry
-
-    lax.fori_loop(0, shards - 1, feed_line, 0)
-    stage_y(0, grads, y_f, z)
-    stage_last(0, grads, z_f, swap_f, feed_out)
-
-    def attn_core(k, carry):
-        stage_core(1, w_up, core_a, y_a, reversed_order(k))
-        return carry
-
-    lax.fori_loop(0, shards, attn_core, 0)
+    rms = jnp.sqrt(energy / (width * jnp.maximum(count, 1.0)))
+
+    lax.fori_loop(jnp.where(edge, 2, 0), shards - 1, feed_line, 0)
+
+    @pl.when(edge)
+    def _():
+        attn_line(0, 0)
 
     x_dh1.wait()
 
@@ -641,32 +746,35 @@
         scaled = dh1 * first_gain[...]
         back = factor * scaled - row * (factor**3 * jnp.mean(row * scaled, axis=1, keepdims=True))
         back = back + dmixed[at] + dscore(at) * w_router[...]
-        rows_grad[at] = (own_c[at].astype(F32) + back).astype(BF16)
+        got[1, at] = (own_c[at].astype(F32) + back).astype(BF16)
         return sums[0] + fold_rows(dscore(at) * row), sums[1] + fold_rows(dh1 * row * factor)
 
     zero = jnp.zeros((8, width), F32)
     router_sum, first_sum = row_tiles(rows, first_back, (zero, zero))
+    put(1, got.at[1]).start()
     parts = [jnp.sum(part, axis=0, keepdims=True) for part in (router_sum, first_sum, second_sum)]
     small = jnp.concatenate(parts + [jnp.zeros((5, width), F32)], axis=0)
-    for k, device in enumerate([core_dev, x_dev, y_dev] + z_partners):
+
+    def small_copy(k):
+        return remote(small_send.at[k], small_got.at[k], sm_s.at[k], sm_r.at[k], small_devices[k])
+
+    for k in range(len(small_devices)):
         small_send[k] = small
-        copy = remote(small_send.at[k], small_got.at[k], sm_s.at[k], sm_r.at[k], device)
-        copy.start()
-        copy.wait()
+        small_copy(k).start()
+        small_copy(k).wait()
         small = small + small_got[k]
-    small_out[...] = small
-
-    def attn_line(k, carry):
-        s = reversed_order(k)
-        stage_y(1, w_up, y_a, s)
-        stage_z(1, w_up, z_a, s, "start")
-        return carry
-
-    lax.fori_loop(0, shards - 1, attn_line, 0)
+    row_at = lax.broadcasted_iota(jnp.int32, (8, 1), 0)
+    small_send[0] = jnp.where(row_at == 3, rms, small)
+    put(2, small_send.at[0]).start()
+    lax.fori_loop(jnp.where(edge, 1, 0), shards - 1, attn_line, 0)
+    stage_y(0, grads, y_f, z)
+    stage_last(0, grads, z_f, swap_f, feed_out)
     stage_y(1, w_up, y_a, z)
     stage_last(1, w_up, z_a, swap_a, attn_out)
     stage_out(0, swap_f, feed_out)
+    put(4, feed_out).start()
     stage_out(1, swap_a, attn_out)
+    put(3, attn_out).start()
 
     drain(attn_mats)
     for copy in (x_h1, x_dfeed, x_h2, x_datt):
@@ -686,6 +794,8 @@
     lax.fori_loop(0, shards, drain_grads, 0)
     swap(0, swap_f).wait_send()
     swap(1, swap_a).wait_send()
+    for k, src in enumerate((sent.at[1], got.at[1], small_send.at[0], attn_out, feed_out)):
+        put(k, src).wait()
 
 
 def run_block(size, operands):
@@ -709,9 +819,8 @@
         vmem(shards, 2, heads * rows, rows),
         vmem(shards, 2 * rows, hidden),
         vmem(shards, 2 * rows, hidden),
-        *([vmem(2 * rows, 3 * narrow)] if size["joined"] else []),
         full(2, rows, width),
-        full(2, 2 * rows, hidden),
+        full(2, rows, hidden),
         vmem(2, rows, width),
         vmem(2, rows, width),
         vmem(rows, width),
@@ -727,10 +836,13 @@
         vmem(shards + 1, 2, cut, attn),
         vmem(2, cut, feed),
         vmem(2, cut, attn),
+        full(2, cut, attn),
+        full(2, cut, feed),
         full(stages, 8, width),
         full(stages, 8, width),
         dma((mats,)),
-        dma((2, 2)),
+        dma((2, 2, 2)),
+        dma((5,)),
         dma((mats, shards + 1)),
         dma((mats, shards)),
         dma((mats, shards)),
@@ -751,7 +863,6 @@
     outs = [
         jax.ShapeDtypeStruct((rows, width), BF16),
         jax.ShapeDtypeStruct((rows, width), BF16),
-        jax.ShapeDtypeStruct((8, 128), F32),
         jax.ShapeDtypeStruct((8, width), F32),
         jax.ShapeDtypeStruct((2, cut, attn), F32),
         jax.ShapeDtypeStruct((2, cut, feed), F32),
@@ -760,7 +871,7 @@
         functools.partial(block_kernel, size),
         out_shape=outs,
         in_specs=[far, far] + [near] * 5 + [far] * (len(operands) - 7),
-        out_specs=[near] * len(outs),
+        out_specs=[pl.BlockSpec(memory_space=pltpu.HBM)] * len(outs),
         scratch_shapes=scratch,
         compiler_params=pltpu.CompilerParams(
             collective_id=0, has_side_effects=True, vmem_limit_bytes=64 * 2**20 - 65536
@@ -768,21 +879,24 @@
     )(*operands)
 
 
-def place_kernel(size, assemble, routed, tok, cot, rows_res, rows_grad, attn, feed, *outs):
+def place_kernel(size, assemble, routed, tok, cot, rows_res, rows_grad, small, attn, feed, *outs):
     block, count = tok.shape[0], routed.shape[1]
     step = pl.program_id(0)
     line = step * block + lax.broadcasted_iota(jnp.int32, (block, count), 0)
     chosen = jnp.where(line == routed[...], 1.0, 0.0)
-    taken = jnp.sum(chosen, axis=1, keepdims=True) > 0.0
+    keep = (1.0 - jnp.sum(chosen, axis=1, keepdims=True)).astype(BF16)
     pick = chosen.astype(BF16)
-    outs[0][...] = jnp.where(taken, mm(pick, rows_res[...]), tok[...].astype(F32)).astype(BF16)
-    outs[1][...] = jnp.where(taken, mm(pick, rows_grad[...]), cot[...].astype(F32)).astype(BF16)
+    outs[0][...] = mm(pick, rows_res[...]).astype(BF16) + tok[...] * keep
+    outs[1][...] = mm(pick, rows_grad[...]).astype(BF16) + cot[...] * keep
     if assemble:
 
         @pl.when(step == 0)
         def _():
             for ref, value in zip(outs[2:], weight_outputs(size, attn, feed)):
                 ref[...] = value
+            for k in range(3):
+                outs[8 + k][...] = small[k : k + 1, :]
+            outs[11][...] = small[3:4, 0:1]
 
 
 def weight_outputs(size, attn, feed):
@@ -801,7 +915,7 @@
     )
 
 
-def place_rows(size, routed, tokens, cotangent, rows_res, rows_grad, attn, feed, assemble):
+def place_rows(size, routed, tokens, cotangent, rows_res, rows_grad, small, attn, feed, assemble):
     length, width, rows = size["L"], size["D"], size["R"]
     block = 256
     cut, narrow, hidden = size["DB"], size["n"], size["f"]
@@ -811,6 +925,7 @@
     out_specs = [moving] * 2
     if assemble:
         shapes = [(cut, 2 * narrow)] * 3 + [(2 * narrow, cut), (cut, 2 * hidden), (2 * hidden, cut)]
+        shapes += [(1, width)] * 3 + [(1, 1)]
         outs = outs + [jax.ShapeDtypeStruct(shape, F32) for shape in shapes]
         out_specs = out_specs + [whole(*shape) for shape in shapes]
     return pl.pallas_call(
@@ -823,12 +938,13 @@
             moving,
             whole(rows, width),
             whole(rows, width),
+            whole(*small.shape),
             whole(*attn.shape),
             whole(*feed.shape),
         ],
         out_specs=out_specs,
         compiler_params=pltpu.CompilerParams(vmem_limit_bytes=48 * 2**20),
-    )(routed, tokens, cotangent, rows_res, rows_grad, attn, feed)
+    )(routed, tokens, cotangent, rows_res, rows_grad, small, attn, feed)
 
 
 def shards_of(
@@ -869,8 +985,9 @@
         tokens, cotangent, routed, valid_mask, row(w_router), row(first_gain), row(second_gain),
         *qkv, output_weight, up_weight.reshape(2, 2, 2, cut, 2 * hidden), down_weight,
     )
-    rows_res, rows_grad, rms, small, attn, feed = run_block(size, operands)
+    rows_res, rows_grad, small, attn, feed = run_block(size, operands)
     whole_group = data == 8
+    rms = small[3, 0:1]
     if not whole_group:
         block = 4 * y + 2 * x + dp % 2
 
@@ -881,21 +998,25 @@
 
         attn, feed = over_groups(attn), over_groups(feed)
         small = lax.psum(small, "dp") / 8.0
-    placed = place_rows(size, routed, tokens[0], cotangent[0], rows_res, rows_grad, attn, feed, whole_group)
+    placed = place_rows(size, routed, tokens[0], cotangent[0], rows_res, rows_grad, small, attn, feed, whole_group)
     residual, grad_tokens = placed[:2]
-    weights = placed[2:] if whole_group else weight_outputs(size, attn, feed)
+    if whole_group:
+        vectors = [vector.reshape(width) for vector in placed[8:11]]
+        weights, rms = placed[2:8], placed[11].reshape(1)
+    else:
+        vectors, weights = [small[k] for k in range(3)], weight_outputs(size, attn, feed)
     grad_query, grad_key, grad_value, grad_output, grad_up, grad_down = weights
     return (
         residual[None],
         grad_tokens[None],
-        rms[0, 0:1],
-        small[0],
-        small[1],
+        rms,
+        vectors[0],
+        vectors[1],
         grad_query,
         grad_key,
         grad_value,
         grad_output,
-        small[2],
+        vectors[2],
         grad_up,
         grad_down,
     )

time: 260 us -> 181 us (0.70)
  Pallas kernels: 251 us -> 173 us
    pallas_call x1, Pallas kernels: 240 us -> 162 us  [run_block(): pl.pallas_call(functools.partial(block_kernel, size), out_shape=outs, in_...]
    slice x2 -> x0, local copies, waits for them, and re-layouts: 2.67 us -> none  [the longest x1 1.47 us: shards_of(): small[2]]
    unnamed x10 -> x12, local copies, waits for them, and re-layouts: 5.03 us -> 5.78 us
where the time goes in v2:
time: 181 us; the launch traced here: 179 us
  Pallas kernels  173 us (96%)
  local copies, waits for them, and re-layouts  5.78 us (3%)
    pallas_call x1, Pallas kernels, run_block(): pl.pallas_call(functools.partial(block_kernel, size), out_shape=outs, in_...  162 us
    pallas_call x1, Pallas kernels, place_rows(): pl.pallas_call(functools.partial(place_kernel, size, assemble), grid=(len...  11.2 us
    unnamed x12, local copies, waits for them, and re-layouts  5.78 us

profile of v2, /device:TPU:0, one launch (start us, length us, event | category | flops | bytes accessed | tf_op | source)
XLA Modules:
  0.0 179.4 jit_solution(11171522966457657797)
XLA Ops:
  0.6 161.6 %shard_map.220 = (bf16[256,1024]{1,0:T(8,128)(2,1)}, bf16[256,1024]{1,0:T(8,128)(2,1)}, f32[8,1024]{1,0:T(8,128)}, f32[2,128,512]{2,1,0:T(8,128)}, f32[2,128,1024]{2,1,0:T(8,128)}) custom-call(bf16[1,2048,1024]{2,1,0:T(8,128)(2,1)} %refs_0_.1, bf16[1,2048,1024]{2,1,0:T(8,128)(2,1)} %refs_1_.1, s32[1,256]{1,0:T(1,128)} %routed.1, s32[1,2048]{1,0:T(1,128)} %refs_3_.1, ...), custom_call_target="tpu_custom_call" | custom-call | tf_op jit(solution)/shard_map/pallas_call | solution.py:870
  162.3 0.0 copy-start
  162.3 1.2 copy-done
  163.5 0.0 copy-start.1
  163.5 1.0 copy-done.1
  164.5 0.0 copy-start.2
  164.5 1.0 copy-done.2
  165.6 0.0 copy-start.3
  165.6 1.0 copy-done.3
  166.6 0.0 copy-start.4
  166.6 0.8 copy-done.4
  167.4 0.0 copy-start.5
  167.4 0.7 copy-done.5
  168.0 11.2 %shard_map.221 = (bf16[2048,1024]{1,0:T(8,128)(2,1)}, bf16[2048,1024]{1,0:T(8,128)(2,1)}, f32[128,256]{1,0:T(8,128)}, f32[128,256]{1,0:T(8,128)}, f32[128,256]{1...) custom-call(s32[1,256]{1,0:T(1,128)S(1)} %copy-done.5, ...), custom_call_target="tpu_custom_call" | custom-call | tf_op jit(solution)/shard_map/pallas_call | solution.py:931
Async XLA Ops:
  162.3 1.2 copy-start
  163.5 1.0 copy-start.1
  164.5 1.0 copy-start.2
  165.6 1.0 copy-start.3
  166.6 0.8 copy-start.4
  167.4 0.7 copy-start.5

commit v3 on v2

--- a/solution.py
+++ b/solution.py
@@ -93,10 +93,7 @@
     y_dev = (dp + ybit * (1 - 2 * y), z)
     up_dev = (dp, z + 1)
     down_dev = (dp, z - 1)
-    x_dp = dp + 2 * (1 - 2 * x)
-    z_bits = [1 << k for k in range(int(math.log2(shards)))]
-    small_devices = [core_dev, x_dev, (x_dp + ybit * (1 - 2 * y), z)]
-    small_devices += [(x_dp, z + bit * (1 - 2 * lax.rem(lax.div(z, bit), 2))) for bit in z_bits]
+    small_devices = [core_dev, x_dev, (dp + 2 * (1 - 2 * x) + ybit * (1 - 2 * y), z)]
 
     def remote(src, dst, send, recv, device):
         return pltpu.make_async_remote_copy(
@@ -160,23 +157,46 @@
             src, dst = down_in.at[lanes(hidden), :], w_down.at[z]
         return pltpu.make_async_copy(src, dst, load_sem.at[i])
 
+    def group_of(i):
+        return 0 if i <= out_at else 1
+
     def own_up(i):
-        return remote(own_piece(i), held(i, z, y, core), wz_s.at[i, z], wz_r.at[i, z], up_dev)
+        return remote(own_piece(i), held(i, z, y, core), wz_s.at[group_of(i), z], wz_r.at[i, z], up_dev)
 
     def own_down(i):
-        return remote(own_piece(i), held(i, z, y, core), wz_s.at[i, shards], wz_r.at[i, z], down_dev)
+        return remote(own_piece(i), held(i, z, y, core), wz_s.at[group_of(i), shards], wz_r.at[i, z], down_dev)
 
     def pass_on(i, s, device):
         piece = held(i, s, y, core)
-        return remote(piece, piece, wz_s.at[i, s], wz_r.at[i, s], device)
+        return remote(piece, piece, wz_s.at[group_of(i), s], wz_r.at[i, s], device)
 
     def across_y(i, s, qy):
         piece = held(i, s, qy, core)
-        return remote(piece, piece, wy_s.at[i, s], wy_r.at[i, s], y_dev)
-
-    def across_core(i, s, qy, qc, slot):
+        return remote(piece, piece, wy_s.at[group_of(i)], wy_r.at[i, s], y_dev)
+
+    def across_core(i, s, qy, qc):
         piece = held(i, s, qy, qc)
-        return remote(piece, piece, wc_s.at[i, slot, s], wc_r.at[i, slot, s], core_dev)
+        group = group_of(i)
+        return remote(piece, piece, wc_s.at[group], wc_r.at[group, s], core_dev)
+
+    def await_pieces(group, sem, count, receiving=False):
+        mats = attn_mats if group == 0 else feed_mats
+        if joined:
+            refs = [held(i, 0, 0, 0) for i in mats] * count
+        else:
+            flat = w_up.at[0, 0, 0] if group == 0 else w_up.at[0, 0]
+            if count == 2:
+                flat = w_up.at[0, 0] if group == 0 else w_up.at[0]
+            elif count == shards - 1:
+                flat = w_up.at[0 : shards - 1, 0, 0] if group == 0 else w_up.at[0 : shards - 1, 0]
+            elif count == 2 * (shards - 1):
+                flat = w_up.at[0 : shards - 1, 0] if group == 0 else w_up.at[0 : shards - 1]
+            refs = [flat]
+        for ref in refs:
+            if receiving:
+                remote(ref, ref, wc_s.at[group], sem, core_dev).wait_recv()
+            else:
+                remote(ref, ref, sem, wc_r.at[group, 0], core_dev).wait_send()
 
     def send_own_up(mats):
         for i in mats:
@@ -195,16 +215,21 @@
         def _():
             action(down_dev)
 
+    edge = (z == 0) | (z == shards - 1)
+    inner = jnp.logical_not(edge)
+
+    def arrive_one(i, j):
+        s = order(j)
+        pass_on(i, s, up_dev).wait_recv()
+        passing(s, lambda device: pass_on(i, s, device).start())
+        across_y(i, s, y).start()
+        across_core(i, s, y, core).start()
+
     def arrive(mats, j):
-        s = order(j)
         for i in mats:
-            pass_on(i, s, up_dev).wait_recv()
-            passing(s, lambda device: pass_on(i, s, device).start())
-            across_y(i, s, y).start()
-            across_core(i, s, y, core, 0).start()
-
-    def arrive_attn(j):
-        arrive(attn_mats, j)
+            arrive_one(i, j)
+
+    def follow(j):
         s = order(j)
 
         @pl.when((s == 0) & (z < shards - 1))
@@ -219,35 +244,28 @@
         s = order(j)
         for i in mats:
             across_y(i, s, 1 - y).wait_recv()
-            across_core(i, s, 1 - y, core, 1).start()
-
-    def settle(mats, j):
-        s = order(j)
-        for i in mats:
-            across_core(i, s, y, 1 - core, 0).wait_recv()
-            across_core(i, s, 1 - y, 1 - core, 1).wait_recv()
-
-    def drain(mats):
+            across_core(i, s, 1 - y, core).start()
+
+    def settle(group, j):
+        await_pieces(group, wc_r.at[group, order(j)], 2, True)
+
+    def drain(group):
         @pl.when(z < shards - 1)
         def _():
-            for i in mats:
-                own_up(i).wait_send()
+            await_pieces(group, wz_s.at[group, z], 1)
 
         @pl.when(z > 0)
         def _():
-            for i in mats:
-                own_down(i).wait_send()
+            await_pieces(group, wz_s.at[group, shards], 1)
 
         def step(j, carry):
             s = order(j)
-            for i in mats:
-                passing(s, lambda device: pass_on(i, s, device).wait_send())
-                across_y(i, s, y).wait_send()
-                across_core(i, s, y, core, 0).wait_send()
-                across_core(i, s, 1 - y, core, 1).wait_send()
+            passing(s, lambda device: await_pieces(group, wz_s.at[group, s], 1))
             return carry
 
         lax.fori_loop(1, shards, step, 0)
+        await_pieces(group, wy_s.at[group], shards - 1)
+        await_pieces(group, wc_s.at[group], 2 * (shards - 1))
 
     def exchange(slot, src, dst):
         return remote(src, dst, x_s.at[slot], x_r.at[slot], x_dev)
@@ -270,10 +288,24 @@
     def block_loads(t):
         copies = []
         for k, (array, buf) in enumerate(zip((tokens, cotangent), stages[t % 2])):
-            for half in range(2):
-                src = array.at[0, (2 * t + half) * rows : (2 * t + half + 1) * rows]
-                copies.append(pltpu.make_async_copy(src, buf.at[half], tok_sem.at[t % 2, k, half]))
+            copies.append(pltpu.make_async_copy(array.at[2 * t : 2 * t + 2], buf, tok_sem.at[t % 2, k]))
         return copies
+
+    barrier = pltpu.get_barrier_semaphore()
+
+    def greet(device):
+        pl.semaphore_signal(barrier, inc=1, device_id=device, device_id_type=pl.DeviceIdType.MESH)
+
+    for device in (core_dev, x_dev, y_dev):
+        greet(device)
+
+    @pl.when(z > 0)
+    def _():
+        greet(down_dev)
+
+    @pl.when(z < shards - 1)
+    def _():
+        greet(up_dev)
 
     for t in range(2):
         for copy in block_loads(t):
@@ -281,40 +313,25 @@
     for i in attn_mats + feed_mats:
         load_own(i).start()
 
-    barrier = pltpu.get_barrier_semaphore()
-
-    def greet(device):
-        pl.semaphore_signal(barrier, inc=1, device_id=device, device_id_type=pl.DeviceIdType.MESH)
-
-    for device in [y_dev] + small_devices:
-        greet(device)
-
-    @pl.when(z > 0)
-    def _():
-        greet(down_dev)
-
-    @pl.when(z < shards - 1)
-    def _():
-        greet(up_dev)
-
-    ends = jnp.where(z == 0, 1, 0) + jnp.where(z == shards - 1, 1, 0)
-    pl.semaphore_wait(barrier, 3 + len(small_devices) - ends)
-
-    @pl.when(z < shards - 1)
-    def _():
-        send_own_up(attn_mats)
-
-    @pl.when(z > 0)
-    def _():
-        send_own_down(attn_mats)
-
-    @pl.when(z == 0)
-    def _():
-        send_own_up(feed_mats)
-
-    @pl.when(z == shards - 1)
-    def _():
-        send_own_down(feed_mats)
+    def begin():
+        ends = jnp.where(z == 0, 1, 0) + jnp.where(z == shards - 1, 1, 0)
+        pl.semaphore_wait(barrier, 5 - ends)
+
+        @pl.when(z < shards - 1)
+        def _():
+            send_own_up(attn_mats)
+
+        @pl.when(z > 0)
+        def _():
+            send_own_down(attn_mats)
+
+        @pl.when(z == 0)
+        def _():
+            send_own_up(feed_mats)
+
+        @pl.when(z == shards - 1)
+        def _():
+            send_own_down(feed_mats)
 
     as_rows = jnp.broadcast_to(routed[...].astype(F32), (8, rows))
     position = jnp.transpose(as_rows)[:, 0:1].astype(jnp.int32)
@@ -333,6 +350,8 @@
                 copy.start()
         mask = valid[:, 2 * t * rows : 2 * (t + 1) * rows].astype(F32)
         flags = flags + jnp.sum(chosen * mask, axis=1, keepdims=True)
+        if t == steps // 2 - 1:
+            begin()
     columns[...] = jnp.broadcast_to(flags, columns.shape)
 
     def prepare(at, carry):
@@ -372,10 +391,28 @@
 
     for i in attn_mats:
         load_own(i).wait()
-    arrive_attn(1)
-    for j in range(2, shards):
-        arrive_attn(j)
-        relay(attn_mats, j - 1)
+
+    @pl.when(edge)
+    def _():
+        for j in range(1, shards):
+            arrive(attn_mats, j)
+            follow(j)
+            if j > 1:
+                relay(attn_mats, j - 1)
+
+    @pl.when(inner)
+    def _():
+        for i in attn_mats:
+            for j in (1, 2):
+                arrive_one(i, j)
+        for j in (1, 2):
+            follow(j)
+        for j in range(3, shards):
+            arrive(attn_mats, j)
+            follow(j)
+        for j in range(1, shards - 1):
+            relay(attn_mats, j)
+
     x_h1.wait_recv()
 
     def attend(j, carry):
@@ -383,12 +420,12 @@
 
         @pl.when(j + 1 == shards)
         def _():
+            relay(attn_mats, j)
             arrive(feed_mats[:1], 1)
-            relay(attn_mats, j)
 
         @pl.when(j > 0)
         def _():
-            settle(attn_mats, j)
+            settle(0, j)
 
         low = mm(h1[...].reshape(2 * rows, width), w_qkv[s]).astype(BF16)
         query = low[:, 0:narrow] * jnp.asarray(HEAD_DIM**-0.5, BF16)
@@ -415,6 +452,11 @@
     attended[...] = project_out(0)
     arrive(feed_mats[1:], 1)
     arrive(feed_mats[:1], 2)
+
+    @pl.when(inner)
+    def _():
+        arrive(feed_mats[1:], 2)
+
     x_att.wait()
 
     def mix(at, carry):
@@ -427,19 +469,23 @@
 
     row_tiles(rows, mix)
     x_h2.start()
-    arrive(feed_mats[1:], 2)
+
+    @pl.when(edge)
+    def _():
+        arrive(feed_mats[1:], 2)
+
     x_dfeed.wait_recv()
 
     def core_send(group, buf, into, s, at=None):
         src = buf.at[s, :, :, 1 - core]
-        return remote(src, into.at[s], gc_s.at[group, s], gc_r.at[group, s], core_dev)
+        return remote(src, into.at[s], gc_s.at[group], gc_r.at[group, s], core_dev)
 
     def y_send(group, buf, into, s):
-        return remote(buf.at[s, 1 - y, :, core], into.at[s], gy_s.at[group, s], gy_r.at[group, s], y_dev)
+        return remote(buf.at[s, 1 - y, :, core], into.at[s], gy_s.at[group], gy_r.at[group, s], y_dev)
 
     def z_send(group, buf, into, s, device, slot):
         src = buf.at[s, y, :, core]
-        return remote(src, into.at[slot], gz_s.at[group, s], gz_r.at[group, slot], device)
+        return remote(src, into.at[slot], gz_s.at[group], gz_r.at[group, slot], device)
 
     def add_into(ref, *others):
         value = ref[...].astype(F32)
@@ -464,29 +510,23 @@
         for b in range(2):
             add_into(buf.at[s, y, b, core], z_got.at[slot, b])
 
-    def stage_z(group, buf, z_got, s, action):
+    def stage_z(group, buf, z_got, s):
         @pl.when(s > z)
         def _():
-            if action == "start":
-
-                @pl.when(z > 0)
-                def _():
-                    line_in(group, buf, z_got, s, s)
-
-            copy = z_send(group, buf, z_got, s, up_dev, s)
-            copy.start() if action == "start" else copy.wait_send()
+            @pl.when(z > 0)
+            def _():
+                line_in(group, buf, z_got, s, s)
+
+            z_send(group, buf, z_got, s, up_dev, s).start()
 
         @pl.when(s < z)
         def _():
-            if action == "start":
-
-                @pl.when(z < shards - 1)
-                def _():
-                    line_in(group, buf, z_got, s, s)
+            @pl.when(z < shards - 1)
+            def _():
+                line_in(group, buf, z_got, s, s)
 
             slot = jnp.where(s == z - 1, shards, s)
-            copy = z_send(group, buf, z_got, s, down_dev, slot)
-            copy.start() if action == "start" else copy.wait_send()
+            z_send(group, buf, z_got, s, down_dev, slot).start()
 
     def swap(group, pair):
         return remote(pair.at[0], pair.at[1], gx_s.at[group], gx_r.at[group], x_dev)
@@ -520,13 +560,28 @@
             value = mm(left[2 * a * quarter : 2 * (a + 1) * quarter, :], right).astype(BF16)
             buf[s, a, :, :, :, lo : lo + count] = value.reshape(2, 2, cut, count)
 
+    def line_step(group, buf, y_got, z_got, j):
+        s = order(j)
+        stage_y(group, buf, y_got, s)
+        stage_z(group, buf, z_got, s)
+
+    def feed_line(j):
+        line_step(0, grads, y_f, z_f, j)
+
+    def attn_line(j):
+        line_step(1, w_up, y_a, z_a, j)
+
     total[...] = jnp.zeros_like(total)
     for i in feed_mats:
         load_own(i).wait()
+
     def feed_grads(s):
         store_grads(grads, s, turn_a, dup[s], 0, hidden)
         store_grads(grads, s, turn_b, act[s], hidden, hidden)
         core_send(0, grads, core_f, s).start()
+
+    def feed_core(s):
+        stage_core(0, grads, core_f, y_f, s)
 
     def feed_chunk(s, half):
         part = pl.ds(pl.multiple_of(half * rows, rows), rows)
@@ -534,12 +589,12 @@
         wide[0] = mm(h2[half], up_here)
         wide[1] = mm_nt(dfeed[half], w_down[s])
 
-        def turn(at, inner):
+        def turn(at, inside):
             active, slope = gelu_both(wide[0, at])
             out = pl.ds(pl.multiple_of(half * rows + at.start, TILE), TILE)
             act[s, out] = active.astype(BF16)
             dup[s, out] = (wide[1, at] * slope).astype(BF16)
-            return inner
+            return inside
 
         row_tiles(rows, turn)
         total[half] += mm_nt(dup[s, part], up_here)
@@ -547,7 +602,7 @@
     def own_step(j, carry):
         @pl.when(j > 0)
         def _():
-            settle(feed_mats, j)
+            settle(1, j)
 
         feed_chunk(order(j), 0)
 
@@ -555,9 +610,7 @@
         def _():
             arrive(feed_mats[1:], j + 2)
 
-        @pl.when(j + 2 < shards)
-        def _():
-            relay(feed_mats, j + 1)
+        relay(feed_mats, j + 1)
 
         @pl.when(j + 3 < shards)
         def _():
@@ -565,27 +618,46 @@
 
         return carry
 
-    lax.fori_loop(0, shards - 1, own_step, 0)
+    lax.fori_loop(0, shards - 2, own_step, 0)
     x_h2.wait_recv()
     turn_a[...] = jnp.transpose(h2[...].reshape(2 * rows, width))
     turn_b[...] = jnp.transpose(dfeed[...].reshape(2 * rows, width))
 
-    def other_step(j, carry):
-        feed_chunk(order(j), 1)
-
-        @pl.when(j == 0)
-        def _():
-            feed_grads(z)
-
-        @pl.when(j == 1)
-        def _():
-            stage_core(0, grads, core_f, y_f, z)
+    quick = shards == 4
+
+    def leaving(k):
+        if not quick:
+            return shards - 1 - k
+        ends, middle = jnp.where(edge, 2, 1), jnp.where(edge, 1, 2)
+        return jnp.where(k == 0, ends, jnp.where(k == 1, 3, jnp.where(k == 2, middle, 0)))
+
+    def other_step(k, carry):
+        late = jnp.where(quick & edge, 0, shards - 2)
+        mine = k == late
+
+        @pl.when(mine)
+        def _():
+            settle(1, shards - 2)
+
+        plain = jnp.where(k < late, k, shards - 2)
+        if quick:
+            plain = jnp.where(edge, jnp.where(k < 2, 2, k - 2), jnp.where(k < 2, 1 - k, 2))
+        feed_chunk(order(plain), jnp.where(mine, 0, 1))
+        if quick:
+
+            @pl.when(k == jnp.where(edge, 1, 0))
+            def _():
+                feed_grads(order(leaving(0)))
+
+            @pl.when(k == jnp.where(edge, 2, 1))
+            def _():
+                feed_core(order(leaving(0)))
 
         return carry
 
-    lax.fori_loop(0, shards - 1, other_step, 0)
+    lax.fori_loop(0, shards, other_step, 0)
     relay(feed_mats, shards - 1)
-    settle(feed_mats, shards - 1)
+    settle(1, shards - 1)
 
     def last_step(k, carry):
         feed_chunk(order(shards - 1), 1 - k)
@@ -598,18 +670,25 @@
         return carry
 
     lax.fori_loop(0, 2, last_step, 0)
+    first_left = 1 if quick else 0
 
     def feed_grads_step(k, carry):
-        feed_grads(reversed_order(k))
-
-        @pl.when(k > 0)
-        def _():
-            stage_core(0, grads, core_f, y_f, reversed_order(k - 1))
+        if quick:
+
+            @pl.when((k == shards - 1) & edge)
+            def _():
+                feed_line(leaving(0))
+
+        feed_grads(order(leaving(k)))
+
+        @pl.when(k > first_left)
+        def _():
+            feed_core(order(leaving(k - 1)))
 
         return carry
 
-    lax.fori_loop(0, shards - 1, feed_grads_step, 0)
-    stage_core(0, grads, core_f, y_f, order(1))
+    lax.fori_loop(first_left, shards, feed_grads_step, 0)
+    feed_core(z)
 
     def feed_rows(half):
         value = mm(act[0, half * rows : (half + 1) * rows], w_down[0])
@@ -666,19 +745,16 @@
         return value
 
     attend_back(0)
+    if quick:
+        feed_line(jnp.where(edge, leaving(1), leaving(0)))
     total[0] = dh1_rows(0)
     turn_a[...] = jnp.transpose(h1[...].reshape(2 * rows, width))
-    drain(feed_mats)
-    edge = (z == 0) | (z == shards - 1)
-
-    @pl.when(edge)
-    def _():
-        far = reversed_order(0)
-        stage_y(0, grads, y_f, far)
-        stage_z(0, grads, z_f, far, "start")
-
+    drain(1)
     x_datt.wait_recv()
     turn_b[...] = jnp.transpose(datt[...].reshape(2 * rows, width))
+
+    if quick:
+        feed_line(jnp.where(edge, leaving(2), leaving(1)))
     attend_back(1)
     sent[0] = dh1_rows(1).astype(BF16)
     x_dh1.start()
@@ -695,26 +771,9 @@
 
         return carry
 
-    @pl.when(edge)
-    def _():
-        near = reversed_order(1)
-        stage_y(0, grads, y_f, near)
-        stage_z(0, grads, z_f, near, "start")
-
     lax.fori_loop(0, shards, attn_grads, 0)
     stage_core(1, w_up, core_a, y_a, z)
 
-    def line_step(group, buf, y_got, z_got):
-        def step(k, carry):
-            s = reversed_order(k)
-            stage_y(group, buf, y_got, s)
-            stage_z(group, buf, z_got, s, "start")
-            return carry
-
-        return step
-
-    feed_line = line_step(0, grads, y_f, z_f)
-    attn_line = line_step(1, w_up, y_a, z_a)
     x_feed.wait()
 
     def finish_forward(at, squares):
@@ -731,11 +790,15 @@
     energy = jnp.sum(jnp.sum(squares, axis=0, keepdims=True), axis=1, keepdims=True)
     rms = jnp.sqrt(energy / (width * jnp.maximum(count, 1.0)))
 
-    lax.fori_loop(jnp.where(edge, 2, 0), shards - 1, feed_line, 0)
+    def feed_rest(k, carry):
+        feed_line(leaving(k))
+        return carry
+
+    lax.fori_loop(jnp.where(edge, 3, 2) if quick else 0, shards - 1, feed_rest, 0)
 
     @pl.when(edge)
     def _():
-        attn_line(0, 0)
+        attn_line(shards - 1)
 
     x_dh1.wait()
 
@@ -758,17 +821,49 @@
     def small_copy(k):
         return remote(small_send.at[k], small_got.at[k], sm_s.at[k], sm_r.at[k], small_devices[k])
 
-    for k in range(len(small_devices)):
+    hops = len(small_devices)
+    for k in range(hops):
         small_send[k] = small
         small_copy(k).start()
         small_copy(k).wait()
         small = small + small_got[k]
+        if k == 0:
+
+            @pl.when(edge)
+            def _():
+                attn_line(shards - 2)
+
+            @pl.when(inner)
+            def _():
+                attn_line(shards - 1)
+
+    def small_spread(far, source):
+        slot = hops + source
+        return remote(
+            small_send.at[hops], small_got.at[slot], sm_s.at[hops + far - 1], sm_r.at[slot], (dp, lax.rem(z + far, shards))
+        )
+
+    small_send[hops] = small
+    small_got[hops + z] = small
+    for far in range(1, shards):
+        small_spread(far, z).start()
+
+    def attn_rest(k, carry):
+        attn_line(shards - 2 - k)
+        return carry
+
+    lax.fori_loop(jnp.where(edge, 1, 0), shards - 2, attn_rest, 0)
+    stage_y(0, grads, y_f, z)
+    stage_last(0, grads, z_f, swap_f, feed_out)
+    for far in range(1, shards):
+        small_spread(far, lax.rem(z + shards - far, shards)).wait_recv()
+        small_spread(far, z).wait_send()
+    small = small_got[hops]
+    for k in range(1, shards):
+        small = small + small_got[hops + k]
     row_at = lax.broadcasted_iota(jnp.int32, (8, 1), 0)
     small_send[0] = jnp.where(row_at == 3, rms, small)
     put(2, small_send.at[0]).start()
-    lax.fori_loop(jnp.where(edge, 1, 0), shards - 1, attn_line, 0)
-    stage_y(0, grads, y_f, z)
-    stage_last(0, grads, z_f, swap_f, feed_out)
     stage_y(1, w_up, y_a, z)
     stage_last(1, w_up, z_a, swap_a, attn_out)
     stage_out(0, swap_f, feed_out)
@@ -776,22 +871,16 @@
     stage_out(1, swap_a, attn_out)
     put(3, attn_out).start()
 
-    drain(attn_mats)
+    drain(0)
     for copy in (x_h1, x_dfeed, x_h2, x_datt):
         copy.wait_send()
 
-    def drain_grads(k, carry):
-        s = reversed_order(k)
-        for group, buf, core_got, y_got, z_got in (
-            (0, grads, core_f, y_f, z_f),
-            (1, w_up, core_a, y_a, z_a),
-        ):
-            core_send(group, buf, core_got, s).wait_send()
-            y_send(group, buf, y_got, s).wait_send()
-            stage_z(group, buf, z_got, s, "wait")
-        return carry
-
-    lax.fori_loop(0, shards, drain_grads, 0)
+    for group, core_got, y_got, z_got in ((0, core_f, y_f, z_f), (1, core_a, y_a, z_a)):
+        remote(core_got, core_got, gc_s.at[group], gc_r.at[group, 0], core_dev).wait_send()
+        remote(y_got, y_got, gy_s.at[group], gy_r.at[group, 0], y_dev).wait_send()
+        moved = z_got.at[0 : shards - 1]
+        remote(moved, moved, gz_s.at[group], gz_r.at[group, 0], up_dev).wait_send()
+
     swap(0, swap_f).wait_send()
     swap(1, swap_a).wait_send()
     for k, src in enumerate((sent.at[1], got.at[1], small_send.at[0], attn_out, feed_out)):
@@ -802,7 +891,7 @@
     shards, rows, width = size["S"], size["R"], size["D"]
     heads, narrow, hidden, cut = size["hh"], size["n"], size["f"], size["DB"]
     mats = (2 if size["joined"] else 4) + 2
-    stages = 3 + int(math.log2(shards))
+    stages = 3 + shards
     attn, feed = 4 * narrow, 2 * hidden
     dma = pltpu.SemaphoreType.DMA
     vmem = lambda *shape: pltpu.VMEM(shape, BF16)
@@ -841,17 +930,21 @@
         full(stages, 8, width),
         full(stages, 8, width),
         dma((mats,)),
-        dma((2, 2, 2)),
+        dma((2, 2)),
         dma((5,)),
-        dma((mats, shards + 1)),
+        dma((2, shards + 1)),
         dma((mats, shards)),
+        dma((2,)),
         dma((mats, shards)),
-        dma((mats, shards)),
-        dma((mats, 2, shards)),
-        dma((mats, 2, shards)),
+        dma((2,)),
+        dma((2, shards)),
         dma((8,)),
         dma((8,)),
-        *[dma((2, shards)) for _ in range(5)],
+        dma((2,)),
+        dma((2, shards)),
+        dma((2,)),
+        dma((2, shards)),
+        dma((2,)),
         dma((2, shards + 1)),
         dma((2,)),
         dma((2,)),
@@ -879,24 +972,57 @@
     )(*operands)
 
 
-def place_kernel(size, assemble, routed, tok, cot, rows_res, rows_grad, small, attn, feed, *outs):
-    block, count = tok.shape[0], routed.shape[1]
-    step = pl.program_id(0)
-    line = step * block + lax.broadcasted_iota(jnp.int32, (block, count), 0)
+def place_kernel(size, assemble, routed, small, tokens, cotangent, *refs):
+    length, width, rows = size["L"], size["D"], size["R"]
+    gathered, refs = refs[: 4 if assemble else 2], refs[4 if assemble else 2 :]
+    outs, refs = refs[: 12 if assemble else 2], refs[12 if assemble else 2 :]
+    bases, staged, refs = refs[:2], refs[2 : 2 + len(gathered)], refs[2 + len(gathered) :]
+    finals, (pick, keep, in_sem, out_sem, part_sem, final_sem) = refs[:-6], refs[-6:]
+    block = 512
+    steps = width // block
+
+    def moving(src, dst, sem, k, b):
+        at = (slice(None), pl.ds(b * block, block))
+        return pltpu.make_async_copy(src[k].at[at], dst[k].at[at], sem.at[k, b])
+
+    sources = (tokens, cotangent)
+    parts = [pltpu.make_async_copy(src, dst, part_sem.at[k]) for k, (src, dst) in enumerate(zip(gathered, staged))]
+    for copy in parts[:2]:
+        copy.start()
+    for b in range(steps):
+        for k in range(2):
+            moving(sources, bases, in_sem, k, b).start()
+    for copy in parts[2:]:
+        copy.start()
+    line = lax.broadcasted_iota(jnp.int32, (length, rows), 0)
     chosen = jnp.where(line == routed[...], 1.0, 0.0)
-    keep = (1.0 - jnp.sum(chosen, axis=1, keepdims=True)).astype(BF16)
-    pick = chosen.astype(BF16)
-    outs[0][...] = mm(pick, rows_res[...]).astype(BF16) + tok[...] * keep
-    outs[1][...] = mm(pick, rows_grad[...]).astype(BF16) + cot[...] * keep
+    pick[...] = chosen.astype(BF16)
+    keep[...] = jnp.broadcast_to((1.0 - jnp.sum(chosen, axis=1, keepdims=True)).astype(BF16), keep.shape)
+    for copy in parts[:2]:
+        copy.wait()
+    for b in range(steps):
+        for k in range(2):
+            at = slice(b * block, (b + 1) * block)
+            moving(sources, bases, in_sem, k, b).wait()
+            kept = jnp.concatenate([keep[...]] * (block // 128), axis=1)
+            bases[k][:, at] = mm(pick[...], staged[k][:, at]).astype(BF16) + bases[k][:, at] * kept
+            moving(bases, outs, out_sem, k, b).start()
+    last = []
     if assemble:
-
-        @pl.when(step == 0)
-        def _():
-            for ref, value in zip(outs[2:], weight_outputs(size, attn, feed)):
-                ref[...] = value
-            for k in range(3):
-                outs[8 + k][...] = small[k : k + 1, :]
-            outs[11][...] = small[3:4, 0:1]
+        for copy in parts[2:]:
+            copy.wait()
+        for k, value in enumerate(weight_outputs(size, *staged[2:])):
+            finals[k][...] = value
+            last.append(pltpu.make_async_copy(finals[k], outs[2 + k], final_sem.at[k]))
+            last[-1].start()
+        for k in range(3):
+            outs[8 + k][...] = small[k : k + 1, :]
+        outs[11][...] = small[3:4, 0:1]
+    for b in range(steps):
+        for k in range(2):
+            moving(bases, outs, out_sem, k, b).wait()
+    for copy in last:
+        copy.wait()
 
 
 def weight_outputs(size, attn, feed):
@@ -917,34 +1043,37 @@
 
 def place_rows(size, routed, tokens, cotangent, rows_res, rows_grad, small, attn, feed, assemble):
     length, width, rows = size["L"], size["D"], size["R"]
-    block = 256
     cut, narrow, hidden = size["DB"], size["n"], size["f"]
     whole = lambda *shape: pl.BlockSpec(shape, lambda i: (0,) * len(shape))
-    moving = pl.BlockSpec((block, width), lambda i: (i, 0))
-    outs = [jax.ShapeDtypeStruct((length, width), BF16)] * 2
-    out_specs = [moving] * 2
+    far = pl.BlockSpec(memory_space=pltpu.HBM)
+    outs, out_specs = [jax.ShapeDtypeStruct((length, width), BF16)] * 2, [far] * 2
+    gathered, finals = [rows_res, rows_grad], []
     if assemble:
-        shapes = [(cut, 2 * narrow)] * 3 + [(2 * narrow, cut), (cut, 2 * hidden), (2 * hidden, cut)]
-        shapes += [(1, width)] * 3 + [(1, 1)]
-        outs = outs + [jax.ShapeDtypeStruct(shape, F32) for shape in shapes]
-        out_specs = out_specs + [whole(*shape) for shape in shapes]
+        gathered += [attn, feed]
+        finals = [(cut, 2 * narrow)] * 3 + [(2 * narrow, cut), (cut, 2 * hidden), (2 * hidden, cut)]
+        tiny = [(1, width)] * 3 + [(1, 1)]
+        outs = outs + [jax.ShapeDtypeStruct(shape, F32) for shape in finals + tiny]
+        out_specs = out_specs + [far] * len(finals) + [whole(*shape) for shape in tiny]
+    dma = pltpu.SemaphoreType.DMA
     return pl.pallas_call(
         functools.partial(place_kernel, size, assemble),
-        grid=(length // block,),
+        grid=(1,),
         out_shape=outs,
-        in_specs=[
-            whole(1, rows),
-            moving,
-            moving,
-            whole(rows, width),
-            whole(rows, width),
-            whole(*small.shape),
-            whole(*attn.shape),
-            whole(*feed.shape),
+        in_specs=[whole(1, rows), whole(*small.shape)] + [far] * (2 + len(gathered)),
+        out_specs=out_specs,
+        scratch_shapes=[
+            *[pltpu.VMEM((length, width), BF16) for _ in range(2)],
+            *[pltpu.VMEM(part.shape, part.dtype) for part in gathered],
+            *[pltpu.VMEM(shape, F32) for shape in finals],
+            pltpu.VMEM((length, rows), BF16),
+            pltpu.VMEM((length, 128), BF16),
+            dma((2, width // 512)),
+            dma((2, width // 512)),
+            dma((4,)),
+            dma((6,)),
         ],
-        out_specs=out_specs,
-        compiler_params=pltpu.CompilerParams(vmem_limit_bytes=48 * 2**20),
-    )(routed, tokens, cotangent, rows_res, rows_grad, small, attn, feed)
+        compiler_params=pltpu.CompilerParams(vmem_limit_bytes=60 * 2**20),
+    )(routed, small, tokens, cotangent, *gathered)
 
 
 def shards_of(
@@ -982,7 +1111,7 @@
         qkv = (jnp.concatenate(halves, axis=1),)
     row = lambda vector: vector.reshape(1, width)
     operands = (
-        tokens, cotangent, routed, valid_mask, row(w_router), row(first_gain), row(second_gain),
+        tokens.reshape(-1, rows, width), cotangent.reshape(-1, rows, width), routed, valid_mask, row(w_router), row(first_gain), row(second_gain),
         *qkv, output_weight, up_weight.reshape(2, 2, 2, cut, 2 * hidden), down_weight,
     )
     rows_res, rows_grad, small, attn, feed = run_block(size, operands)

time: 181 us -> 162 us (0.90)
  Pallas kernels: 173 us -> 161 us
  local copies, waits for them, and re-layouts: 5.78 us -> 0 us
    pallas_call x1, Pallas kernels: 162 us -> 152 us  [run_block(): pl.pallas_call(functools.partial(block_kernel, size), out_shape=outs, in_...]
    unnamed x12 -> x0, local copies, waits for them, and re-layouts: 5.78 us -> none
    pallas_call x1, Pallas kernels: 11.2 us -> 8.57 us  [place_rows(): pl.pallas_call(functools.partial(place_kernel, size, assemble), grid=(1,)...]
where the time goes in v3:
time: 162 us
  Pallas kernels  161 us (99%)
    pallas_call x1, Pallas kernels, run_block(): pl.pallas_call(functools.partial(block_kernel, size), out_shape=outs, in_...  152 us
    pallas_call x1, Pallas kernels, place_rows(): pl.pallas_call(functools.partial(place_kernel, size, assemble), grid=(1,)...  8.57 us

profile of v3, /device:TPU:0, one launch (start us, length us, event | category | flops | bytes accessed | tf_op | source)
XLA Modules:
  0.0 161.8 jit_solution(7728140654293754402)
XLA Ops:
  0.6 152.4 %shard_map.220 = (bf16[256,1024]{1,0:T(8,128)(2,1)}, bf16[256,1024]{1,0:T(8,128)(2,1)}, f32[8,1024]{1,0:T(8,128)}, f32[2,128,512]{2,1,0:T(8,128)}, f32[2,128,1024]{2,1,0:T(8,128)}) custom-call(bf16[8,256,1024]{2,1,0:T(8,128)(2,1)} %bitcast.14, bf16[8,256,1024]{2,1,0:T(8,128)(2,1)} %bitcast.16, s32[1,256]{1,0:T(1,128)} %routed.1, s32[1,2048]{1,0:T(1,128)} %refs_3_.1, ...), custom_call_target="tpu_custom_call" | custom-call | tf_op jit(solution)/shard_map/pallas_call | solution.py:963
  153.0 8.6 %shard_map.221 = (bf16[2048,1024]{1,0:T(8,128)(2,1)}, bf16[2048,1024]{1,0:T(8,128)(2,1)}, f32[128,256]{1,0:T(8,128)}, f32[128,256]{1,0:T(8,128)}, f32[128,256]{1...) custom-call(s32[1,256]{1,0:T(1,128)} %routed.1, ...), custom_call_target="tpu_custom_call" | custom-call | tf_op jit(solution)/shard_map/pallas_call | solution.py:1058

commit v4 on v3

--- a/solution.py
+++ b/solution.py
@@ -480,73 +480,74 @@
         src = buf.at[s, :, :, 1 - core]
         return remote(src, into.at[s], gc_s.at[group], gc_r.at[group, s], core_dev)
 
-    def y_send(group, buf, into, s):
-        return remote(buf.at[s, 1 - y, :, core], into.at[s], gy_s.at[group], gy_r.at[group, s], y_dev)
-
-    def z_send(group, buf, into, s, device, slot):
-        src = buf.at[s, y, :, core]
-        return remote(src, into.at[slot], gz_s.at[group], gz_r.at[group, slot], device)
-
-    def add_into(ref, *others):
-        value = ref[...].astype(F32)
-        for other in others:
-            value = value + other[...].astype(F32)
-        ref[...] = value.astype(BF16)
+    halves = (1 - x, x)
+
+    def y_send(group, buf, into, s, b):
+        src = buf.at[s, 1 - y, b, core]
+        return remote(src, into.at[s, b], gy_s.at[group], gy_r.at[group, s, b], y_dev)
+
+    def z_send(group, buf, into, s, device, slot, b):
+        src = buf.at[s, y, b, core]
+        return remote(src, into.at[slot, b], gz_s.at[group], gz_r.at[group, slot, b], device)
+
+    def add_into(ref, other):
+        ref[...] = (ref[...].astype(F32) + other[...].astype(F32)).astype(BF16)
 
     def stage_core(group, buf, core_got, y_got, s):
         core_send(group, buf, core_got, s).wait_recv()
-        for a in range(2):
-            for b in range(2):
-                add_into(buf.at[s, a, b, core], core_got.at[s, a, b])
-        y_send(group, buf, y_got, s).start()
-
-    def stage_y(group, buf, y_got, s):
-        y_send(group, buf, y_got, s).wait_recv()
+        for b in halves:
+            add_into(buf.at[s, 1 - y, b, core], core_got.at[s, 1 - y, b])
+            y_send(group, buf, y_got, s, b).start()
         for b in range(2):
-            add_into(buf.at[s, y, b, core], y_got.at[s, b])
-
-    def line_in(group, buf, z_got, s, slot):
-        z_send(group, buf, z_got, s, up_dev, slot).wait_recv()
-        for b in range(2):
-            add_into(buf.at[s, y, b, core], z_got.at[slot, b])
-
-    def stage_z(group, buf, z_got, s):
+            add_into(buf.at[s, y, b, core], core_got.at[s, y, b])
+
+    def stage_y(group, buf, y_got, s, b):
+        y_send(group, buf, y_got, s, b).wait_recv()
+        add_into(buf.at[s, y, b, core], y_got.at[s, b])
+
+    def line_in(group, buf, z_got, s, slot, b):
+        z_send(group, buf, z_got, s, up_dev, slot, b).wait_recv()
+        add_into(buf.at[s, y, b, core], z_got.at[slot, b])
+
+    def stage_z(group, buf, z_got, s, b):
         @pl.when(s > z)
         def _():
             @pl.when(z > 0)
             def _():
-                line_in(group, buf, z_got, s, s)
-
-            z_send(group, buf, z_got, s, up_dev, s).start()
+                line_in(group, buf, z_got, s, s, b)
+
+            z_send(group, buf, z_got, s, up_dev, s, b).start()
 
         @pl.when(s < z)
         def _():
             @pl.when(z < shards - 1)
             def _():
-                line_in(group, buf, z_got, s, s)
+                line_in(group, buf, z_got, s, s, b)
 
             slot = jnp.where(s == z - 1, shards, s)
-            z_send(group, buf, z_got, s, down_dev, slot).start()
+            z_send(group, buf, z_got, s, down_dev, slot, b).start()
 
     def swap(group, pair):
         return remote(pair.at[0], pair.at[1], gx_s.at[group], gx_r.at[group], x_dev)
 
-    def stage_last(group, buf, z_got, pair, out):
-        for b in range(2):
+    def stage_last(group, buf, y_got, z_got, pair, out):
+        for b in halves:
+            stage_y(group, buf, y_got, z, b)
             out[b] = buf[z, y, b, core].astype(F32)
 
-        @pl.when(z > 0)
-        def _():
-            z_send(group, buf, z_got, z, up_dev, z).wait_recv()
-            out[...] += z_got[z].astype(F32)
-
-        @pl.when(z < shards - 1)
-        def _():
-            z_send(group, buf, z_got, z, up_dev, shards).wait_recv()
-            out[...] += z_got[shards].astype(F32)
-
-        pair[0] = out[1 - x].astype(BF16)
-        swap(group, pair).start()
+            @pl.when(z > 0)
+            def _():
+                z_send(group, buf, z_got, z, up_dev, z, b).wait_recv()
+                out[b] += z_got[z, b].astype(F32)
+
+            @pl.when(z < shards - 1)
+            def _():
+                z_send(group, buf, z_got, z, up_dev, shards, b).wait_recv()
+                out[b] += z_got[shards, b].astype(F32)
+
+            if b is halves[0]:
+                pair[0] = out[b].astype(BF16)
+                swap(group, pair).start()
 
     def stage_out(group, pair, out):
         swap(group, pair).wait_recv()
@@ -560,16 +561,46 @@
             value = mm(left[2 * a * quarter : 2 * (a + 1) * quarter, :], right).astype(BF16)
             buf[s, a, :, :, :, lo : lo + count] = value.reshape(2, 2, cut, count)
 
-    def line_step(group, buf, y_got, z_got, j):
-        s = order(j)
-        stage_y(group, buf, y_got, s)
-        stage_z(group, buf, z_got, s)
-
-    def feed_line(j):
-        line_step(0, grads, y_f, z_f, j)
-
-    def attn_line(j):
-        line_step(1, w_up, y_a, z_a, j)
+    def line_half(group, buf, y_got, z_got, s, m):
+        b = jnp.where(lax.rem(m, 2) == 0, 1 - x, x)
+        stage_y(group, buf, y_got, s, b)
+        stage_z(group, buf, z_got, s, b)
+
+    def feed_half(m):
+        line_half(0, grads, y_f, z_f, order(leaving(lax.div(m, 2))), m)
+
+    def attn_half(m):
+        line_half(1, w_up, y_a, z_a, reversed_order(lax.div(m, 2)), m)
+
+    def run_halves(step, first, last):
+        def body(m, carry):
+            step(m)
+            return carry
+
+        lax.fori_loop(first, last, body, 0)
+
+    total_halves = 2 * (shards - 1)
+
+    quick = shards == 4
+
+    def leaving(k):
+        if not quick:
+            return shards - 1 - k
+        ends, middle = jnp.where(edge, 2, 1), jnp.where(edge, 1, 2)
+        return jnp.where(k == 0, ends, jnp.where(k == 1, 3, jnp.where(k == 2, middle, 0)))
+
+    def feed_point(ends, middle):
+        if quick and ends is not None:
+
+            @pl.when(edge)
+            def _():
+                run_halves(feed_half, *ends)
+
+        if quick and middle is not None:
+
+            @pl.when(inner)
+            def _():
+                run_halves(feed_half, *middle)
 
     total[...] = jnp.zeros_like(total)
     for i in feed_mats:
@@ -606,11 +637,13 @@
 
         feed_chunk(order(j), 0)
 
-        @pl.when((j > 0) & (j + 2 < shards))
-        def _():
-            arrive(feed_mats[1:], j + 2)
-
-        relay(feed_mats, j + 1)
+        @pl.when((j > 1) & (j + 1 < shards))
+        def _():
+            arrive(feed_mats[1:], j + 1)
+
+        @pl.when(j + 2 < shards)
+        def _():
+            relay(feed_mats, j + 1)
 
         @pl.when(j + 3 < shards)
         def _():
@@ -618,44 +651,29 @@
 
         return carry
 
-    lax.fori_loop(0, shards - 2, own_step, 0)
+    lax.fori_loop(0, shards - 1, own_step, 0)
     x_h2.wait_recv()
     turn_a[...] = jnp.transpose(h2[...].reshape(2 * rows, width))
     turn_b[...] = jnp.transpose(dfeed[...].reshape(2 * rows, width))
 
-    quick = shards == 4
-
-    def leaving(k):
-        if not quick:
-            return shards - 1 - k
-        ends, middle = jnp.where(edge, 2, 1), jnp.where(edge, 1, 2)
-        return jnp.where(k == 0, ends, jnp.where(k == 1, 3, jnp.where(k == 2, middle, 0)))
-
     def other_step(k, carry):
-        late = jnp.where(quick & edge, 0, shards - 2)
-        mine = k == late
-
-        @pl.when(mine)
-        def _():
-            settle(1, shards - 2)
-
-        plain = jnp.where(k < late, k, shards - 2)
+        j = k
         if quick:
-            plain = jnp.where(edge, jnp.where(k < 2, 2, k - 2), jnp.where(k < 2, 1 - k, 2))
-        feed_chunk(order(plain), jnp.where(mine, 0, 1))
+            j = jnp.where(edge, jnp.where(k == 0, 2, k - 1), jnp.where(k < 2, 1 - k, k))
+        feed_chunk(order(j), 1)
         if quick:
 
-            @pl.when(k == jnp.where(edge, 1, 0))
+            @pl.when(k == 0)
             def _():
                 feed_grads(order(leaving(0)))
 
-            @pl.when(k == jnp.where(edge, 2, 1))
+            @pl.when(k == 1)
             def _():
                 feed_core(order(leaving(0)))
 
         return carry
 
-    lax.fori_loop(0, shards, other_step, 0)
+    lax.fori_loop(0, shards - 1, other_step, 0)
     relay(feed_mats, shards - 1)
     settle(1, shards - 1)
 
@@ -675,9 +693,9 @@
     def feed_grads_step(k, carry):
         if quick:
 
-            @pl.when((k == shards - 1) & edge)
+            @pl.when((k == 2) & edge)
             def _():
-                feed_line(leaving(0))
+                feed_half(0)
 
         feed_grads(order(leaving(k)))
 
@@ -688,6 +706,7 @@
         return carry
 
     lax.fori_loop(first_left, shards, feed_grads_step, 0)
+    feed_point((1, 2), None)
     feed_core(z)
 
     def feed_rows(half):
@@ -696,8 +715,6 @@
             value += mm(act[s, half * rows : (half + 1) * rows], w_down[s])
         return value
 
-    sent[1] = feed_rows(1).astype(BF16)
-    feed_own[...] = feed_rows(0)
     x_dh2.wait()
 
     def second_back(at, carry):
@@ -712,7 +729,10 @@
 
     second_sum = row_tiles(rows, second_back, jnp.zeros((8, width), F32))
     x_datt.start()
+    sent[1] = feed_rows(1).astype(BF16)
     x_feed.start()
+    feed_point((2, 3), (0, 1))
+    feed_own[...] = feed_rows(0)
 
     def attend_back(half):
         part = slice(half * rows, (half + 1) * rows)
@@ -745,19 +765,19 @@
         return value
 
     attend_back(0)
-    if quick:
-        feed_line(jnp.where(edge, leaving(1), leaving(0)))
+    feed_point((3, 4), (1, 2))
     total[0] = dh1_rows(0)
     turn_a[...] = jnp.transpose(h1[...].reshape(2 * rows, width))
     drain(1)
+    feed_point(None, (2, 3))
     x_datt.wait_recv()
     turn_b[...] = jnp.transpose(datt[...].reshape(2 * rows, width))
 
-    if quick:
-        feed_line(jnp.where(edge, leaving(2), leaving(1)))
+    feed_point((4, 5), None)
     attend_back(1)
     sent[0] = dh1_rows(1).astype(BF16)
     x_dh1.start()
+    feed_point((5, 6), (3, 5))
 
     def attn_grads(k, carry):
         s = reversed_order(k)
@@ -790,16 +810,12 @@
     energy = jnp.sum(jnp.sum(squares, axis=0, keepdims=True), axis=1, keepdims=True)
     rms = jnp.sqrt(energy / (width * jnp.maximum(count, 1.0)))
 
-    def feed_rest(k, carry):
-        feed_line(leaving(k))
-        return carry
-
-    lax.fori_loop(jnp.where(edge, 3, 2) if quick else 0, shards - 1, feed_rest, 0)
-
-    @pl.when(edge)
-    def _():
-        attn_line(shards - 1)
-
+    if quick:
+        feed_point(None, (5, 6))
+    else:
+        run_halves(feed_half, 0, total_halves)
+    ahead = jnp.where(edge, 2, 1)
+    run_halves(attn_half, 0, ahead)
     x_dh1.wait()
 
     def first_back(at, sums):
@@ -825,17 +841,13 @@
     for k in range(hops):
         small_send[k] = small
         small_copy(k).start()
+        if k > 0:
+            attn_half(ahead + k)
         small_copy(k).wait()
         small = small + small_got[k]
         if k == 0:
-
-            @pl.when(edge)
-            def _():
-                attn_line(shards - 2)
-
-            @pl.when(inner)
-            def _():
-                attn_line(shards - 1)
+            attn_half(ahead)
+    stage_last(0, grads, y_f, z_f, swap_f, feed_out)
 
     def small_spread(far, source):
         slot = hops + source
@@ -848,13 +860,8 @@
     for far in range(1, shards):
         small_spread(far, z).start()
 
-    def attn_rest(k, carry):
-        attn_line(shards - 2 - k)
-        return carry
-
-    lax.fori_loop(jnp.where(edge, 1, 0), shards - 2, attn_rest, 0)
-    stage_y(0, grads, y_f, z)
-    stage_last(0, grads, z_f, swap_f, feed_out)
+    run_halves(attn_half, ahead + hops, total_halves)
+    stage_last(1, w_up, y_a, z_a, swap_a, attn_out)
     for far in range(1, shards):
         small_spread(far, lax.rem(z + shards - far, shards)).wait_recv()
         small_spread(far, z).wait_send()
@@ -864,8 +871,6 @@
     row_at = lax.broadcasted_iota(jnp.int32, (8, 1), 0)
     small_send[0] = jnp.where(row_at == 3, rms, small)
     put(2, small_send.at[0]).start()
-    stage_y(1, w_up, y_a, z)
-    stage_last(1, w_up, z_a, swap_a, attn_out)
     stage_out(0, swap_f, feed_out)
     put(4, feed_out).start()
     stage_out(1, swap_a, attn_out)
@@ -877,9 +882,9 @@
 
     for group, core_got, y_got, z_got in ((0, core_f, y_f, z_f), (1, core_a, y_a, z_a)):
         remote(core_got, core_got, gc_s.at[group], gc_r.at[group, 0], core_dev).wait_send()
-        remote(y_got, y_got, gy_s.at[group], gy_r.at[group, 0], y_dev).wait_send()
+        remote(y_got, y_got, gy_s.at[group], gy_r.at[group, 0, 0], y_dev).wait_send()
         moved = z_got.at[0 : shards - 1]
-        remote(moved, moved, gz_s.at[group], gz_r.at[group, 0], up_dev).wait_send()
+        remote(moved, moved, gz_s.at[group], gz_r.at[group, 0, 0], up_dev).wait_send()
 
     swap(0, swap_f).wait_send()
     swap(1, swap_a).wait_send()
@@ -943,9 +948,9 @@
         dma((2,)),
         dma((2, shards)),
         dma((2,)),
-        dma((2, shards)),
+        dma((2, shards, 2)),
         dma((2,)),
-        dma((2, shards + 1)),
+        dma((2, shards + 1, 2)),
         dma((2,)),
         dma((2,)),
         dma((stages,)),

time: 162 us -> 154 us (0.951)
  Pallas kernels: 161 us -> 153 us
    pallas_call x1, Pallas kernels: 152 us -> 144 us  [run_block(): pl.pallas_call(functools.partial(block_kernel, size), out_shape=outs, in_...]
where the time goes in v4:
time: 154 us
  Pallas kernels  153 us (99%)
    pallas_call x1, Pallas kernels, run_block(): pl.pallas_call(functools.partial(block_kernel, size), out_shape=outs, in_...  144 us
    pallas_call x1, Pallas kernels, place_rows(): pl.pallas_call(functools.partial(place_kernel, size, assemble), grid=(1,)...  8.58 us

profile of v4, /device:TPU:0, one launch (start us, length us, event | category | flops | bytes accessed | tf_op | source)
XLA Modules:
  0.0 153.7 jit_solution(7986892158548771529)
XLA Ops:
  0.6 144.3 %shard_map.220 = (bf16[256,1024]{1,0:T(8,128)(2,1)}, bf16[256,1024]{1,0:T(8,128)(2,1)}, f32[8,1024]{1,0:T(8,128)}, f32[2,128,512]{2,1,0:T(8,128)}, f32[2,128,1024]{2,1,0:T(8,128)}) custom-call(bf16[8,256,1024]{2,1,0:T(8,128)(2,1)} %bitcast.14, bf16[8,256,1024]{2,1,0:T(8,128)(2,1)} %bitcast.16, s32[1,256]{1,0:T(1,128)} %routed.1, s32[1,2048]{1,0:T(1,128)} %refs_3_.1, ...), custom_call_target="tpu_custom_call" | custom-call | tf_op jit(solution)/shard_map/pallas_call | solution.py:968
  145.0 8.6 %shard_map.221 = (bf16[2048,1024]{1,0:T(8,128)(2,1)}, bf16[2048,1024]{1,0:T(8,128)(2,1)}, f32[128,256]{1,0:T(8,128)}, f32[128,256]{1,0:T(8,128)}, f32[128,256]{1...) custom-call(s32[1,256]{1,0:T(1,128)} %routed.1, ...), custom_call_target="tpu_custom_call" | custom-call | tf_op jit(solution)/shard_map/pallas_call | solution.py:1063

commit v5 on v4

--- a/solution.py
+++ b/solution.py
@@ -28,9 +28,9 @@
     return lax.dot_general(left, right, (((0,), (0,)), ((), ())), preferred_element_type=F32)
 
 
-def row_tiles(rows, body, init=0):
+def row_tiles(rows, body, init=0, first=0):
     def step(index, carry):
-        return body(pl.ds(pl.multiple_of(index * TILE, TILE), TILE), carry)
+        return body(pl.ds(pl.multiple_of(first + index * TILE, TILE), TILE), carry)
 
     return lax.fori_loop(0, rows // TILE, step, init)
 
@@ -114,8 +114,13 @@
         return pick + high * (shards - 1 - 2 * pick)
 
     attn_mats = list(range(len(qkv_in) + 1))
-    feed_mats = [len(attn_mats), len(attn_mats) + 1]
-    out_at, up_at = attn_mats[-1], feed_mats[0]
+    up_mats = [len(attn_mats), len(attn_mats) + 1]
+    down_mats = [len(attn_mats) + 2, len(attn_mats) + 3]
+    feed_mats = up_mats + down_mats
+    out_at, up_at, down_at = attn_mats[-1], up_mats[0], down_mats[0]
+
+    def down_rows(i, start=0):
+        return pl.ds(pl.multiple_of(start + (i - down_at) * (hidden // 2), hidden // 2), hidden // 2)
 
     def span(qy, qc):
         return pl.ds(pl.multiple_of((2 * qy + qc) * quarter, quarter), quarter)
@@ -129,9 +134,9 @@
             return part.at[s, span(qy, qc)]
         if i == out_at:
             return w_out.at[s, :, span(qy, qc)]
-        if i == up_at:
-            return w_up.at[s, qy, qc]
-        return w_down.at[s, :, span(qy, qc)]
+        if i < down_at:
+            return w_up.at[s, qy, qc, i - up_at]
+        return w_down.at[s, down_rows(i), span(qy, qc)]
 
     def own_piece(i):
         if i < out_at:
@@ -139,9 +144,9 @@
             return part if joined else part.at[:, lanes(narrow)]
         if i == out_at:
             return out_in.at[lanes(narrow), span(y, core)]
-        if i == up_at:
-            return up_in.at[y, core, :, :, lanes(hidden)]
-        return down_in.at[lanes(hidden), span(y, core)]
+        if i < down_at:
+            return up_in.at[y, core, i - up_at, :, lanes(hidden)]
+        return down_in.at[down_rows(i, x * hidden), span(y, core)]
 
     def load_own(i):
         if i < out_at:
@@ -151,10 +156,11 @@
                 src, dst = qkv_in[i].at[:, lanes(narrow)], w_qkv.at[z, :, i * narrow : (i + 1) * narrow]
         elif i == out_at:
             src, dst = out_in.at[lanes(narrow), :], w_out.at[z]
-        elif i == up_at:
-            src, dst = up_in.at[:, :, :, :, lanes(hidden)], w_up.at[z]
+        elif i < down_at:
+            b = i - up_at
+            src, dst = up_in.at[:, :, b, :, lanes(hidden)], w_up.at[z, :, :, b]
         else:
-            src, dst = down_in.at[lanes(hidden), :], w_down.at[z]
+            src, dst = down_in.at[down_rows(i, x * hidden), :], w_down.at[z, down_rows(i)]
         return pltpu.make_async_copy(src, dst, load_sem.at[i])
 
     def group_of(i):
@@ -272,8 +278,9 @@
 
     x_h1 = exchange(0, h1.at[0], h1.at[1])
     x_dfeed = exchange(1, dfeed.at[0], dfeed.at[1])
-    x_att = exchange(2, sent.at[0], got.at[0])
-    x_h2 = exchange(3, h2.at[0], h2.at[1])
+    upper, lower = slice(0, rows // 2), slice(rows // 2, rows)
+    x_att = [exchange(2 + 6 * k, sent.at[0, part], got.at[0, part]) for k, part in enumerate((upper, lower))]
+    x_h2 = [exchange(3 + 6 * k, h2.at[0, part], h2.at[1, part]) for k, part in enumerate((upper, lower))]
     x_dh2 = exchange(4, sent.at[0], got.at[0])
     x_feed = exchange(5, sent.at[1], got.at[1])
     x_datt = exchange(6, datt.at[0], datt.at[1])
@@ -421,7 +428,7 @@
         @pl.when(j + 1 == shards)
         def _():
             relay(attn_mats, j)
-            arrive(feed_mats[:1], 1)
+            arrive(up_mats, 1)
 
         @pl.when(j > 0)
         def _():
@@ -448,16 +455,17 @@
         return mm(jnp.concatenate(parts, axis=1), w_out[...].reshape(shards * narrow, width))
 
     sent[0] = project_out(1).astype(BF16)
-    x_att.start()
+    for copy in x_att:
+        copy.start()
     attended[...] = project_out(0)
-    arrive(feed_mats[1:], 1)
-    arrive(feed_mats[:1], 2)
+    arrive(down_mats, 1)
+    arrive(up_mats, 2)
 
     @pl.when(inner)
     def _():
-        arrive(feed_mats[1:], 2)
-
-    x_att.wait()
+        arrive(down_mats, 2)
+        for j in range(3, shards):
+            arrive(feed_mats, j)
 
     def mix(at, carry):
         att = attended[at] + got[0, at].astype(F32)
@@ -467,18 +475,22 @@
         h2[0, at] = (mixed * factor * second_gain[...]).astype(BF16)
         return carry
 
-    row_tiles(rows, mix)
-    x_h2.start()
+    for k in range(2):
+        x_att[k].wait()
+        row_tiles(rows // 2, mix, first=k * (rows // 2))
+        x_h2[k].start()
 
     @pl.when(edge)
     def _():
-        arrive(feed_mats[1:], 2)
+        arrive(down_mats, 2)
 
     x_dfeed.wait_recv()
 
-    def core_send(group, buf, into, s, at=None):
-        src = buf.at[s, :, :, 1 - core]
-        return remote(src, into.at[s], gc_s.at[group], gc_r.at[group, s], core_dev)
+    parts_of = (1 - y, y)
+
+    def core_send(group, buf, into, s, a):
+        src = buf.at[s, a, :, 1 - core]
+        return remote(src, into.at[s, a], gc_s.at[group], gc_r.at[group, s, a], core_dev)
 
     halves = (1 - x, x)
 
@@ -494,10 +506,11 @@
         ref[...] = (ref[...].astype(F32) + other[...].astype(F32)).astype(BF16)
 
     def stage_core(group, buf, core_got, y_got, s):
-        core_send(group, buf, core_got, s).wait_recv()
+        core_send(group, buf, core_got, s, 1 - y).wait_recv()
         for b in halves:
             add_into(buf.at[s, 1 - y, b, core], core_got.at[s, 1 - y, b])
             y_send(group, buf, y_got, s, b).start()
+        core_send(group, buf, core_got, s, y).wait_recv()
         for b in range(2):
             add_into(buf.at[s, y, b, core], core_got.at[s, y, b])
 
@@ -556,10 +569,10 @@
     def reversed_order(k):
         return order(shards - 1 - k)
 
-    def store_grads(buf, s, left, right, lo, count):
-        for a in range(2):
-            value = mm(left[2 * a * quarter : 2 * (a + 1) * quarter, :], right).astype(BF16)
-            buf[s, a, :, :, :, lo : lo + count] = value.reshape(2, 2, cut, count)
+    def store_grads(buf, s, a, left, right, lo, count):
+        part = pl.ds(pl.multiple_of(2 * a * quarter, 2 * quarter), 2 * quarter)
+        value = mm(left[part, :], right).astype(BF16)
+        buf[s, a, :, :, :, lo : lo + count] = value.reshape(2, 2, cut, count)
 
     def line_half(group, buf, y_got, z_got, s, m):
         b = jnp.where(lax.rem(m, 2) == 0, 1 - x, x)
@@ -603,13 +616,16 @@
                 run_halves(feed_half, *middle)
 
     total[...] = jnp.zeros_like(total)
+    turn_a[:, 0:rows] = jnp.transpose(h2[0])
+    turn_b[...] = jnp.transpose(dfeed[...].reshape(2 * rows, width))
     for i in feed_mats:
         load_own(i).wait()
 
     def feed_grads(s):
-        store_grads(grads, s, turn_a, dup[s], 0, hidden)
-        store_grads(grads, s, turn_b, act[s], hidden, hidden)
-        core_send(0, grads, core_f, s).start()
+        for a in parts_of:
+            store_grads(grads, s, a, turn_a, dup[s], 0, hidden)
+            store_grads(grads, s, a, turn_b, act[s], hidden, hidden)
+            core_send(0, grads, core_f, s, a).start()
 
     def feed_core(s):
         stage_core(0, grads, core_f, y_f, s)
@@ -637,24 +653,24 @@
 
         feed_chunk(order(j), 0)
 
-        @pl.when((j > 1) & (j + 1 < shards))
-        def _():
-            arrive(feed_mats[1:], j + 1)
+        @pl.when(edge & (j > 1) & (j + 1 < shards))
+        def _():
+            arrive(down_mats, j + 1)
 
         @pl.when(j + 2 < shards)
         def _():
             relay(feed_mats, j + 1)
 
-        @pl.when(j + 3 < shards)
-        def _():
-            arrive(feed_mats[:1], j + 3)
+        @pl.when(edge & (j + 3 < shards))
+        def _():
+            arrive(up_mats, j + 3)
 
         return carry
 
     lax.fori_loop(0, shards - 1, own_step, 0)
-    x_h2.wait_recv()
-    turn_a[...] = jnp.transpose(h2[...].reshape(2 * rows, width))
-    turn_b[...] = jnp.transpose(dfeed[...].reshape(2 * rows, width))
+    for copy in x_h2:
+        copy.wait_recv()
+    turn_a[:, rows : 2 * rows] = jnp.transpose(h2[1])
 
     def other_step(k, carry):
         j = k
@@ -781,9 +797,10 @@
 
     def attn_grads(k, carry):
         s = reversed_order(k)
-        store_grads(w_up, s, turn_a, act[s, :, 0 : 3 * narrow], 0, 3 * narrow)
-        store_grads(w_up, s, turn_b, ctx[s], 3 * narrow, narrow)
-        core_send(1, w_up, core_a, s).start()
+        for a in parts_of:
+            store_grads(w_up, s, a, turn_a, act[s, :, 0 : 3 * narrow], 0, 3 * narrow)
+            store_grads(w_up, s, a, turn_b, ctx[s], 3 * narrow, narrow)
+            core_send(1, w_up, core_a, s, a).start()
 
         @pl.when(k > 0)
         def _():
@@ -877,11 +894,11 @@
     put(3, attn_out).start()
 
     drain(0)
-    for copy in (x_h1, x_dfeed, x_h2, x_datt):
+    for copy in (x_h1, x_dfeed, *x_h2, x_datt):
         copy.wait_send()
 
     for group, core_got, y_got, z_got in ((0, core_f, y_f, z_f), (1, core_a, y_a, z_a)):
-        remote(core_got, core_got, gc_s.at[group], gc_r.at[group, 0], core_dev).wait_send()
+        remote(core_got, core_got, gc_s.at[group], gc_r.at[group, 0, 0], core_dev).wait_send()
         remote(y_got, y_got, gy_s.at[group], gy_r.at[group, 0, 0], y_dev).wait_send()
         moved = z_got.at[0 : shards - 1]
         remote(moved, moved, gz_s.at[group], gz_r.at[group, 0, 0], up_dev).wait_send()
@@ -895,7 +912,7 @@
 def run_block(size, operands):
     shards, rows, width = size["S"], size["R"], size["D"]
     heads, narrow, hidden, cut = size["hh"], size["n"], size["f"], size["DB"]
-    mats = (2 if size["joined"] else 4) + 2
+    mats = (2 if size["joined"] else 4) + 4
     stages = 3 + shards
     attn, feed = 4 * narrow, 2 * hidden
     dma = pltpu.SemaphoreType.DMA
@@ -943,10 +960,10 @@
         dma((mats, shards)),
         dma((2,)),
         dma((2, shards)),
-        dma((8,)),
-        dma((8,)),
+        dma((10,)),
+        dma((10,)),
         dma((2,)),
-        dma((2, shards)),
+        dma((2, shards, 2)),
         dma((2,)),
         dma((2, shards, 2)),
         dma((2,)),

time: 154 us -> 151 us (0.981); the launches traced: 154 us -> 148 us
  Pallas kernels: 153 us -> 148 us
    pallas_call x1, Pallas kernels: 144 us -> 139 us  [run_block(): pl.pallas_call(functools.partial(block_kernel, size), out_shape=outs, in_...]
where the time goes in v5:
time: 151 us; the launch traced here: 148 us
  Pallas kernels  148 us (98%)
    pallas_call x1, Pallas kernels, run_block(): pl.pallas_call(functools.partial(block_kernel, size), out_shape=outs, in_...  139 us
    pallas_call x1, Pallas kernels, place_rows(): pl.pallas_call(functools.partial(place_kernel, size, assemble), grid=(1,)...  8.57 us

profile of v5, /device:TPU:0, one launch (start us, length us, event | category | flops | bytes accessed | tf_op | source)
XLA Modules:
  0.0 148.4 jit_solution(15834940908905156508)
XLA Ops:
  0.6 139.0 %shard_map.220 = (bf16[256,1024]{1,0:T(8,128)(2,1)}, bf16[256,1024]{1,0:T(8,128)(2,1)}, f32[8,1024]{1,0:T(8,128)}, f32[2,128,512]{2,1,0:T(8,128)}, f32[2,128,1024]{2,1,0:T(8,128)}) custom-call(bf16[8,256,1024]{2,1,0:T(8,128)(2,1)} %bitcast.14, bf16[8,256,1024]{2,1,0:T(8,128)(2,1)} %bitcast.16, s32[1,256]{1,0:T(1,128)} %routed.1, s32[1,2048]{1,0:T(1,128)} %refs_3_.1, ...), custom_call_target="tpu_custom_call" | custom-call | tf_op jit(solution)/shard_map/pallas_call | solution.py:985
  139.7 8.6 %shard_map.221 = (bf16[2048,1024]{1,0:T(8,128)(2,1)}, bf16[2048,1024]{1,0:T(8,128)(2,1)}, f32[128,256]{1,0:T(8,128)}, f32[128,256]{1,0:T(8,128)}, f32[128,256]{1...) custom-call(s32[1,256]{1,0:T(1,128)} %routed.1, ...), custom_call_target="tpu_custom_call" | custom-call | tf_op jit(solution)/shard_map/pallas_call | solution.py:1080

commit v6 on v5

--- a/solution.py
+++ b/solution.py
@@ -56,7 +56,8 @@
         taken, refs[:count] = refs[:count], []
         return taken
 
-    tokens, cotangent, routed, valid, w_router, first_gain, second_gain = take(7)
+    tokens, cotangent = take(2)
+    small_in = take(5)
     qkv_in = take(1 if joined else 3)
     out_in, up_in, down_in = take(3)
     outputs = take(5)
@@ -77,11 +78,13 @@
     grads, core_f, y_f, z_f, core_a, y_a, z_a, swap_f, swap_a = take(9)
     attn_out, feed_out = take(2)
     small_send, small_got = take(2)
-    load_sem, tok_sem, out_sem = take(3)
+    routed, valid, w_router, first_gain, second_gain = small_held = take(5)
+    load_sem, tok_sem, out_sem, small_sem = take(4)
     wz_s, wz_r, wy_s, wy_r, wc_s, wc_r = take(6)
     x_s, x_r = take(2)
     gc_s, gc_r, gy_s, gy_r, gz_s, gz_r, gx_s, gx_r = take(8)
     sm_s, sm_r = take(2)
+    ex_sem = take(1)[0]
 
     dp = lax.axis_index("dp")
     z = lax.axis_index("mp")
@@ -166,6 +169,9 @@
     def group_of(i):
         return 0 if i <= out_at else 1
 
+    def y_group(i):
+        return 0 if i <= out_at else 1 if i < down_at else 2 + i - down_at
+
     def own_up(i):
         return remote(own_piece(i), held(i, z, y, core), wz_s.at[group_of(i), z], wz_r.at[i, z], up_dev)
 
@@ -178,7 +184,7 @@
 
     def across_y(i, s, qy):
         piece = held(i, s, qy, core)
-        return remote(piece, piece, wy_s.at[group_of(i)], wy_r.at[i, s], y_dev)
+        return remote(piece, piece, wy_s.at[y_group(i)], wy_r.at[i, s], y_dev)
 
     def across_core(i, s, qy, qc):
         piece = held(i, s, qy, qc)
@@ -224,11 +230,21 @@
     edge = (z == 0) | (z == shards - 1)
     inner = jnp.logical_not(edge)
 
+    def by_z_here(i, j):
+        return quick and i == by_z and isinstance(j, int) and j == 1
+
     def arrive_one(i, j):
         s = order(j)
         pass_on(i, s, up_dev).wait_recv()
         passing(s, lambda device: pass_on(i, s, device).start())
-        across_y(i, s, y).start()
+        if by_z_here(i, j):
+
+            @pl.when(inner)
+            def _():
+                across_y(i, s, y).start()
+
+        else:
+            across_y(i, s, y).start()
         across_core(i, s, y, core).start()
 
     def arrive(mats, j):
@@ -249,11 +265,33 @@
     def relay(mats, j):
         s = order(j)
         for i in mats:
-            across_y(i, s, 1 - y).wait_recv()
+            if by_z_here(i, j):
+
+                @pl.when(edge)
+                def _():
+                    bypass(s, up_dev).wait_recv()
+
+                @pl.when(inner)
+                def _():
+                    across_y(i, s, 1 - y).wait_recv()
+
+            else:
+                across_y(i, s, 1 - y).wait_recv()
             across_core(i, s, 1 - y, core).start()
 
     def settle(group, j):
         await_pieces(group, wc_r.at[group, order(j)], 2, True)
+
+    def await_y(index, blocks, count):
+        flat = w_up.at[0:count, 0, 0] if blocks == 2 else w_up.at[0:count, 0, 0, 0]
+        remote(flat, flat, wy_s.at[index], wy_r.at[0, 0], y_dev).wait_send()
+
+    quick = shards == 4
+    by_z = down_mats[-1]
+
+    def bypass(s, device):
+        src = down_in.at[down_rows(by_z, x * hidden), span(1 - y, core)]
+        return remote(src, held(by_z, s, 1 - y, core), ex_sem.at[0], ex_sem.at[1], device)
 
     def drain(group):
         @pl.when(z < shards - 1)
@@ -270,7 +308,24 @@
             return carry
 
         lax.fori_loop(1, shards, step, 0)
-        await_pieces(group, wy_s.at[group], shards - 1)
+        if group == 0:
+            await_pieces(0, wy_s.at[0], shards - 1)
+        else:
+            await_y(1, 2, shards - 1)
+            await_y(2, 1, shards - 1)
+            if not quick:
+                await_y(3, 1, shards - 1)
+            else:
+
+                @pl.when(edge)
+                def _():
+                    await_y(3, 1, shards - 2)
+
+                @pl.when(inner)
+                def _():
+                    await_y(3, 1, shards - 1)
+                    bypass(z, up_dev).wait_send()
+
         await_pieces(group, wc_s.at[group], 2 * (shards - 1))
 
     def exchange(slot, src, dst):
@@ -281,9 +336,9 @@
     upper, lower = slice(0, rows // 2), slice(rows // 2, rows)
     x_att = [exchange(2 + 6 * k, sent.at[0, part], got.at[0, part]) for k, part in enumerate((upper, lower))]
     x_h2 = [exchange(3 + 6 * k, h2.at[0, part], h2.at[1, part]) for k, part in enumerate((upper, lower))]
-    x_dh2 = exchange(4, sent.at[0], got.at[0])
+    x_dh2 = [exchange(4 + 6 * k, sent.at[0, part], got.at[0, part]) for k, part in enumerate((upper, lower))]
     x_feed = exchange(5, sent.at[1], got.at[1])
-    x_datt = exchange(6, datt.at[0], datt.at[1])
+    x_datt = [exchange(6 + 5 * k, datt.at[0, part], datt.at[1, part]) for k, part in enumerate((upper, lower))]
     x_dh1 = exchange(7, sent.at[0], got.at[0])
 
     def put(k, src):
@@ -314,6 +369,9 @@
     def _():
         greet(up_dev)
 
+    small_loads = [pltpu.make_async_copy(src, dst, small_sem.at[k]) for k, (src, dst) in enumerate(zip(small_in, small_held))]
+    for copy in small_loads:
+        copy.start()
     for t in range(2):
         for copy in block_loads(t):
             copy.start()
@@ -340,6 +398,8 @@
         def _():
             send_own_down(feed_mats)
 
+    for copy in small_loads:
+        copy.wait()
     as_rows = jnp.broadcast_to(routed[...].astype(F32), (8, rows))
     position = jnp.transpose(as_rows)[:, 0:1].astype(jnp.int32)
     flags = jnp.zeros((rows, 1), F32)
@@ -466,6 +526,15 @@
         arrive(down_mats, 2)
         for j in range(3, shards):
             arrive(feed_mats, j)
+        if quick:
+
+            @pl.when(z == 1)
+            def _():
+                bypass(z, down_dev).start()
+
+            @pl.when(z == shards - 2)
+            def _():
+                bypass(z, up_dev).start()
 
     def mix(at, carry):
         att = attended[at] + got[0, at].astype(F32)
@@ -480,9 +549,10 @@
         row_tiles(rows // 2, mix, first=k * (rows // 2))
         x_h2[k].start()
 
-    @pl.when(edge)
-    def _():
-        arrive(down_mats, 2)
+        @pl.when(edge)
+        def _():
+            arrive(down_mats[k : k + 1], 2)
+
 
     x_dfeed.wait_recv()
 
@@ -494,13 +564,26 @@
 
     halves = (1 - x, x)
 
-    def y_send(group, buf, into, s, b):
-        src = buf.at[s, 1 - y, b, core]
-        return remote(src, into.at[s, b], gy_s.at[group], gy_r.at[group, s, b], y_dev)
-
-    def z_send(group, buf, into, s, device, slot, b):
-        src = buf.at[s, y, b, core]
-        return remote(src, into.at[slot, b], gz_s.at[group], gz_r.at[group, slot, b], device)
+    def columns_of(group, c):
+        return slice(c * 2 * narrow, (c + 1) * 2 * narrow) if group == 1 else slice(0, 2 * hidden)
+
+    def pieces(group):
+        return range(2) if group == 1 else range(1)
+
+    def sem_at(group, b, c):
+        return 2 + 2 * b + c if group == 1 else b
+
+    def y_send(group, buf, into, s, b, c):
+        cols = columns_of(group, c)
+        src = buf.at[s, 1 - y, b, core, :, cols]
+        recv = gy_r.at[s, sem_at(group, b, c)]
+        return remote(src, into.at[s, b, :, cols], gy_s.at[group], recv, y_dev)
+
+    def z_send(group, buf, into, s, device, slot, b, c):
+        cols = columns_of(group, c)
+        src = buf.at[s, y, b, core, :, cols]
+        recv = gz_r.at[slot, sem_at(group, b, c)]
+        return remote(src, into.at[slot, b, :, cols], gz_s.at[group], recv, device)
 
     def add_into(ref, other):
         ref[...] = (ref[...].astype(F32) + other[...].astype(F32)).astype(BF16)
@@ -509,61 +592,69 @@
         core_send(group, buf, core_got, s, 1 - y).wait_recv()
         for b in halves:
             add_into(buf.at[s, 1 - y, b, core], core_got.at[s, 1 - y, b])
-            y_send(group, buf, y_got, s, b).start()
+            for c in pieces(group):
+                y_send(group, buf, y_got, s, b, c).start()
         core_send(group, buf, core_got, s, y).wait_recv()
         for b in range(2):
             add_into(buf.at[s, y, b, core], core_got.at[s, y, b])
 
-    def stage_y(group, buf, y_got, s, b):
-        y_send(group, buf, y_got, s, b).wait_recv()
-        add_into(buf.at[s, y, b, core], y_got.at[s, b])
-
-    def line_in(group, buf, z_got, s, slot, b):
-        z_send(group, buf, z_got, s, up_dev, slot, b).wait_recv()
-        add_into(buf.at[s, y, b, core], z_got.at[slot, b])
-
-    def stage_z(group, buf, z_got, s, b):
+    def stage_y(group, buf, y_got, s, b, c):
+        y_send(group, buf, y_got, s, b, c).wait_recv()
+        cols = columns_of(group, c)
+        add_into(buf.at[s, y, b, core, :, cols], y_got.at[s, b, :, cols])
+
+    def line_in(group, buf, z_got, s, slot, b, c):
+        z_send(group, buf, z_got, s, up_dev, slot, b, c).wait_recv()
+        cols = columns_of(group, c)
+        add_into(buf.at[s, y, b, core, :, cols], z_got.at[slot, b, :, cols])
+
+    def stage_z(group, buf, z_got, s, b, c):
         @pl.when(s > z)
         def _():
             @pl.when(z > 0)
             def _():
-                line_in(group, buf, z_got, s, s, b)
-
-            z_send(group, buf, z_got, s, up_dev, s, b).start()
+                line_in(group, buf, z_got, s, s, b, c)
+
+            z_send(group, buf, z_got, s, up_dev, s, b, c).start()
 
         @pl.when(s < z)
         def _():
             @pl.when(z < shards - 1)
             def _():
-                line_in(group, buf, z_got, s, s, b)
+                line_in(group, buf, z_got, s, s, b, c)
 
             slot = jnp.where(s == z - 1, shards, s)
-            z_send(group, buf, z_got, s, down_dev, slot, b).start()
-
-    def swap(group, pair):
-        return remote(pair.at[0], pair.at[1], gx_s.at[group], gx_r.at[group], x_dev)
+            z_send(group, buf, z_got, s, down_dev, slot, b, c).start()
+
+    def swap(group, pair, c):
+        cols = columns_of(group, c)
+        index = 1 + c if group == 1 else 0
+        return remote(pair.at[0, :, cols], pair.at[1, :, cols], gx_s.at[index], gx_r.at[index], x_dev)
 
     def stage_last(group, buf, y_got, z_got, pair, out):
         for b in halves:
-            stage_y(group, buf, y_got, z, b)
-            out[b] = buf[z, y, b, core].astype(F32)
-
-            @pl.when(z > 0)
-            def _():
-                z_send(group, buf, z_got, z, up_dev, z, b).wait_recv()
-                out[b] += z_got[z, b].astype(F32)
-
-            @pl.when(z < shards - 1)
-            def _():
-                z_send(group, buf, z_got, z, up_dev, shards, b).wait_recv()
-                out[b] += z_got[shards, b].astype(F32)
-
-            if b is halves[0]:
-                pair[0] = out[b].astype(BF16)
-                swap(group, pair).start()
+            for c in pieces(group):
+                cols = columns_of(group, c)
+                stage_y(group, buf, y_got, z, b, c)
+                out[b, :, cols] = buf[z, y, b, core, :, cols].astype(F32)
+
+                @pl.when(z > 0)
+                def _():
+                    z_send(group, buf, z_got, z, up_dev, z, b, c).wait_recv()
+                    out[b, :, cols] += z_got[z, b, :, cols].astype(F32)
+
+                @pl.when(z < shards - 1)
+                def _():
+                    z_send(group, buf, z_got, z, up_dev, shards, b, c).wait_recv()
+                    out[b, :, cols] += z_got[shards, b, :, cols].astype(F32)
+
+                if b is halves[0]:
+                    pair[0, :, cols] = out[b, :, cols].astype(BF16)
+                    swap(group, pair, c).start()
 
     def stage_out(group, pair, out):
-        swap(group, pair).wait_recv()
+        for c in pieces(group):
+            swap(group, pair, c).wait_recv()
         out[1 - x] = pair[1].astype(F32)
 
     def reversed_order(k):
@@ -576,8 +667,9 @@
 
     def line_half(group, buf, y_got, z_got, s, m):
         b = jnp.where(lax.rem(m, 2) == 0, 1 - x, x)
-        stage_y(group, buf, y_got, s, b)
-        stage_z(group, buf, z_got, s, b)
+        for c in pieces(group):
+            stage_y(group, buf, y_got, s, b, c)
+            stage_z(group, buf, z_got, s, b, c)
 
     def feed_half(m):
         line_half(0, grads, y_f, z_f, order(leaving(lax.div(m, 2))), m)
@@ -593,8 +685,6 @@
         lax.fori_loop(first, last, body, 0)
 
     total_halves = 2 * (shards - 1)
-
-    quick = shards == 4
 
     def leaving(k):
         if not quick:
@@ -646,24 +736,52 @@
         row_tiles(rows, turn)
         total[half] += mm_nt(dup[s, part], up_here)
 
-    def own_step(j, carry):
-        @pl.when(j > 0)
+    def own_step(i, carry):
+        j = jnp.where(edge, 2 * i, i) if quick else i
+        active = inner | (i < 2) if quick else i >= 0
+
+        @pl.when(active & (i > 0))
         def _():
             settle(1, j)
 
-        feed_chunk(order(j), 0)
-
-        @pl.when(edge & (j > 1) & (j + 1 < shards))
-        def _():
-            arrive(down_mats, j + 1)
-
-        @pl.when(j + 2 < shards)
-        def _():
-            relay(feed_mats, j + 1)
-
-        @pl.when(edge & (j + 3 < shards))
-        def _():
-            arrive(up_mats, j + 3)
+        @pl.when(active)
+        def _():
+            feed_chunk(order(j), 0)
+
+        if quick:
+
+            @pl.when(edge & (i == 0))
+            def _():
+                relay(feed_mats[:-1], 1)
+                arrive(up_mats, 3)
+                relay(feed_mats, 2)
+
+            @pl.when(edge & (i == 1))
+            def _():
+                arrive(down_mats, 3)
+                relay(up_mats, 3)
+
+            @pl.when(inner & (i == 0))
+            def _():
+                relay(feed_mats, 1)
+
+            @pl.when(inner & (i == 1))
+            def _():
+                relay(feed_mats, 2)
+
+        else:
+
+            @pl.when(edge & (j > 1) & (j + 1 < shards))
+            def _():
+                arrive(down_mats, j + 1)
+
+            @pl.when(j + 2 < shards)
+            def _():
+                relay(feed_mats, j + 1)
+
+            @pl.when(edge & (j + 3 < shards))
+            def _():
+                arrive(up_mats, j + 3)
 
         return carry
 
@@ -673,38 +791,73 @@
     turn_a[:, rows : 2 * rows] = jnp.transpose(h2[1])
 
     def other_step(k, carry):
-        j = k
+        j, active = k, k >= 0
         if quick:
-            j = jnp.where(edge, jnp.where(k == 0, 2, k - 1), jnp.where(k < 2, 1 - k, k))
-        feed_chunk(order(j), 1)
+            j = jnp.where(edge, 2 - 2 * k, jnp.where(k < 2, 1 - k, 2))
+            active = inner | (k < 2)
+
+        @pl.when(active)
+        def _():
+            feed_chunk(order(j), 1)
+
         if quick:
 
             @pl.when(k == 0)
             def _():
                 feed_grads(order(leaving(0)))
-
-            @pl.when(k == 1)
-            def _():
                 feed_core(order(leaving(0)))
 
         return carry
 
     lax.fori_loop(0, shards - 1, other_step, 0)
-    relay(feed_mats, shards - 1)
-    settle(1, shards - 1)
 
     def last_step(k, carry):
-        feed_chunk(order(shards - 1), 1 - k)
+        j, half, final = shards - 1, 1 - k, 0
+        if quick:
+            j = jnp.where(edge & (lax.rem(k, 2) == 1), 1, shards - 1)
+            half = jnp.where(edge, jnp.where(k < 2, 1, 0), 1 - k)
+            final = jnp.where(edge, 1, 0)
+
+            @pl.when(inner & (k == 0))
+            def _():
+                relay(up_mats, shards - 1)
 
         @pl.when(k == 0)
         def _():
+            relay(down_mats if quick else feed_mats, shards - 1)
+
+        if quick:
+
+            @pl.when(edge & (k == 0))
+            def _():
+                relay([by_z], 1)
+
+        @pl.when(k <= final)
+        def _():
+            settle(1, j)
+
+        feed_chunk(order(j), half)
+
+        @pl.when(k == final)
+        def _():
             sent[0] = total[1].astype(BF16)
-            x_dh2.start()
+            for copy in x_dh2:
+                copy.start()
+
+        if quick:
+
+            @pl.when(edge & (k == 2))
+            def _():
+                feed_grads(order(leaving(1)))
+
+            @pl.when(edge & (k == 3))
+            def _():
+                feed_core(order(leaving(1)))
 
         return carry
 
-    lax.fori_loop(0, 2, last_step, 0)
-    first_left = 1 if quick else 0
+    lax.fori_loop(0, jnp.where(edge, 4, 2) if quick else 2, last_step, 0)
+    first_left = jnp.where(edge, 2, 1) if quick else 0
 
     def feed_grads_step(k, carry):
         if quick:
@@ -730,8 +883,6 @@
         for s in range(1, shards):
             value += mm(act[s, half * rows : (half + 1) * rows], w_down[s])
         return value
-
-    x_dh2.wait()
 
     def second_back(at, carry):
         dh2 = total[0, at] + got[0, at].astype(F32)
@@ -743,8 +894,11 @@
         datt[0, at] = (gate(at) * own_c[at].astype(F32) + back).astype(BF16)
         return carry + fold_rows(dh2 * mixed * factor)
 
-    second_sum = row_tiles(rows, second_back, jnp.zeros((8, width), F32))
-    x_datt.start()
+    second_sum = jnp.zeros((8, width), F32)
+    for k in range(2):
+        x_dh2[k].wait()
+        second_sum = row_tiles(rows // 2, second_back, second_sum, first=k * (rows // 2))
+        x_datt[k].start()
     sent[1] = feed_rows(1).astype(BF16)
     x_feed.start()
     feed_point((2, 3), (0, 1))
@@ -786,7 +940,8 @@
     turn_a[...] = jnp.transpose(h1[...].reshape(2 * rows, width))
     drain(1)
     feed_point(None, (2, 3))
-    x_datt.wait_recv()
+    for copy in x_datt:
+        copy.wait_recv()
     turn_b[...] = jnp.transpose(datt[...].reshape(2 * rows, width))
 
     feed_point((4, 5), None)
@@ -894,17 +1049,18 @@
     put(3, attn_out).start()
 
     drain(0)
-    for copy in (x_h1, x_dfeed, *x_h2, x_datt):
+    for copy in (x_h1, x_dfeed, *x_h2, *x_datt):
         copy.wait_send()
 
     for group, core_got, y_got, z_got in ((0, core_f, y_f, z_f), (1, core_a, y_a, z_a)):
         remote(core_got, core_got, gc_s.at[group], gc_r.at[group, 0, 0], core_dev).wait_send()
-        remote(y_got, y_got, gy_s.at[group], gy_r.at[group, 0, 0], y_dev).wait_send()
+        remote(y_got, y_got, gy_s.at[group], gy_r.at[0, 0], y_dev).wait_send()
         moved = z_got.at[0 : shards - 1]
-        remote(moved, moved, gz_s.at[group], gz_r.at[group, 0, 0], up_dev).wait_send()
-
-    swap(0, swap_f).wait_send()
-    swap(1, swap_a).wait_send()
+        remote(moved, moved, gz_s.at[group], gz_r.at[0, 0], up_dev).wait_send()
+
+    swap(0, swap_f, 0).wait_send()
+    for c in pieces(1):
+        swap(1, swap_a, c).wait_send()
     for k, src in enumerate((sent.at[1], got.at[1], small_send.at[0], attn_out, feed_out)):
         put(k, src).wait()
 
@@ -951,29 +1107,33 @@
         full(2, cut, feed),
         full(stages, 8, width),
         full(stages, 8, width),
+        pltpu.VMEM((1, rows), jnp.int32),
+        pltpu.VMEM((1, size["L"]), jnp.int32),
+        *[full(1, width) for _ in range(3)],
         dma((mats,)),
         dma((2, 2)),
         dma((5,)),
+        dma((5,)),
         dma((2, shards + 1)),
         dma((mats, shards)),
-        dma((2,)),
+        dma((4,)),
         dma((mats, shards)),
         dma((2,)),
         dma((2, shards)),
-        dma((10,)),
-        dma((10,)),
+        dma((12,)),
+        dma((12,)),
         dma((2,)),
         dma((2, shards, 2)),
         dma((2,)),
-        dma((2, shards, 2)),
+        dma((shards, 6)),
         dma((2,)),
-        dma((2, shards + 1, 2)),
-        dma((2,)),
-        dma((2,)),
+        dma((shards + 1, 6)),
+        dma((3,)),
+        dma((3,)),
         dma((stages,)),
         dma((stages,)),
+        dma((2,)),
     ]
-    near = pl.BlockSpec(memory_space=pltpu.VMEM)
     far = pl.BlockSpec(memory_space=pl.ANY)
     outs = [
         jax.ShapeDtypeStruct((rows, width), BF16),
@@ -985,7 +1145,7 @@
     return pl.pallas_call(
         functools.partial(block_kernel, size),
         out_shape=outs,
-        in_specs=[far, far] + [near] * 5 + [far] * (len(operands) - 7),
+        in_specs=[far] * len(operands),
         out_specs=[pl.BlockSpec(memory_space=pltpu.HBM)] * len(outs),
         scratch_shapes=scratch,
         compiler_params=pltpu.CompilerParams(

time: 151 us -> 149 us (0.987)
  no operation moved by 1% of the time
where the time goes in v6:
time: 149 us; the launch traced here: 148 us
  Pallas kernels  147 us (99%)
    pallas_call x1, Pallas kernels, run_block(): pl.pallas_call(functools.partial(block_kernel, size), out_shape=outs, in_...  138 us
    pallas_call x1, Pallas kernels, place_rows(): pl.pallas_call(functools.partial(place_kernel, size, assemble), grid=(1,)...  8.54 us

profile of v6, /device:TPU:0, one launch (start us, length us, event | category | flops | bytes accessed | tf_op | source)
XLA Modules:
  0.0 147.5 jit_solution(6746251830668241740)
XLA Ops:
  0.6 138.2 %shard_map.220 = (bf16[256,1024]{1,0:T(8,128)(2,1)}, bf16[256,1024]{1,0:T(8,128)(2,1)}, f32[8,1024]{1,0:T(8,128)}, f32[2,128,512]{2,1,0:T(8,128)}, f32[2,128,1024]{2,1,0:T(8,128)}) custom-call(bf16[8,256,1024]{2,1,0:T(8,128)(2,1)} %bitcast.14, bf16[8,256,1024]{2,1,0:T(8,128)(2,1)} %bitcast.16, s32[1,256]{1,0:T(1,128)} %routed.1, s32[1,2048]{1,0:T(1,128)} %refs_3_.1, ...), custom_call_target="tpu_custom_call" | custom-call | tf_op jit(solution)/shard_map/pallas_call | solution.py:1145
  138.8 8.5 %shard_map.221 = (bf16[2048,1024]{1,0:T(8,128)(2,1)}, bf16[2048,1024]{1,0:T(8,128)(2,1)}, f32[128,256]{1,0:T(8,128)}, f32[128,256]{1,0:T(8,128)}, f32[128,256]{1...) custom-call(s32[1,256]{1,0:T(1,128)} %routed.1, ...), custom_call_target="tpu_custom_call" | custom-call | tf_op jit(solution)/shard_map/pallas_call | solution.py:1240

commit v7 on v6

--- a/solution.py
+++ b/solution.py
@@ -397,6 +397,8 @@
         @pl.when(z == shards - 1)
         def _():
             send_own_down(feed_mats)
+
+    begin()
 
     for copy in small_loads:
         copy.wait()
@@ -417,8 +419,6 @@
                 copy.start()
         mask = valid[:, 2 * t * rows : 2 * (t + 1) * rows].astype(F32)
         flags = flags + jnp.sum(chosen * mask, axis=1, keepdims=True)
-        if t == steps // 2 - 1:
-            begin()
     columns[...] = jnp.broadcast_to(flags, columns.shape)
 
     def prepare(at, carry):

time: 149 us -> 146 us (0.980)
  Pallas kernels: 147 us -> 144 us
    pallas_call x1, Pallas kernels: 138 us -> 136 us  [run_block(): pl.pallas_call(functools.partial(block_kernel, size), out_shape=outs, in_...]
where the time goes in v7:
time: 146 us; the launch traced here: 145 us
  Pallas kernels  144 us (99%)
    pallas_call x1, Pallas kernels, run_block(): pl.pallas_call(functools.partial(block_kernel, size), out_shape=outs, in_...  136 us
    pallas_call x1, Pallas kernels, place_rows(): pl.pallas_call(functools.partial(place_kernel, size, assemble), grid=(1,)...  8.55 us

profile of v7, /device:TPU:0, one launch (start us, length us, event | category | flops | bytes accessed | tf_op | source)
XLA Modules:
  0.0 145.3 jit_solution(16480759657603887143)
XLA Ops:
  0.6 135.9 %shard_map.220 = (bf16[256,1024]{1,0:T(8,128)(2,1)}, bf16[256,1024]{1,0:T(8,128)(2,1)}, f32[8,1024]{1,0:T(8,128)}, f32[2,128,512]{2,1,0:T(8,128)}, f32[2,128,1024]{2,1,0:T(8,128)}) custom-call(bf16[8,256,1024]{2,1,0:T(8,128)(2,1)} %bitcast.14, bf16[8,256,1024]{2,1,0:T(8,128)(2,1)} %bitcast.16, s32[1,256]{1,0:T(1,128)} %routed.1, s32[1,2048]{1,0:T(1,128)} %refs_3_.1, ...), custom_call_target="tpu_custom_call" | custom-call | tf_op jit(solution)/shard_map/pallas_call | solution.py:1145
  136.5 8.5 %shard_map.221 = (bf16[2048,1024]{1,0:T(8,128)(2,1)}, bf16[2048,1024]{1,0:T(8,128)(2,1)}, f32[128,256]{1,0:T(8,128)}, f32[128,256]{1,0:T(8,128)}, f32[128,256]{1...) custom-call(s32[1,256]{1,0:T(1,128)} %routed.1, ...), custom_call_target="tpu_custom_call" | custom-call | tf_op jit(solution)/shard_map/pallas_call | solution.py:1240

commit v8 on v7

--- a/solution.py
+++ b/solution.py
@@ -485,10 +485,14 @@
     def attend(j, carry):
         s = order(j)
 
+        @pl.when(j + 2 == shards)
+        def _():
+            arrive(up_mats[:1], 1)
+
         @pl.when(j + 1 == shards)
         def _():
             relay(attn_mats, j)
-            arrive(up_mats, 1)
+            arrive(up_mats[1:], 1)
 
         @pl.when(j > 0)
         def _():
@@ -758,8 +762,7 @@
 
             @pl.when(edge & (i == 1))
             def _():
-                arrive(down_mats, 3)
-                relay(up_mats, 3)
+                arrive(down_mats[:1], 3)
 
             @pl.when(inner & (i == 0))
             def _():
@@ -802,10 +805,18 @@
 
         if quick:
 
+            @pl.when(edge & (k == 0))
+            def _():
+                arrive(down_mats[1:], 3)
+
             @pl.when(k == 0)
             def _():
                 feed_grads(order(leaving(0)))
                 feed_core(order(leaving(0)))
+
+            @pl.when(edge & (k == 0))
+            def _():
+                relay(up_mats, 3)
 
         return carry
 
@@ -1015,6 +1026,12 @@
         small_copy(k).start()
         if k > 0:
             attn_half(ahead + k)
+        if k == hops - 1:
+
+            @pl.when(inner)
+            def _():
+                attn_half(ahead + hops)
+
         small_copy(k).wait()
         small = small + small_got[k]
         if k == 0:
@@ -1032,7 +1049,7 @@
     for far in range(1, shards):
         small_spread(far, z).start()
 
-    run_halves(attn_half, ahead + hops, total_halves)
+    run_halves(attn_half, ahead + hops + jnp.where(edge, 0, 1), total_halves)
     stage_last(1, w_up, y_a, z_a, swap_a, attn_out)
     for far in range(1, shards):
         small_spread(far, lax.rem(z + shards - far, shards)).wait_recv()

time: 146 us -> 145 us (level)
  no operation moved by 1% of the time
where the time goes in v8:
time: 145 us
  Pallas kernels  144 us (99%)
    pallas_call x1, Pallas kernels, run_block(): pl.pallas_call(functools.partial(block_kernel, size), out_shape=outs, in_...  136 us
    pallas_call x1, Pallas kernels, place_rows(): pl.pallas_call(functools.partial(place_kernel, size, assemble), grid=(1,)...  8.58 us

profile of v8, /device:TPU:0, one launch (start us, length us, event | category | flops | bytes accessed | tf_op | source)
XLA Modules:
  0.0 145.2 jit_solution(2234627052574920921)
XLA Ops:
  0.6 135.7 %shard_map.220 = (bf16[256,1024]{1,0:T(8,128)(2,1)}, bf16[256,1024]{1,0:T(8,128)(2,1)}, f32[8,1024]{1,0:T(8,128)}, f32[2,128,512]{2,1,0:T(8,128)}, f32[2,128,1024]{2,1,0:T(8,128)}) custom-call(bf16[8,256,1024]{2,1,0:T(8,128)(2,1)} %bitcast.14, bf16[8,256,1024]{2,1,0:T(8,128)(2,1)} %bitcast.16, s32[1,256]{1,0:T(1,128)} %routed.1, s32[1,2048]{1,0:T(1,128)} %refs_3_.1, ...), custom_call_target="tpu_custom_call" | custom-call | tf_op jit(solution)/shard_map/pallas_call | solution.py:1162
  136.4 8.6 %shard_map.221 = (bf16[2048,1024]{1,0:T(8,128)(2,1)}, bf16[2048,1024]{1,0:T(8,128)(2,1)}, f32[128,256]{1,0:T(8,128)}, f32[128,256]{1,0:T(8,128)}, f32[128,256]{1...) custom-call(s32[1,256]{1,0:T(1,128)} %routed.1, ...), custom_call_target="tpu_custom_call" | custom-call | tf_op jit(solution)/shard_map/pallas_call | solution.py:1257

commit v9 on v8

--- a/solution.py
+++ b/solution.py
@@ -344,6 +344,9 @@
     def put(k, src):
         return pltpu.make_async_copy(src, outputs[k], out_sem.at[k])
 
+    def put_half(b, index):
+        return pltpu.make_async_copy(attn_out.at[b], outputs[3].at[b], out_sem.at[5 + index])
+
     steps = length // (2 * rows)
     stages = ((got, sent), (h2, datt))
 
@@ -358,9 +361,6 @@
     def greet(device):
         pl.semaphore_signal(barrier, inc=1, device_id=device, device_id_type=pl.DeviceIdType.MESH)
 
-    for device in (core_dev, x_dev, y_dev):
-        greet(device)
-
     @pl.when(z > 0)
     def _():
         greet(down_dev)
@@ -368,6 +368,9 @@
     @pl.when(z < shards - 1)
     def _():
         greet(up_dev)
+
+    for device in (y_dev, x_dev, core_dev):
+        greet(device)
 
     small_loads = [pltpu.make_async_copy(src, dst, small_sem.at[k]) for k, (src, dst) in enumerate(zip(small_in, small_held))]
     for copy in small_loads:
@@ -1062,8 +1065,9 @@
     put(2, small_send.at[0]).start()
     stage_out(0, swap_f, feed_out)
     put(4, feed_out).start()
+    put_half(x, 0).start()
     stage_out(1, swap_a, attn_out)
-    put(3, attn_out).start()
+    put_half(1 - x, 1).start()
 
     drain(0)
     for copy in (x_h1, x_dfeed, *x_h2, *x_datt):
@@ -1079,7 +1083,10 @@
     for c in pieces(1):
         swap(1, swap_a, c).wait_send()
     for k, src in enumerate((sent.at[1], got.at[1], small_send.at[0], attn_out, feed_out)):
-        put(k, src).wait()
+        if k != 3:
+            put(k, src).wait()
+    put_half(x, 0).wait()
+    put_half(1 - x, 1).wait()
 
 
 def run_block(size, operands):
@@ -1129,7 +1136,7 @@
         *[full(1, width) for _ in range(3)],
         dma((mats,)),
         dma((2, 2)),
-        dma((5,)),
+        dma((7,)),
         dma((5,)),
         dma((2, shards + 1)),
         dma((mats, shards)),

time: 145 us -> 145 us (level)
  no operation moved by 1% of the time
where the time goes in v9:
time: 145 us
  Pallas kernels  144 us (99%)
    pallas_call x1, Pallas kernels, run_block(): pl.pallas_call(functools.partial(block_kernel, size), out_shape=outs, in_...  136 us
    pallas_call x1, Pallas kernels, place_rows(): pl.pallas_call(functools.partial(place_kernel, size, assemble), grid=(1,)...  8.57 us

profile of v9, /device:TPU:0, one launch (start us, length us, event | category | flops | bytes accessed | tf_op | source)
XLA Modules:
  0.0 145.0 jit_solution(5975271883643733064)
XLA Ops:
  0.6 135.6 %shard_map.220 = (bf16[256,1024]{1,0:T(8,128)(2,1)}, bf16[256,1024]{1,0:T(8,128)(2,1)}, f32[8,1024]{1,0:T(8,128)}, f32[2,128,512]{2,1,0:T(8,128)}, f32[2,128,1024]{2,1,0:T(8,128)}) custom-call(bf16[8,256,1024]{2,1,0:T(8,128)(2,1)} %bitcast.14, bf16[8,256,1024]{2,1,0:T(8,128)(2,1)} %bitcast.16, s32[1,256]{1,0:T(1,128)} %routed.1, s32[1,2048]{1,0:T(1,128)} %refs_3_.1, ...), custom_call_target="tpu_custom_call" | custom-call | tf_op jit(solution)/shard_map/pallas_call | solution.py:1169
  136.2 8.6 %shard_map.221 = (bf16[2048,1024]{1,0:T(8,128)(2,1)}, bf16[2048,1024]{1,0:T(8,128)(2,1)}, f32[128,256]{1,0:T(8,128)}, f32[128,256]{1,0:T(8,128)}, f32[128,256]{1...) custom-call(s32[1,256]{1,0:T(1,128)} %routed.1, ...), custom_call_target="tpu_custom_call" | custom-call | tf_op jit(solution)/shard_map/pallas_call | solution.py:1264
